TPU v7x, 32 devices: a whole 2x2x4 slice. The times are simulated.
32 devices in a mesh: item: 2 (over core), seq: 4 (over z), tensor: 4 (over y, x).
Axes of the slice: x: 2, y: 2, z: 4, core: 2. Of those that a mesh axis runs over, the one named last changes fastest.
Arguments:
- dec_input: bfloat16 [4, 2048, 768], P('item', 'seq'), may hold values from -6 to 6
- encoder_states: bfloat16 [4, 4608, 768], P('item', 'seq'), may hold values from -6 to 6
- retrieved: int32 [4, 12, 1024], P('item', 'tensor'), may hold values from 0 to 4607, as said below
- self_wq: bfloat16 [768, 768], P(None, 'tensor'), may hold values from -0.21875 to 0.21875
- self_bq: float32 [768], P('tensor'), may hold values from -1.8 to 1.8
- self_wk: bfloat16 [768, 768], P(None, 'tensor'), may hold values from -0.21875 to 0.21875
- self_wv: bfloat16 [768, 768], P(None, 'tensor'), may hold values from -0.21875 to 0.21875
- self_bv: float32 [768], P('tensor'), may hold values from -1.8 to 1.8
- self_wo: bfloat16 [768, 768], P('tensor'), may hold values from -1.5 to 1.5
- self_bo: float32 [768], replicated, may hold values from -1.8 to 1.8
- norm1_gain: float32 [768], replicated, may hold values from 0.5 to 1.5
- norm1_bias: float32 [768], replicated, may hold values from -1.8 to 1.8
- cross_wq: bfloat16 [768, 768], P(None, 'tensor'), may hold values from -0.21875 to 0.21875
- cross_bq: float32 [768], P('tensor'), may hold values from -1.8 to 1.8
- cross_wk: bfloat16 [768, 768], P(None, 'tensor'), may hold values from -0.21875 to 0.21875
- cross_wv: bfloat16 [768, 768], P(None, 'tensor'), may hold values from -0.21875 to 0.21875
- cross_bv: float32 [768], P('tensor'), may hold values from -1.8 to 1.8
- cross_wo: bfloat16 [768, 768], P('tensor'), may hold values from -3 to 3
- cross_bo: float32 [768], replicated, may hold values from -1.8 to 1.8
- norm2_gain: float32 [768], replicated, may hold values from 0.5 to 1.5
- norm2_bias: float32 [768], replicated, may hold values from -1.8 to 1.8
- ffn_w1: bfloat16 [768, 3072], P(None, 'tensor'), may hold values from -0.21875 to 0.21875
- ffn_b1: float32 [3072], P('tensor'), may hold values from -1.8 to 1.8
- ffn_w2: bfloat16 [3072, 768], P('tensor'), may hold values from -0.109375 to 0.109375
- ffn_b2: float32 [768], replicated, may hold values from -1.8 to 1.8
- norm3_gain: float32 [768], replicated, may hold values from 0.5 to 1.5
- norm3_bias: float32 [768], replicated, may hold values from -1.8 to 1.8
- out_grad: bfloat16 [4, 2048, 768], P('item', 'seq'), may hold values from -6 to 6
Outputs:
- layer_out: bfloat16 [4, 2048, 768], P('item', 'seq')
- input_grad: bfloat16 [4, 2048, 768], P('item', 'seq')
- encoder_grad: bfloat16 [4, 4608, 768], P('item', 'seq', 'tensor')
- gself_wq: float32 [768, 768], P(('item', 'seq'), 'tensor')
- gself_bq: float32 [768], P('tensor')
- gself_wk: float32 [768, 768], P(('item', 'seq'), 'tensor')
- gself_wv: float32 [768, 768], P(('item', 'seq'), 'tensor')
- gself_bv: float32 [768], P('tensor')
- gself_wo: float32 [768, 768], P('tensor', ('item', 'seq'))
- gself_bo: float32 [768], replicated
- gnorm1_gain: float32 [768], replicated
- gnorm1_bias: float32 [768], replicated
- gcross_wq: float32 [768, 768], P(('item', 'seq'), 'tensor')
- gcross_bq: float32 [768], P('tensor')
- gcross_wk: float32 [768, 768], P(('item', 'seq'), 'tensor')
- gcross_wv: float32 [768, 768], P(('item', 'seq'), 'tensor')
- gcross_bv: float32 [768], P('tensor')
- gcross_wo: float32 [768, 768], P('tensor', ('item', 'seq'))
- gcross_bo: float32 [768], replicated
- gnorm2_gain: float32 [768], replicated
- gnorm2_bias: float32 [768], replicated
- gffn_w1: float32 [768, 3072], P(('item', 'seq'), 'tensor')
- gffn_b1: float32 [3072], P('tensor')
- gffn_w2: float32 [3072, 768], P('tensor', ('item', 'seq'))
- gffn_b2: float32 [768], replicated
- gnorm3_gain: float32 [768], replicated
- gnorm3_bias: float32 [768], replicated
Inputs may be any that keep to these rules, and one draw needn't show every extreme that they name: `retrieved`: for each item and head, 1024 distinct positions below 4608, among them always 0 and 4607; a position may appear under several heads, and positions fall unevenly over the blocks of 1152.
All inputs are finite; a program needn't handle non-finite values.
Results may differ from a plain program's by a relative error of at most 0.024.
Values may be sent and summed in bfloat16 or wider, within the bound.
A program may use at most 512 MiB of HBM per device.

v0:
```python
import jax
import jax.numpy as jnp
from jax import lax
from jax.sharding import PartitionSpec as P

EPS = 1e-05
SCALE = 0.125
NEG = -1e30


def matmul(first_op, second_op):
    return jnp.dot(first_op, second_op, preferred_element_type=jnp.float32)


def layer_norm(rows_in, norm_gain, norm_shift):
    center = rows_in - jnp.mean(rows_in, axis=-1, keepdims=True)
    spread = jnp.mean(center * center, axis=-1, keepdims=True)
    return center * lax.rsqrt(spread + EPS) * norm_gain + norm_shift


def exact_gelu(values_in):
    return jax.nn.gelu(values_in, approximate=False)


def tensor_total(partial_rows):
    return lax.psum(partial_rows, "tensor")


def row_total(values_in):
    return jnp.sum(values_in.astype(jnp.float32), axis=(0, 1))


def softmax_stats(scores):
    row_max = jnp.max(scores, axis=-1, keepdims=True)
    shifted = jnp.exp(scores - row_max)
    row_sum = jnp.sum(shifted, axis=-1, keepdims=True)
    return (shifted / row_sum, row_max + jnp.log(row_sum))


def owned_pick(encoder_states, kv_weights, kv_bias, flat_index, owned_mask):
    kv_table = (
        jnp.einsum("ind,dhf->inhf", encoder_states, kv_weights, preferred_element_type=jnp.float32)
        + kv_bias
    ).astype(jnp.bfloat16)
    flat_table = kv_table.reshape(-1, kv_table.shape[-1])
    picked = jnp.take(flat_table, flat_index, axis=0)
    return jnp.where(owned_mask, picked.astype(jnp.float32), 0.0)


def body(
    dec_input,
    encoder_states,
    retrieved,
    self_wq,
    self_bq,
    self_wk,
    self_wv,
    self_bv,
    self_wo,
    self_bo,
    norm1_gain,
    norm1_bias,
    cross_wq,
    cross_bq,
    cross_wk,
    cross_wv,
    cross_bv,
    cross_wo,
    cross_bo,
    norm2_gain,
    norm2_bias,
    ffn_w1,
    ffn_b1,
    ffn_w2,
    ffn_b2,
    norm3_gain,
    norm3_bias,
    out_grad,
):
    item_count, dec_rows, model_width = dec_input.shape
    local_heads = retrieved.shape[1]
    enc_rows = encoder_states.shape[1]
    head_cols = self_wq.shape[1]
    head_size = head_cols // local_heads
    seq_devices = lax.axis_size("seq")
    seq_rank = lax.axis_index("seq")
    seq_length = dec_rows * seq_devices
    queries = ((matmul(dec_input, self_wq) + self_bq) * SCALE).astype(jnp.bfloat16)
    keys_local = matmul(dec_input, self_wk).astype(jnp.bfloat16)
    values_local = (matmul(dec_input, self_wv) + self_bv).astype(jnp.bfloat16)
    kv_all = lax.all_gather(
        jnp.concatenate([keys_local, values_local], axis=-1), "seq", axis=1, tiled=True
    )
    keys_all = kv_all[..., :head_cols].reshape(item_count, seq_length, local_heads, head_size)
    values_all = kv_all[..., head_cols:].reshape(item_count, seq_length, local_heads, head_size)
    query_heads = queries.reshape(item_count, dec_rows, local_heads, head_size)
    query_pos = seq_rank * dec_rows + jnp.arange(dec_rows)
    causal = query_pos[:, None] >= jnp.arange(seq_length)[None, :]

    def self_scores():
        raw_scores = jnp.einsum(
            "irhe,ilhe->ihrl", query_heads, keys_all, preferred_element_type=jnp.float32
        )
        return jnp.where(causal, raw_scores, NEG)

    prob_self, lse_self = softmax_stats(self_scores())
    attended = (
        jnp.einsum(
            "ihrl,ilhe->irhe",
            prob_self.astype(jnp.bfloat16),
            values_all,
            preferred_element_type=jnp.float32,
        )
        .astype(jnp.bfloat16)
        .reshape(item_count, dec_rows, head_cols)
    )
    branch_one = tensor_total(matmul(attended, self_wo)) + self_bo
    hidden_one = dec_input.astype(jnp.float32) + branch_one
    normed_one = layer_norm(hidden_one, norm1_gain, norm1_bias).astype(jnp.bfloat16)
    queries_x = (
        ((matmul(normed_one, cross_wq) + cross_bq) * SCALE)
        .astype(jnp.bfloat16)
        .reshape(item_count, dec_rows, local_heads, head_size)
    )
    kv_weights = jnp.concatenate(
        [
            cross_wk.reshape(model_width, local_heads, head_size),
            cross_wv.reshape(model_width, local_heads, head_size),
        ],
        axis=-1,
    )
    kv_bias = jnp.concatenate(
        [
            jnp.zeros((local_heads, head_size), jnp.float32),
            cross_bv.reshape(local_heads, head_size),
        ],
        axis=-1,
    )
    local_row = retrieved - seq_rank * enc_rows
    owned_mask = ((local_row >= 0) & (local_row < enc_rows))[..., None]
    flat_index = (
        jnp.arange(item_count, dtype=jnp.int32)[:, None, None] * enc_rows
        + jnp.clip(local_row, 0, enc_rows - 1)
    ) * local_heads + jnp.arange(local_heads, dtype=jnp.int32)[None, :, None]
    retrieved_kv = lax.psum(
        owned_pick(encoder_states, kv_weights, kv_bias, flat_index, owned_mask).astype(
            jnp.bfloat16
        ),
        "seq",
    )

    def cross_scores(kv_pair):
        return jnp.einsum(
            "irhe,ihke->ihrk",
            queries_x,
            kv_pair[..., :head_size],
            preferred_element_type=jnp.float32,
        )

    prob_cross, lse_cross = softmax_stats(cross_scores(retrieved_kv))
    attended_x = (
        jnp.einsum(
            "ihrk,ihke->irhe",
            prob_cross.astype(jnp.bfloat16),
            retrieved_kv[..., head_size:],
            preferred_element_type=jnp.float32,
        )
        .astype(jnp.bfloat16)
        .reshape(item_count, dec_rows, head_cols)
    )
    branch_two = tensor_total(matmul(attended_x, cross_wo)) + cross_bo
    hidden_two = normed_one.astype(jnp.float32) + branch_two
    normed_two = layer_norm(hidden_two, norm2_gain, norm2_bias).astype(jnp.bfloat16)
    pre_act = matmul(normed_two, ffn_w1) + ffn_b1
    activated = exact_gelu(pre_act).astype(jnp.bfloat16)
    branch_three = tensor_total(matmul(activated, ffn_w2)) + ffn_b2
    hidden_three = normed_two.astype(jnp.float32) + branch_three
    layer_out = layer_norm(hidden_three, norm3_gain, norm3_bias)
    _, back_three = jax.vjp(layer_norm, hidden_three, norm3_gain, norm3_bias)
    d_hidden3, gnorm3_gain, gnorm3_bias = back_three(out_grad.astype(jnp.float32))
    d_branch3 = d_hidden3.astype(jnp.bfloat16)
    gffn_b2 = row_total(d_branch3)
    gffn_w2 = jnp.einsum("irf,ird->fd", activated, d_branch3, preferred_element_type=jnp.float32)
    d_activated = jnp.einsum("ird,fd->irf", d_branch3, ffn_w2, preferred_element_type=jnp.float32)
    _, gelu_back = jax.vjp(exact_gelu, pre_act)
    d_pre = gelu_back(d_activated)[0].astype(jnp.bfloat16)
    gffn_b1 = row_total(d_pre)
    gffn_w1 = jnp.einsum("ird,irf->df", normed_two, d_pre, preferred_element_type=jnp.float32)
    d_normed2 = d_hidden3 + tensor_total(
        jnp.einsum("irf,df->ird", d_pre, ffn_w1, preferred_element_type=jnp.float32)
    )
    _, back_two = jax.vjp(layer_norm, hidden_two, norm2_gain, norm2_bias)
    d_hidden2, gnorm2_gain, gnorm2_bias = back_two(d_normed2)
    d_branch2 = d_hidden2.astype(jnp.bfloat16)
    gcross_bo = row_total(d_branch2)
    gcross_wo = jnp.einsum("irc,ird->cd", attended_x, d_branch2, preferred_element_type=jnp.float32)
    d_attended2 = (
        jnp.einsum("ird,cd->irc", d_branch2, cross_wo, preferred_element_type=jnp.float32)
        .astype(jnp.bfloat16)
        .reshape(item_count, dec_rows, local_heads, head_size)
    )
    kv_back = lax.psum(
        owned_pick(encoder_states, kv_weights, kv_bias, flat_index, owned_mask).astype(
            jnp.bfloat16
        ),
        "seq",
    )
    redo_cross = jnp.exp(cross_scores(kv_back) - lse_cross)
    dprob_cross = jnp.einsum(
        "irhe,ihke->ihrk", d_attended2, kv_back[..., head_size:], preferred_element_type=jnp.float32
    )
    d_scores2 = (
        redo_cross * (dprob_cross - jnp.sum(dprob_cross * redo_cross, axis=-1, keepdims=True))
    ).astype(jnp.bfloat16)
    d_query2 = (
        jnp.einsum(
            "ihrk,ihke->irhe",
            d_scores2,
            kv_back[..., :head_size],
            preferred_element_type=jnp.float32,
        )
        .astype(jnp.bfloat16)
        .reshape(item_count, dec_rows, head_cols)
    )
    kv_grad_part = jnp.concatenate(
        [
            jnp.einsum("ihrk,irhe->ihke", d_scores2, queries_x, preferred_element_type=jnp.float32),
            jnp.einsum(
                "ihrk,irhe->ihke",
                redo_cross.astype(jnp.bfloat16),
                d_attended2,
                preferred_element_type=jnp.float32,
            ),
        ],
        axis=-1,
    )
    kv_grad = lax.psum(kv_grad_part, "seq").astype(jnp.bfloat16)
    kv_owned = jnp.where(owned_mask, kv_grad.astype(jnp.float32), 0.0)
    table_grad = (
        jnp.zeros((item_count * enc_rows * local_heads, 2 * head_size), jnp.float32)
        .at[flat_index.reshape(-1)]
        .add(kv_owned.reshape(-1, 2 * head_size))
    )
    table_low = table_grad.astype(jnp.bfloat16).reshape(
        item_count, enc_rows, local_heads, 2 * head_size
    )
    grad_kv_weights = jnp.einsum(
        "ind,inhf->dhf", encoder_states, table_low, preferred_element_type=jnp.float32
    )
    gcross_wk = grad_kv_weights[..., :head_size].reshape(model_width, head_cols)
    gcross_wv = grad_kv_weights[..., head_size:].reshape(model_width, head_cols)
    gcross_bv = row_total(table_low[..., head_size:]).reshape(head_cols)
    encoder_part = jnp.einsum(
        "inhf,dhf->ind", table_low, kv_weights, preferred_element_type=jnp.float32
    )
    encoder_grad = lax.psum_scatter(encoder_part, "tensor", scatter_dimension=2, tiled=True).astype(
        jnp.bfloat16
    )
    gcross_bq = row_total(d_query2) * SCALE
    gcross_wq = (
        jnp.einsum("ird,irc->dc", normed_one, d_query2, preferred_element_type=jnp.float32) * SCALE
    )
    d_normed1 = d_hidden2 + tensor_total(
        jnp.einsum("irc,dc->ird", d_query2, cross_wq, preferred_element_type=jnp.float32) * SCALE
    )
    _, back_one = jax.vjp(layer_norm, hidden_one, norm1_gain, norm1_bias)
    d_hidden1, gnorm1_gain, gnorm1_bias = back_one(d_normed1)
    d_branch1 = d_hidden1.astype(jnp.bfloat16)
    gself_bo = row_total(d_branch1)
    gself_wo = jnp.einsum("irc,ird->cd", attended, d_branch1, preferred_element_type=jnp.float32)
    d_attended1 = (
        jnp.einsum("ird,cd->irc", d_branch1, self_wo, preferred_element_type=jnp.float32)
        .astype(jnp.bfloat16)
        .reshape(item_count, dec_rows, local_heads, head_size)
    )
    redo_self = jnp.exp(self_scores() - lse_self)
    dprob_self = jnp.einsum(
        "irhe,ilhe->ihrl", d_attended1, values_all, preferred_element_type=jnp.float32
    )
    d_scores1 = (
        redo_self * (dprob_self - jnp.sum(dprob_self * redo_self, axis=-1, keepdims=True))
    ).astype(jnp.bfloat16)
    probs_low = redo_self.astype(jnp.bfloat16)
    d_query1 = (
        jnp.einsum("ihrl,ilhe->irhe", d_scores1, keys_all, preferred_element_type=jnp.float32)
        .astype(jnp.bfloat16)
        .reshape(item_count, dec_rows, head_cols)
    )
    row_count = dec_rows * lax.axis_size("seq")
    key_grad = jnp.einsum(
        "ihrl,irhe->lihe", d_scores1, query_heads, preferred_element_type=jnp.float32
    ).reshape(row_count, item_count, head_cols)
    value_grad = jnp.einsum(
        "ihrl,irhe->lihe", probs_low, d_attended1, preferred_element_type=jnp.float32
    ).reshape(row_count, item_count, head_cols)
    kv_self = lax.psum_scatter(
        jnp.concatenate([key_grad, value_grad], axis=-1), "seq", scatter_dimension=0, tiled=True
    ).astype(jnp.bfloat16)
    kv_self = jnp.swapaxes(kv_self, 0, 1)
    d_key1 = kv_self[..., :head_cols]
    d_value1 = kv_self[..., head_cols:]
    gself_bq = row_total(d_query1) * SCALE
    gself_wq = (
        jnp.einsum("ird,irc->dc", dec_input, d_query1, preferred_element_type=jnp.float32) * SCALE
    )
    gself_wk = jnp.einsum("ird,irc->dc", dec_input, d_key1, preferred_element_type=jnp.float32)
    gself_wv = jnp.einsum("ird,irc->dc", dec_input, d_value1, preferred_element_type=jnp.float32)
    gself_bv = row_total(d_value1)
    input_part = (
        jnp.einsum("irc,dc->ird", d_query1, self_wq, preferred_element_type=jnp.float32) * SCALE
        + jnp.einsum("irc,dc->ird", d_key1, self_wk, preferred_element_type=jnp.float32)
        + jnp.einsum("irc,dc->ird", d_value1, self_wv, preferred_element_type=jnp.float32)
    )
    input_grad = (d_hidden1 + tensor_total(input_part)).astype(jnp.bfloat16)
    matrices = (
        lax.psum_scatter(gself_wq, ("item", "seq"), scatter_dimension=0, tiled=True),
        lax.psum_scatter(gself_wk, ("item", "seq"), scatter_dimension=0, tiled=True),
        lax.psum_scatter(gself_wv, ("item", "seq"), scatter_dimension=0, tiled=True),
        lax.psum_scatter(gself_wo, ("item", "seq"), scatter_dimension=1, tiled=True),
        lax.psum_scatter(gcross_wq, ("item", "seq"), scatter_dimension=0, tiled=True),
        lax.psum_scatter(gcross_wk, ("item", "seq"), scatter_dimension=0, tiled=True),
        lax.psum_scatter(gcross_wv, ("item", "seq"), scatter_dimension=0, tiled=True),
        lax.psum_scatter(gcross_wo, ("item", "seq"), scatter_dimension=1, tiled=True),
        lax.psum_scatter(gffn_w1, ("item", "seq"), scatter_dimension=0, tiled=True),
        lax.psum_scatter(gffn_w2, ("item", "seq"), scatter_dimension=1, tiled=True),
    )
    vectors = lax.psum(
        (
            gself_bq,
            gself_bv,
            gself_bo,
            gnorm1_gain,
            gnorm1_bias,
            gcross_bq,
            gcross_bv,
            gcross_bo,
            gnorm2_gain,
            gnorm2_bias,
            gffn_b1,
            gffn_b2,
            gnorm3_gain,
            gnorm3_bias,
        ),
        ("item", "seq"),
    )
    return (
        layer_out.astype(jnp.bfloat16),
        input_grad,
        encoder_grad,
        matrices[0],
        vectors[0],
        matrices[1],
        matrices[2],
        vectors[1],
        matrices[3],
        vectors[2],
        vectors[3],
        vectors[4],
        matrices[4],
        vectors[5],
        matrices[5],
        matrices[6],
        vectors[6],
        matrices[7],
        vectors[7],
        vectors[8],
        vectors[9],
        matrices[8],
        vectors[10],
        matrices[9],
        vectors[11],
        vectors[12],
        vectors[13],
    )


def solution(mesh):
    placed = (
        P("item", "seq", None),
        P("item", "seq", None),
        P("item", "tensor", None),
        P(None, "tensor"),
        P("tensor"),
        P(None, "tensor"),
        P(None, "tensor"),
        P("tensor"),
        P("tensor", None),
        P(),
        P(),
        P(),
        P(None, "tensor"),
        P("tensor"),
        P(None, "tensor"),
        P(None, "tensor"),
        P("tensor"),
        P("tensor", None),
        P(),
        P(),
        P(),
        P(None, "tensor"),
        P("tensor"),
        P("tensor", None),
        P(),
        P(),
        P(),
        P("item", "seq", None),
    )
    return jax.shard_map(
        body,
        mesh=mesh,
        in_specs=placed,
        out_specs=(
            P("item", "seq", None),
            P("item", "seq", None),
            P("item", "seq", "tensor"),
            P(("item", "seq"), "tensor"),
            P("tensor"),
            P(("item", "seq"), "tensor"),
            P(("item", "seq"), "tensor"),
            P("tensor"),
            P("tensor", ("item", "seq")),
            P(),
            P(),
            P(),
            P(("item", "seq"), "tensor"),
            P("tensor"),
            P(("item", "seq"), "tensor"),
            P(("item", "seq"), "tensor"),
            P("tensor"),
            P("tensor", ("item", "seq")),
            P(),
            P(),
            P(),
            P(("item", "seq"), "tensor"),
            P("tensor"),
            P("tensor", ("item", "seq")),
            P(),
            P(),
            P(),
        ),
        check_vma=False,
    )
```

profile of v0, /device:TPU:0, one launch (start us, length us, event | category | flops | bytes accessed | tf_op | source)
XLA Modules:
  0.0 1557.6 jit_solution(12805018805111972139)
XLA Ops:
  12.8 2.9 fusion.48
  17.2 61.7 %all-gather.2.cloned.1.call-done = bf16[2,2048,384]{1,2,0:T(8,128)(2,1)} async-done(((bf16[2,512,384]{1,2,0:T(8,128)(2,1)}), bf16[2,2048,384]{1,2,0:T(8,128)(2,1)}) %all-gather.2.cloned.1.call-update) | async-done | bytes 3145744 | tf_op jit(solution)/shard_map/all_gather | solution.py:91
  81.3 10.4 select_reduce_fusion
  91.7 11.7 fusion
  103.5 11.3 fusion.51
  123.2 3.9 fusion.30
  127.1 4.9 copy.87
  132.0 5.5 reshape.303
  138.8 25.0 %gather_fusion = bf16[6144,128]{1,0:T(8,128)(2,1)} fusion(bf16[6912,128]{1,0:T(8,128)(2,1)} %reshape.303, s32[6144]{0:T(1024)} %broadcast_clamp_fusion), kind=kCustom, calls=%fused_computation.clone | custom fusion | bytes 3170304 | tf_op jit(solution)/shard_map/jit(_take)/gather | solution.py:46
  166.4 3.2 select_convert_fusion
  169.6 34.4 %all-reduce.11.cloned.1.call-done = f32[2,512,768]{2,1,0:T(8,128)} async-done(((f32[2,512,768]{2,1,0:T(8,128)}), f32[2,512,768]{2,1,0:T(8,128)}) %all-reduce.11.cloned.1.call-update) | async-done | bytes 3145744 | tf_op jit(solution)/shard_map/psum | solution.py:26
  204.0 2.9 fusion.102
  211.2 65.1 %all-reduce.13.cloned.1.call-done = bf16[2,3,1024,128]{2,3,1,0:T(8,128)(2,1)} async-done(((bf16[2,3,1024,128]{2,3,1,0:T(8,128)(2,1)}), bf16[2,3,1024,128]{2,3,1,0:T(8,128)(2,1)}) %all-reduce.13.cloned.1.call-update) | async-done | bytes 1572880 | tf_op jit(solution)/shard_map/psum | solution.py:145
  276.2 3.2 fusion.105
  284.2 3.2 fusion.50
  291.1 85.8 %all-reduce.15.cloned.1.call-done = f32[2,512,768]{2,1,0:T(8,128)} async-done(((f32[2,512,768]{2,1,0:T(8,128)}), f32[2,512,768]{2,1,0:T(8,128)}) %all-reduce.15.cloned.1.call-update) | async-done | bytes 3145744 | tf_op jit(solution)/shard_map/psum | solution.py:26
  377.0 3.8 fusion.101
  385.5 8.3 multiply_convert_fusion.2
  394.9 3.2 fusion.53
  398.4 87.1 %all-reduce.17.cloned.1.call-done = f32[2,512,768]{2,1,0:T(8,128)} async-done(((f32[2,512,768]{2,1,0:T(8,128)}), f32[2,512,768]{2,1,0:T(8,128)}) %all-reduce.17.cloned.1.call-update) | async-done | bytes 3145744 | tf_op jit(solution)/shard_map/psum | solution.py:26
  485.5 3.9 fusion.99
  496.8 2.9 convert_reduce_fusion.3
  500.8 3.1 fusion.55
  505.0 86.3 %all-reduce.19.cloned.1.call-done = f32[2,512,768]{2,1,0:T(8,128)} async-done(((f32[2,512,768]{2,1,0:T(8,128)}), f32[2,512,768]{2,1,0:T(8,128)}) %all-reduce.19.cloned.1.call-update) | async-done | bytes 3145744 | tf_op jit(solution)/shard_map/psum | solution.py:26
  591.3 7.2 multiply_reduce_fusion.2
  602.9 6.0 multiply_reduce_fusion.1
  608.9 6.2 multiply_convert_fusion.1
  622.0 86.3 %all-reduce.21.cloned.1.call-done = f32[2,512,768]{2,1,0:T(8,128)} async-done(((f32[2,512,768]{2,1,0:T(8,128)}), f32[2,512,768]{2,1,0:T(8,128)}) %all-reduce.21.cloned.1.call-update) | async-done | bytes 3145744 | tf_op jit(solution)/shard_map/psum | solution.py:26
  708.3 5.4 multiply_reduce_fusion.3
  718.5 12.8 fusion.2
  731.3 18.1 %multiply_reduce_fusion = (f32[2,3,512]{2,1,0:T(4,128)}, f32[2,3,512,2048]{3,2,1,0:T(8,128)}) fusion(f32[2,3,512,2048]{3,2,1,0:T(8,128)} %get-tuple-element.167, f32[2,3,512]{2,1,0:T(4,128)S(1)} %log_add_fusion, pred[512,2048]{1,0:T(8,128)(4,1)} %iota_compare_fusion, bf16[2,512,3,64]{1,3,2,0:T(8,128)(2,1)} %bitcast.208, bf16[2,2048,3,64]{1,3,2,0:T(8,128)(2,1)} %bitcast.198), kind=kOutput, calls=%fused_computation.3 | convolution fusion | flops 830469120 | bytes 53370880 | tf_op jit(solution)/shard_map/irhe,ilhe->ihrl/dot_general | solution.py:277
  749.5 18.4 %multiply_convert_fusion = bf16[2,3,512,2048]{3,2,1,0:T(8,128)(2,1)S(1)} fusion(f32[2,3,512,2048]{3,2,1,0:T(8,128)} %get-tuple-element.174, f32[2,3,512,2048]{3,2,1,0:T(8,128)} %get-tuple-element.167, f32[2,3,512]{2,1,0:T(4,128)} %get-tuple-element.173, f32[2,3,512]{2,1,0:T(4,128)S(1)} %log_add_fusion, pred[512,2048]{1,0:T(8,128)(4,1)} %iota_compare_fusion), kind=kLoop, calls=%fused_computation.2 | loop fusion | flops 31457280 | bytes 63987712 | tf_op jit(solution)/shard_map/convert_element_type | solution.py:282
  770.2 3.0 copy-done.2
  773.2 3.5 pad_maximum_fusion
  780.9 3.2 convolution_bitcast_fusion.3
  784.2 4.2 fusion.107
  788.5 5.8 fusion.10
  798.4 198.8 %all-reduce.24 = bf16[2,3,1024,128]{2,3,1,0:T(8,128)(2,1)} all-reduce(f32[2,3,1024,128]{2,3,1,0:T(8,128)} %pad_maximum_fusion.1), channel_id=1, replica_groups=mesh['item'=2,'seq'=4,'tensor'=4] {'seq'}, use_global_device_ids=true, to_apply=%region_26.28 | all-reduce | flops 786432 | bytes 4718592 | tf_op jit(solution)/shard_map/psum | solution.py:237
  997.2 3.5 convert_select_fusion
  1000.7 3.5 copy.91
  1004.2 37.5 %scatter_custom_fusion = f32[6912,128]{1,0:T(8,128)} fusion(s32[6144]{0:T(1024)} %bitcast.225, f32[6144,128]{1,0:T(8,128)} %bitcast.202, f32[]{:T(128)} %constant.59.clone.1), kind=kCustom, calls=%fused_computation.96 | custom fusion | flops 786432 | bytes 3539456 | tf_op jit(solution)/shard_map/scatter-add | solution.py:242
  1041.7 3.4 convert_element_type.195
  1045.1 5.8 reshape.314
  1050.9 6.6 convolution_bitcast_fusion
  1057.6 9.8 convert_reduce_fusion.8
  1076.7 3.0 fusion.44
  1079.7 3.5 fusion.37
  1089.0 4.9 convolution_bitcast_fusion.1
  1094.3 5.7 convolution_bitcast_fusion.2
  1105.2 2.9 convolution_bitcast_fusion.6
  1110.4 2.9 convolution_bitcast_fusion.7
  1118.2 4.5 convert_reduce_fusion.1
  1129.9 3.0 reduce-scatter.25.cloned.1.call-done
  1137.1 30.6 %all-reduce.1 = (f32[192]{0:T(256)}, f32[192]{0:T(256)}, f32[768]{0:T(1024)}, f32[768]{0:T(1024)}, f32[768]{0:T(1024)}, /*index=5*/f32[192]{0:T(256)}, f32[192]{...) all-reduce(f32[192]{0:T(256)} %mul.330, ...), channel_id=1, replica_groups=mesh['item'=2,'seq'=4,'tensor'=4] {'item','seq'}, use_global_device_ids=true, to_apply=%region_31.33 | all-reduce | flops 8448 | bytes 67584 | tf_op jit(solution)/shard_map/psum | solution.py:327
  1167.6 55.7 %all-reduce.23.cloned.1.call-done = f32[2,512,768]{2,1,0:T(8,128)} async-done(((f32[2,512,768]{2,1,0:T(8,128)}), f32[2,512,768]{2,1,0:T(8,128)}) %all-reduce.23.cloned.1.call-update) | async-done | bytes 3145744 | tf_op jit(solution)/shard_map/psum | solution.py:26
  1223.4 4.3 add_convert_fusion
  1227.7 32.6 %reduce-scatter.27.cloned.1.call-done = f32[96,192]{1,0:T(8,128)} async-done(((f32[768,192]{1,0:T(8,128)}), f32[96,192]{1,0:T(8,128)}) %reduce-scatter.27.cloned.1.call-update) | async-done | bytes 73744 | tf_op jit(solution)/shard_map/reduce_scatter | solution.py:320
  1260.3 35.7 %reduce-scatter.29.cloned.1.call-done = f32[96,192]{1,0:T(8,128)} async-done(((f32[768,192]{1,0:T(8,128)}), f32[96,192]{1,0:T(8,128)}) %reduce-scatter.29.cloned.1.call-update) | async-done | bytes 73744 | tf_op jit(solution)/shard_map/reduce_scatter | solution.py:321
  1296.0 35.4 %reduce-scatter.31.cloned.1.call-done = f32[96,192]{1,0:T(8,128)} async-done(((f32[768,192]{1,0:T(8,128)}), f32[96,192]{1,0:T(8,128)}) %reduce-scatter.31.cloned.1.call-update) | async-done | bytes 73744 | tf_op jit(solution)/shard_map/reduce_scatter | solution.py:322
  1331.4 55.7 %reduce-scatter.35.cloned.1.call-done = f32[768,96]{0,1:T(8,128)} async-done(((f32[768,768]{0,1:T(8,128)}), f32[768,96]{0,1:T(8,128)}) %reduce-scatter.35.cloned.1.call-update) | async-done | bytes 294928 | tf_op jit(solution)/shard_map/reduce_scatter | solution.py:325
  1387.2 56.0 %reduce-scatter.33.cloned.1.call-done = f32[96,768]{1,0:T(8,128)} async-done(((f32[768,768]{1,0:T(8,128)}), f32[96,768]{1,0:T(8,128)}) %reduce-scatter.33.cloned.1.call-update) | async-done | bytes 294928 | tf_op jit(solution)/shard_map/reduce_scatter | solution.py:324
  1443.2 36.0 %reduce-scatter.37.cloned.1.call-done = f32[96,192]{1,0:T(8,128)} async-done(((f32[768,192]{1,0:T(8,128)}), f32[96,192]{1,0:T(8,128)}) %reduce-scatter.37.cloned.1.call-update) | async-done | bytes 73744
  1479.2 35.7 %reduce-scatter.41.cloned.1.call-done = f32[96,192]{1,0:T(8,128)} async-done(((f32[768,192]{1,0:T(8,128)}), f32[96,192]{1,0:T(8,128)}) %reduce-scatter.41.cloned.1.call-update) | async-done | bytes 73744
  1514.9 35.7 %reduce-scatter.39.cloned.1.call-done = f32[96,192]{1,0:T(8,128)} async-done(((f32[768,192]{1,0:T(8,128)}), f32[96,192]{1,0:T(8,128)}) %reduce-scatter.39.cloned.1.call-update) | async-done | bytes 73744
  (324 shorter events, 115.2 us)
Async XLA Ops:
  7.2 116.0 %copy-start = (bf16[2,1152,768]{2,1,0:T(8,128)(2,1)S(1)}, bf16[2,1152,768]{2,1,0:T(8,128)(2,1)}, u32[]{:S(2)}) copy-start(bf16[2,1152,768]{2,1,0:T(8,128)(2,1)} %param.31) | copy-start | bytes 10616836
  7.2 5.5 copy-start.97
  7.2 71.8 %all-gather.2.cloned.1.call-start = ((), (), s32[]{:S(2)}) async-start(), calls=%async_computation.12 | async-start | bytes 3932160 | tf_op jit(solution)/shard_map/all_gather | solution.py:91
  12.7 191.3 %all-reduce.11.cloned.1.call-start = ((), (), s32[]{:S(2)}) async-start(), calls=%async_computation.13 | async-start | bytes 6291456 | tf_op jit(solution)/shard_map/psum | solution.py:26
  81.3 10.5 copy-start.14
  81.3 22.2 %copy-start.18 = (bf16[2,2048,192]{1,2,0:T(8,128)(2,1)}, bf16[2,2048,192]{1,2,0:T(8,128)(2,1)S(1)}, u32[]{:S(2)}) copy-start(bf16[2,2048,192]{1,2,0:T(8,128)(2,1)S(1)} %get-tuple-element.160) | copy-start | bytes 4718596
  91.7 11.7 copy-start.53
  103.4 11.3 copy-start.70
  103.5 12.1 copy-start.45
  117.9 158.3 %all-reduce.13.cloned.1.call-start = ((), (), s32[]{:S(2)}) async-start(), calls=%async_computation.14 | async-start | bytes 3145728 | tf_op jit(solution)/shard_map/psum | solution.py:145
  119.9 46.5 %copy-start.61 = (pred[2,3,1024]{2,1,0:T(4,128)(4,1)}, pred[2,3,1024]{2,1,0:T(4,128)(4,1)S(1)}, u32[]{:S(2)}) copy-start(pred[2,3,1024]{2,1,0:T(4,128)(4,1)S(1)} %copy.85) | copy-start | bytes 18436
  169.6 207.4 %all-reduce.15.cloned.1.call-start = ((), (), s32[]{:S(2)}) async-start(), calls=%async_computation.15 | async-start | bytes 6291456 | tf_op jit(solution)/shard_map/psum | solution.py:26
  206.9 170.1 %copy-start.51 = (f32[2,512]{1,0:T(2,128)}, f32[2,512]{1,0:T(2,128)S(1)}, u32[]{:S(2)}) copy-start(f32[2,512]{1,0:T(2,128)S(1)} %broadcast_multiply_fusion.2) | copy-start | bytes 12292
  208.0 169.0 %copy-start.55 = (f32[2,512]{1,0:T(2,128)}, f32[2,512]{1,0:T(2,128)S(1)}, u32[]{:S(2)}) copy-start(f32[2,512]{1,0:T(2,128)S(1)} %fusion.89) | copy-start | bytes 12292
  279.4 4.7 copy-start.1
  279.4 4.7 copy-start.54
  290.6 194.9 %all-reduce.17.cloned.1.call-start = ((), (), s32[]{:S(2)}) async-start(), calls=%async_computation.16 | async-start | bytes 6291456 | tf_op jit(solution)/shard_map/psum | solution.py:26
  380.9 104.6 %copy-start.57 = (f32[2,512]{1,0:T(2,128)}, f32[2,512]{1,0:T(2,128)S(1)}, u32[]{:S(2)}) copy-start(f32[2,512]{1,0:T(2,128)S(1)} %broadcast_multiply_fusion.1) | copy-start | bytes 12292
  383.1 102.4 %copy-start.65 = (f32[2,512]{1,0:T(2,128)}, f32[2,512]{1,0:T(2,128)S(1)}, u32[]{:S(2)}) copy-start(f32[2,512]{1,0:T(2,128)S(1)} %fusion.90) | copy-start | bytes 12292
  385.5 8.3 copy-start.25
  385.5 9.5 copy-start.93
  398.1 91.4 %copy-start.72 = (f32[768]{0:T(1024)S(1)}, f32[768]{0:T(1024)}, u32[]{:S(2)}) copy-start(f32[768]{0:T(1024)} %param.55) | copy-start | bytes 9220
  398.1 193.2 %all-reduce.19.cloned.1.call-start = ((), (), s32[]{:S(2)}) async-start(), calls=%async_computation.17 | async-start | bytes 6291456 | tf_op jit(solution)/shard_map/psum | solution.py:26
  504.0 204.3 %all-reduce.21.cloned.1.call-start = ((), (), s32[]{:S(2)}) async-start(), calls=%async_computation.18 | async-start | bytes 6291456 | tf_op jit(solution)/shard_map/psum | solution.py:26
  505.0 104.0 %copy-start.48 = (f32[2,3,512]{2,1,0:T(4,128)}, f32[2,3,512]{2,1,0:T(4,128)S(1)}, u32[]{:S(2)}) copy-start(f32[2,3,512]{2,1,0:T(4,128)S(1)} %log_add_fusion.1) | copy-start | bytes 36868
  591.3 7.2 copy-start.83
  591.3 7.2 copy-start.9
  591.3 7.2 copy-start.58
  591.3 7.2 copy-start.66
  591.3 7.2 copy-start.77
  591.3 11.3 slice-start
  591.3 11.3 slice-start.1
  602.6 6.4 copy-start.38
  620.9 449.5 %reduce-scatter.23.cloned.1.call-start = ((), (), s32[]{:S(2)}) async-start(), calls=%async_computation.19 | async-start | bytes 7864320 | tf_op jit(solution)/shard_map/reduce_scatter | solution.py:296
  708.3 5.4 copy-start.81
  708.3 5.4 copy-start.4
  708.3 5.4 copy-start.52
  708.3 5.4 copy-start.56
  708.3 5.5 copy-start.64
  749.5 18.4 %copy-start.30 = (bf16[2,512,192]{1,2,0:T(8,128)(2,1)S(1)}, bf16[2,512,192]{1,2,0:T(8,128)(2,1)}, u32[]{:S(2)}) copy-start(bf16[2,512,192]{1,2,0:T(8,128)(2,1)} %fusion.48) | copy-start | bytes 1179652
  767.9 5.3 copy-start.2
  767.9 5.3 copy-start.15
  776.7 347.3 %reduce-scatter.45.cloned.1.call-start = ((), (), s32[]{:S(2)}) async-start(), calls=%async_computation.31 | async-start | bytes 884736
  784.2 344.1 %reduce-scatter.43.cloned.1.call-start = ((), (), s32[]{:S(2)}) async-start(), calls=%async_computation.30 | async-start | bytes 884736
  798.3 198.9 %copy-start.62 = (pred[2,3,1024]{2,1,0:T(4,128)(4,1)S(1)}, pred[2,3,1024]{2,1,0:T(4,128)(4,1)}, u32[]{:S(2)}) copy-start(pred[2,3,1024]{2,1,0:T(4,128)(4,1)} %copy-done.61) | copy-start | bytes 18436
  798.3 334.6 %reduce-scatter.25.cloned.1.call-start = ((), (), s32[]{:S(2)}) async-start(), calls=%async_computation.21 | async-start | bytes 8847360 | tf_op jit(solution)/shard_map/reduce_scatter | solution.py:256
  1057.6 165.8 %all-reduce.23.cloned.1.call-start = ((), (), s32[]{:S(2)}) async-start(), calls=%async_computation.20 | async-start | bytes 6291456 | tf_op jit(solution)/shard_map/psum | solution.py:26
  1057.6 10.6 copy-start.47
  1076.6 183.7 %reduce-scatter.27.cloned.1.call-start = ((), (), s32[]{:S(2)}) async-start(), calls=%async_computation.22 | async-start | bytes 884736 | tf_op jit(solution)/shard_map/reduce_scatter | solution.py:320
  1079.6 216.4 %reduce-scatter.29.cloned.1.call-start = ((), (), s32[]{:S(2)}) async-start(), calls=%async_computation.23 | async-start | bytes 884736 | tf_op jit(solution)/shard_map/reduce_scatter | solution.py:321
  1086.6 244.8 %reduce-scatter.31.cloned.1.call-start = ((), (), s32[]{:S(2)}) async-start(), calls=%async_computation.24 | async-start | bytes 884736 | tf_op jit(solution)/shard_map/reduce_scatter | solution.py:322
  1088.9 5.3 copy-start.59
  1088.9 5.3 copy-start.67
  1088.9 5.3 copy-start.78
  1088.9 5.3 copy-start.91
  1089.0 298.2 %reduce-scatter.35.cloned.1.call-start = ((), (), s32[]{:S(2)}) async-start(), calls=%async_computation.26 | async-start | bytes 2654208 | tf_op jit(solution)/shard_map/reduce_scatter | solution.py:325
  1094.0 349.2 %reduce-scatter.33.cloned.1.call-start = ((), (), s32[]{:S(2)}) async-start(), calls=%async_computation.25 | async-start | bytes 2654208 | tf_op jit(solution)/shard_map/reduce_scatter | solution.py:324
  1100.0 379.1 %reduce-scatter.37.cloned.1.call-start = ((), (), s32[]{:S(2)}) async-start(), calls=%async_computation.27 | async-start | bytes 884736
  1105.1 409.7 %reduce-scatter.41.cloned.1.call-start = ((), (), s32[]{:S(2)}) async-start(), calls=%async_computation.29 | async-start | bytes 884736
  1110.3 440.2 %reduce-scatter.39.cloned.1.call-start = ((), (), s32[]{:S(2)}) async-start(), calls=%async_computation.28 | async-start | bytes 884736
  1115.6 21.5 %copy-start.84 = (f32[768]{0:T(1024)S(1)}, f32[768]{0:T(1024)}, u32[]{:S(2)}) copy-start(f32[768]{0:T(1024)} %get-tuple-element.111) | copy-start | bytes 9220
  1115.6 21.5 %copy-start.85 = (f32[768]{0:T(1024)S(1)}, f32[768]{0:T(1024)}, u32[]{:S(2)}) copy-start(f32[768]{0:T(1024)} %get-tuple-element.120) | copy-start | bytes 9220
  1115.6 21.5 %copy-start.87 = (f32[768]{0:T(1024)S(1)}, f32[768]{0:T(1024)}, u32[]{:S(2)}) copy-start(f32[768]{0:T(1024)} %get-tuple-element.113) | copy-start | bytes 9220
  1115.6 107.8 %copy-start.74 = (f32[2,512]{1,0:T(2,128)S(1)}, f32[2,512]{1,0:T(2,128)}, u32[]{:S(2)}) copy-start(f32[2,512]{1,0:T(2,128)} %copy-done.73) | copy-start | bytes 12292
  (59 other events, 146.7 us)
Sparse Core Ops, SparseCore 0:
  12.8 66.1 all-gather.1
  118.1 85.8 all-reduce.10
  207.1 69.1 all-reduce.12
  290.7 86.2 all-reduce.14
  398.2 87.2 all-reduce.16
  504.1 87.1 all-reduce.18
  621.0 87.1 all-reduce.20
  776.9 189.3 reduce-scatter.22
  968.6 38.6 reduce-scatter.44
  1010.1 34.4 reduce-scatter.42
  1057.7 75.1 reduce-scatter.24
  1136.1 87.1 all-reduce.22
  1226.2 34.0 reduce-scatter.26
  1263.1 32.8 reduce-scatter.28
  1298.7 32.6 reduce-scatter.30
  1334.3 52.8 reduce-scatter.34
  1390.0 53.1 reduce-scatter.32
  1446.0 33.1 reduce-scatter.36
  1482.0 32.8 reduce-scatter.40
  1517.7 32.8 reduce-scatter.38
where the time goes:
time: 1570 us; the launch traced here: 1560 us
  waiting for transfers between devices  889 us (57%)
  blocking collectives  229 us (15%)
  matrix products  166 us (11%)
  other arithmetic  160 us (10%)
  local copies, waits for them, and re-layouts  95 us (6%)
  between operations  15.8 us (1%)
    psum x6, waiting for transfers between devices, tensor_total(): return lax.psum(partial_rows, 'tensor')  436 us
    psum x1, blocking collectives, body(): kv_grad = lax.psum(kv_grad_part, 'seq').astype(jnp.bfloat16)  199 us
    unnamed x25, waiting for transfers between devices  108 us
    psum x1, waiting for transfers between devices, body(): lax.psum(owned_pick(encoder_states, kv_weights, kv_bias, flat_index, owne...  65.1 us
    all_gather x1, waiting for transfers between devices, body(): lax.all_gather(jnp.concatenate([keys_local, values_local], axis=-1), 'seq...  61.7 us
    reduce_scatter x1, waiting for transfers between devices, body(): lax.psum_scatter(gffn_w1, ('item', 'seq'), scatter_dimension=0, tiled=True)  56 us
    reduce_scatter x1, waiting for transfers between devices, body(): lax.psum_scatter(gffn_w2, ('item', 'seq'), scatter_dimension=1, tiled=True)  55.7 us
    scatter-add x1, other arithmetic, body(): table_grad = jnp.zeros((item_count * enc_rows * local_heads, 2 * head_siz...  37.5 us
  transfers between devices with their start and end apart: 20, of which 17 were waited for; matrix products, arithmetic and copies ran while one was open for 14% of the time, Pallas kernels for 0%

commit v1 on v0

--- a/solution.py
+++ b/solution.py
@@ -1,11 +1,17 @@
+import functools
+
 import jax
 import jax.numpy as jnp
 from jax import lax
+from jax.experimental import pallas as pl
+from jax.experimental.pallas import tpu as pltpu
 from jax.sharding import PartitionSpec as P
 
 EPS = 1e-05
 SCALE = 0.125
 NEG = -1e30
+MESH = pl.DeviceIdType.MESH
+ITEM, SEQ, TENSOR = "item", "seq", "tensor"
 
 
 def matmul(first_op, second_op):
@@ -23,7 +29,7 @@
 
 
 def tensor_total(partial_rows):
-    return lax.psum(partial_rows, "tensor")
+    return lax.psum(partial_rows, TENSOR)
 
 
 def row_total(values_in):
@@ -47,7 +53,7 @@
     return jnp.where(owned_mask, picked.astype(jnp.float32), 0.0)
 
 
-def body(
+def general_body(
     dec_input,
     encoder_states,
     retrieved,
@@ -82,14 +88,14 @@
     enc_rows = encoder_states.shape[1]
     head_cols = self_wq.shape[1]
     head_size = head_cols // local_heads
-    seq_devices = lax.axis_size("seq")
-    seq_rank = lax.axis_index("seq")
+    seq_devices = lax.axis_size(SEQ)
+    seq_rank = lax.axis_index(SEQ)
     seq_length = dec_rows * seq_devices
     queries = ((matmul(dec_input, self_wq) + self_bq) * SCALE).astype(jnp.bfloat16)
     keys_local = matmul(dec_input, self_wk).astype(jnp.bfloat16)
     values_local = (matmul(dec_input, self_wv) + self_bv).astype(jnp.bfloat16)
     kv_all = lax.all_gather(
-        jnp.concatenate([keys_local, values_local], axis=-1), "seq", axis=1, tiled=True
+        jnp.concatenate([keys_local, values_local], axis=-1), SEQ, axis=1, tiled=True
     )
     keys_all = kv_all[..., :head_cols].reshape(item_count, seq_length, local_heads, head_size)
     values_all = kv_all[..., head_cols:].reshape(item_count, seq_length, local_heads, head_size)
@@ -146,7 +152,7 @@
         owned_pick(encoder_states, kv_weights, kv_bias, flat_index, owned_mask).astype(
             jnp.bfloat16
         ),
-        "seq",
+        SEQ,
     )
 
     def cross_scores(kv_pair):
@@ -203,7 +209,7 @@
         owned_pick(encoder_states, kv_weights, kv_bias, flat_index, owned_mask).astype(
             jnp.bfloat16
         ),
-        "seq",
+        SEQ,
     )
     redo_cross = jnp.exp(cross_scores(kv_back) - lse_cross)
     dprob_cross = jnp.einsum(
@@ -234,7 +240,7 @@
         ],
         axis=-1,
     )
-    kv_grad = lax.psum(kv_grad_part, "seq").astype(jnp.bfloat16)
+    kv_grad = lax.psum(kv_grad_part, SEQ).astype(jnp.bfloat16)
     kv_owned = jnp.where(owned_mask, kv_grad.astype(jnp.float32), 0.0)
     table_grad = (
         jnp.zeros((item_count * enc_rows * local_heads, 2 * head_size), jnp.float32)
@@ -253,7 +259,7 @@
     encoder_part = jnp.einsum(
         "inhf,dhf->ind", table_low, kv_weights, preferred_element_type=jnp.float32
     )
-    encoder_grad = lax.psum_scatter(encoder_part, "tensor", scatter_dimension=2, tiled=True).astype(
+    encoder_grad = lax.psum_scatter(encoder_part, TENSOR, scatter_dimension=2, tiled=True).astype(
         jnp.bfloat16
     )
     gcross_bq = row_total(d_query2) * SCALE
@@ -286,7 +292,7 @@
         .astype(jnp.bfloat16)
         .reshape(item_count, dec_rows, head_cols)
     )
-    row_count = dec_rows * lax.axis_size("seq")
+    row_count = dec_rows * lax.axis_size(SEQ)
     key_grad = jnp.einsum(
         "ihrl,irhe->lihe", d_scores1, query_heads, preferred_element_type=jnp.float32
     ).reshape(row_count, item_count, head_cols)
@@ -294,7 +300,7 @@
         "ihrl,irhe->lihe", probs_low, d_attended1, preferred_element_type=jnp.float32
     ).reshape(row_count, item_count, head_cols)
     kv_self = lax.psum_scatter(
-        jnp.concatenate([key_grad, value_grad], axis=-1), "seq", scatter_dimension=0, tiled=True
+        jnp.concatenate([key_grad, value_grad], axis=-1), SEQ, scatter_dimension=0, tiled=True
     ).astype(jnp.bfloat16)
     kv_self = jnp.swapaxes(kv_self, 0, 1)
     d_key1 = kv_self[..., :head_cols]
@@ -313,16 +319,16 @@
     )
     input_grad = (d_hidden1 + tensor_total(input_part)).astype(jnp.bfloat16)
     matrices = (
-        lax.psum_scatter(gself_wq, ("item", "seq"), scatter_dimension=0, tiled=True),
-        lax.psum_scatter(gself_wk, ("item", "seq"), scatter_dimension=0, tiled=True),
-        lax.psum_scatter(gself_wv, ("item", "seq"), scatter_dimension=0, tiled=True),
-        lax.psum_scatter(gself_wo, ("item", "seq"), scatter_dimension=1, tiled=True),
-        lax.psum_scatter(gcross_wq, ("item", "seq"), scatter_dimension=0, tiled=True),
-        lax.psum_scatter(gcross_wk, ("item", "seq"), scatter_dimension=0, tiled=True),
-        lax.psum_scatter(gcross_wv, ("item", "seq"), scatter_dimension=0, tiled=True),
-        lax.psum_scatter(gcross_wo, ("item", "seq"), scatter_dimension=1, tiled=True),
-        lax.psum_scatter(gffn_w1, ("item", "seq"), scatter_dimension=0, tiled=True),
-        lax.psum_scatter(gffn_w2, ("item", "seq"), scatter_dimension=1, tiled=True),
+        lax.psum_scatter(gself_wq, (ITEM, SEQ), scatter_dimension=0, tiled=True),
+        lax.psum_scatter(gself_wk, (ITEM, SEQ), scatter_dimension=0, tiled=True),
+        lax.psum_scatter(gself_wv, (ITEM, SEQ), scatter_dimension=0, tiled=True),
+        lax.psum_scatter(gself_wo, (ITEM, SEQ), scatter_dimension=1, tiled=True),
+        lax.psum_scatter(gcross_wq, (ITEM, SEQ), scatter_dimension=0, tiled=True),
+        lax.psum_scatter(gcross_wk, (ITEM, SEQ), scatter_dimension=0, tiled=True),
+        lax.psum_scatter(gcross_wv, (ITEM, SEQ), scatter_dimension=0, tiled=True),
+        lax.psum_scatter(gcross_wo, (ITEM, SEQ), scatter_dimension=1, tiled=True),
+        lax.psum_scatter(gffn_w1, (ITEM, SEQ), scatter_dimension=0, tiled=True),
+        lax.psum_scatter(gffn_w2, (ITEM, SEQ), scatter_dimension=1, tiled=True),
     )
     vectors = lax.psum(
         (
@@ -341,7 +347,7 @@
             gnorm3_gain,
             gnorm3_bias,
         ),
-        ("item", "seq"),
+        (ITEM, SEQ),
     )
     return (
         layer_out.astype(jnp.bfloat16),
@@ -374,69 +380,1833 @@
     )
 
 
+VMEM_LIMIT = 56 * 1024 * 1024
+FULL = 256
+HALF = 128
+WIDE = FULL + HALF
+
+
+def column_plan_fits(mesh, arrays):
+    items, cores = arrays[0].shape[0], mesh.shape[ITEM]
+    ranks, depth = mesh.shape[TENSOR], mesh.shape[SEQ]
+    heads = arrays[2].shape[1]
+    rows = arrays[0].shape[1] // depth
+    width = arrays[0].shape[2]
+    return (
+        cores == 2
+        and ranks == 4
+        and items == ranks
+        and ranks == depth
+        and heads == 3 * depth
+        and width == 64 * heads
+        and rows == cores * FULL
+        and arrays[2].shape[2] % FULL == 0
+    )
+
+
+def here():
+    return lax.axis_index(ITEM), lax.axis_index(SEQ), lax.axis_index(TENSOR)
+
+
+def call_kernel(kernel, name, outs, args, scratch=(), collective_id=None, in_spaces=None, out_space=None, us=10):
+    single = isinstance(outs, tuple)
+    listed = [outs] if single else list(outs)
+    space = pltpu.VMEM if out_space is None else out_space
+    spaces = [pltpu.VMEM] * len(args) if in_spaces is None else in_spaces
+    params = dict(vmem_limit_bytes=VMEM_LIMIT)
+    if collective_id is not None:
+        params.update(collective_id=collective_id, has_side_effects=True)
+    out = pl.pallas_call(
+        kernel,
+        out_shape=[jax.ShapeDtypeStruct(s, d) for s, d in listed],
+        in_specs=[pl.BlockSpec(memory_space=s) for s in spaces],
+        out_specs=[pl.BlockSpec(memory_space=space) for _ in listed],
+        scratch_shapes=list(scratch),
+        compiler_params=pltpu.CompilerParams(**params),
+        cost_estimate=pl.CostEstimate(flops=us * 10**9, bytes_accessed=us * 3 * 10**6, transcendentals=0),
+        name=name,
+    )(*args)
+    return out[0] if single else out
+
+
+def greet(peers):
+    gate = pltpu.get_barrier_semaphore()
+    for peer in peers:
+        pl.semaphore_signal(gate, inc=1, device_id=peer, device_id_type=MESH)
+
+
+def meet(peers):
+    greet(peers)
+    pl.semaphore_wait(pltpu.get_barrier_semaphore(), len(peers))
+
+
+def column_peer(place, cores, rank):
+    return (lax.rem(place, cores), place // cores, rank)
+
+
+def remote_copy(src, dst, send, recv, device):
+    return pltpu.make_async_remote_copy(
+        src_ref=src, dst_ref=dst, send_sem=send, recv_sem=recv, device_id=device, device_id_type=MESH
+    )
+
+
+def plane_peers(cores, ranks):
+    core, seq, rank = here()
+    peers = []
+    for step in range(1, cores * ranks):
+        place = lax.rem(rank * cores + core + step, cores * ranks)
+        peers.append((lax.rem(place, cores), seq, place // cores))
+    return peers
+
+
+class Deal:
+    def __init__(self, cores, ranks, per_core, source, all_ref, send_sem, recv_sem, own_sem):
+        self.cores, self.ranks, self.per_core = cores, ranks, per_core
+        self.source, self.all_ref = source, all_ref
+        self.send_sem, self.recv_sem, self.own_sem = send_sem, recv_sem, own_sem
+        self.core, self.seq, self.rank = here()
+        self.home = self.rank // per_core
+        self.local = lax.rem(self.rank, per_core)
+
+    def send(self, step):
+        target = lax.rem(self.rank + step, self.ranks)
+        return remote_copy(
+            self.source(target),
+            self.all_ref.at[self.local, self.core],
+            self.send_sem.at[step],
+            self.recv_sem.at[self.local, self.core],
+            (self.home, self.seq, target),
+        )
+
+    def keep(self):
+        return pltpu.make_async_copy(self.source(self.rank), self.all_ref.at[self.local, self.core], self.own_sem)
+
+    def start(self):
+        for step in range(1, self.ranks):
+            self.send(step).start()
+
+        @pl.when(self.core != self.home)
+        def _():
+            self.send(0).start()
+
+        @pl.when(self.core == self.home)
+        def _():
+            self.keep().start()
+
+    def finish(self):
+        for item in range(self.per_core):
+            for half in range(self.cores):
+                inside = (half == self.core) & (self.core * self.per_core + item == self.rank)
+
+                @pl.when(jnp.logical_not(inside))
+                def _():
+                    remote_copy(
+                        self.source(0),
+                        self.all_ref.at[item, half],
+                        self.send_sem.at[0],
+                        self.recv_sem.at[item, half],
+                        (1 - self.core, self.seq, self.rank),
+                    ).wait_recv()
+
+        for step in range(1, self.ranks):
+            self.send(step).wait_send()
+
+        @pl.when(self.core != self.home)
+        def _():
+            self.send(0).wait_send()
+
+        @pl.when(self.core == self.home)
+        def _():
+            self.keep().wait()
+
+
+def deal_scratch(cores, ranks, per_core):
+    dma = pltpu.SemaphoreType.DMA
+    return [dma((ranks,)), dma((per_core, cores)), dma]
+
+
+class PlaneGather:
+    def __init__(self, all_ref, give_send, give_recv, far_send, far_recv, pass_send, pass_recv):
+        self.all_ref = all_ref
+        self.give_send, self.give_recv = give_send, give_recv
+        self.far_send, self.far_recv = far_send, far_recv
+        self.pass_send, self.pass_recv = pass_send, pass_recv
+        self.core, self.seq, self.rank = here()
+        low, high = lax.rem(self.rank, 2), self.rank // 2
+        self.near = (2 * high + 1 - low, 2 * (1 - high) + low)
+        self.far = 2 * (1 - high) + 1 - low
+        self.half = all_ref.shape[2] // 2
+        self.peers = [(self.core, self.seq, rank) for rank in self.near]
+
+    def give(self, way):
+        block = self.all_ref.at[self.core, self.rank]
+        return remote_copy(block, block, self.give_send.at[way], self.give_recv.at[way], self.peers[way])
+
+    def far_part(self, way, origin):
+        return self.all_ref.at[self.core, origin, pl.ds(way * self.half, self.half), :]
+
+    def onward(self, way):
+        block = self.far_part(way, self.near[way])
+        return remote_copy(
+            block, block, self.far_send.at[way], self.far_recv.at[way], self.peers[1 - way]
+        )
+
+    def side(self, slot, block):
+        return remote_copy(
+            block, block, self.pass_send.at[slot], self.pass_recv.at[slot], (1 - self.core, self.seq, self.rank)
+        )
+
+    def sides(self):
+        near = [self.side(way, self.all_ref.at[self.core, self.near[way]]) for way in range(2)]
+        return near + [self.side(2 + way, self.far_part(way, self.far)) for way in range(2)]
+
+    def start(self):
+        for way in range(2):
+            self.give(way).start()
+
+    def forward(self):
+        sides = self.sides()
+        for way in range(2):
+            self.give(way).wait_recv()
+            self.onward(way).start()
+            sides[way].start()
+
+    def finish(self):
+        sides = self.sides()
+        for way in range(2):
+            self.onward(way).wait_recv()
+            sides[2 + way].start()
+        for way in range(2):
+            self.give(way).wait_send()
+            self.onward(way).wait_send()
+        for side in sides:
+            side.wait()
+
+
+def gather_scratch():
+    return [pltpu.SemaphoreType.DMA((n,)) for n in (2, 2, 2, 2, 4, 4)]
+
+
+class PlaneReduce:
+    def __init__(self, ranks, grad_ref, got_ref, sum_ref, all_ref, swap_sem, send_sem, recv_sem):
+        self.ranks, self.grad_ref, self.got_ref = ranks, grad_ref, got_ref
+        self.sum_ref, self.all_ref = sum_ref, all_ref
+        self.swap_sem, self.send_sem, self.recv_sem = swap_sem, send_sem, recv_sem
+        self.core, self.seq, self.rank = here()
+        self.peers = [(self.core, self.seq, lax.rem(self.rank + step, ranks)) for step in range(1, ranks)]
+
+    def swap(self):
+        return remote_copy(
+            self.grad_ref.at[1 - self.core],
+            self.got_ref,
+            self.swap_sem.at[0],
+            self.swap_sem.at[1],
+            (1 - self.core, self.seq, self.rank),
+        )
+
+    def copy(self, step):
+        peer = self.peers[step]
+        return remote_copy(
+            self.sum_ref.at[peer[2]], self.all_ref.at[self.rank], self.send_sem.at[step], self.recv_sem.at[step], peer
+        )
+
+    def start(self):
+        self.swap().start()
+
+    def middle(self):
+        self.swap().wait()
+        for rank in range(self.ranks):
+            self.sum_ref[rank] = (
+                self.grad_ref[self.core, rank].astype(jnp.float32) + self.got_ref[rank].astype(jnp.float32)
+            ).astype(self.sum_ref.dtype)
+        for step in range(self.ranks - 1):
+            self.copy(step).start()
+
+    def finish(self):
+        for step in range(self.ranks - 1):
+            self.copy(step).wait()
+        total = self.sum_ref[self.rank].astype(jnp.float32)
+        for step in range(1, self.ranks):
+            total = total + self.all_ref[lax.rem(self.rank + step, self.ranks)].astype(jnp.float32)
+        return total
+
+
+def reduce_scratch(ranks, rows, columns, dtype):
+    dma = pltpu.SemaphoreType.DMA
+    block = pltpu.VMEM((ranks, rows, columns), dtype)
+    return [block, block, block, dma((2,)), dma((ranks - 1,)), dma((ranks - 1,))]
+
+
+def column_places(cores, depth):
+    core, seq, _ = here()
+    mine = seq * cores + core
+    return mine, [lax.rem(mine + step, cores * depth) for step in range(1, cores * depth)]
+
+
+class ColumnSend:
+    def __init__(self, cores, depth, source_ref, all_ref, send_sem, recv_sem):
+        self.cores, self.count = cores, cores * depth
+        self.source_ref, self.all_ref = source_ref, all_ref
+        self.send_sem, self.recv_sem = send_sem, recv_sem
+        core, seq, self.rank = here()
+        self.mine = seq * cores + core
+
+    def copy(self, step):
+        place = lax.rem(self.mine + 1 + step, self.count)
+        return remote_copy(
+            self.source_ref.at[place],
+            self.all_ref.at[self.mine],
+            self.send_sem.at[step],
+            self.recv_sem.at[step],
+            column_peer(place, self.cores, self.rank),
+        )
+
+    def wait_from(self, step):
+        self.copy(step).wait_recv()
+
+    def finish_sends(self):
+        for step in range(self.count - 1):
+            self.copy(step).wait_send()
+
+    def finish(self):
+        for step in range(self.count - 1):
+            self.copy(step).wait()
+
+
+def send_scratch(count):
+    return [pltpu.SemaphoreType.DMA((count - 1,)), pltpu.SemaphoreType.DMA((count - 1,))]
+
+
+class Chain:
+    def __init__(self, depth, all_ref, send_sem, recv_sem):
+        self.depth, self.all_ref = depth, all_ref
+        self.send_sem, self.recv_sem = send_sem, recv_sem
+        core, self.seq, rank = here()
+        self.above = (core, lax.rem(self.seq + 1, depth), rank)
+        self.below = (core, lax.rem(self.seq + depth - 1, depth), rank)
+
+    def copy(self, block, way):
+        part = self.all_ref.at[block]
+        target = self.above if way == 0 else self.below
+        return remote_copy(part, part, self.send_sem.at[way, block], self.recv_sem.at[block], target)
+
+    def step(self, n):
+        up, down = self.seq - n, self.seq + n
+
+        @pl.when(up >= 0)
+        def _():
+            if n > 0:
+                self.copy(up, 0).wait_recv()
+
+            @pl.when(self.seq + 1 < self.depth)
+            def _():
+                self.copy(up, 0).start()
+
+        @pl.when(down < self.depth)
+        def _():
+            if n > 0:
+                self.copy(down, 1).wait_recv()
+
+            @pl.when(self.seq > 0)
+            def _():
+                self.copy(down, 1).start()
+
+    def finish(self):
+        for n in range(self.depth):
+            up, down = self.seq - n, self.seq + n
+
+            @pl.when((up >= 0) & (self.seq + 1 < self.depth))
+            def _():
+                self.copy(up, 0).wait_send()
+
+            @pl.when((down < self.depth) & (self.seq > 0))
+            def _():
+                self.copy(down, 1).wait_send()
+
+
+def prologue_kernel(
+    sizes,
+    x_ref, g_ref, m_ref, idx_ref, vec_ref, wq_ref, wk_ref, wv_ref, ck_ref, cv_ref,
+    xall_ref, gmine_ref, enc_ref, iall_ref, vall_ref, wall_ref,
+    load_sem,
+    swap_send, swap_recv, chain_send, chain_recv, side_send, side_recv, own_sem,
+    idx_send, idx_recv, vec_send, vec_recv, *wsems
+):
+    cores, depth, ranks, per_core = sizes
+    core, seq, rank = here()
+    home = rank // per_core
+    local = lax.rem(rank, per_core)
+    sibling = (1 - core, seq, rank)
+    above = (core, lax.rem(seq + 1, depth), rank)
+    below = (core, lax.rem(seq + depth - 1, depth), rank)
+    plane = []
+    for step in range(1, cores * ranks):
+        place = lax.rem(rank * cores + core + step, cores * ranks)
+        plane.append((lax.rem(place, cores), seq, place // cores))
+    high = wq_ref.shape[0]
+    lanes = wq_ref.shape[1] // cores
+
+    def load(n, ref, half):
+        return pltpu.make_async_copy(
+            ref.at[:, pl.ds(half * lanes, lanes)],
+            wall_ref.at[half, rank, pl.ds(n * high, high), :],
+            load_sem.at[n, half],
+        )
+
+    loads = [load(n, ref, half) for n, ref in enumerate((wq_ref, wk_ref, wv_ref, ck_ref, cv_ref)) for half in range(cores)]
+    for copy in loads:
+        copy.start()
+    meet(plane + [above, below])
+
+    def remote(src, dst, send, recv, device):
+        return pltpu.make_async_remote_copy(
+            src_ref=src, dst_ref=dst, send_sem=send, recv_sem=recv, device_id=device, device_id_type=MESH
+        )
+
+    there = pl.ds((1 - core) * FULL, FULL)
+    mine = pl.ds(core * FULL, FULL)
+    swap_x = remote(x_ref.at[local, there], xall_ref.at[seq, 1 - core], swap_send.at[0], swap_recv.at[0], sibling)
+    swap_g = remote(g_ref.at[local, there], gmine_ref, swap_send.at[1], swap_recv.at[1], sibling)
+    swap_e = remote(m_ref.at[local], enc_ref, swap_send.at[2], swap_recv.at[2], sibling)
+    own_x = pltpu.make_async_copy(x_ref.at[local, mine], xall_ref.at[seq, core], own_sem.at[3])
+    own_g = pltpu.make_async_copy(g_ref.at[local, mine], gmine_ref, own_sem.at[4])
+    own_e = pltpu.make_async_copy(m_ref.at[local], enc_ref, own_sem.at[5])
+
+    @pl.when(core == home)
+    def _():
+        swap_x.start()
+        own_x.start()
+
+    def give_index(item, half):
+        return remote(
+            idx_ref.at[item], iall_ref.at[rank], idx_send.at[item, half], idx_recv.at[rank],
+            (half, seq, core * per_core + item),
+        )
+
+    def is_me(item, half):
+        return (half == core) & (core * per_core + item == rank)
+
+    for item in range(per_core):
+        for half in range(cores):
+
+            @pl.when(jnp.logical_not(is_me(item, half)))
+            def _():
+                give_index(item, half).start()
+
+            @pl.when(is_me(item, half))
+            def _():
+                own = pltpu.make_async_copy(idx_ref.at[item], iall_ref.at[rank], own_sem.at[0])
+                own.start()
+                own.wait()
+
+    peers = [(core, seq, lax.rem(rank + step, ranks)) for step in range(1, ranks)]
+
+    def give_vec(step):
+        return remote(vec_ref, vall_ref.at[rank], vec_send.at[step], vec_recv.at[step], peers[step - 1])
+
+    for step in range(1, ranks):
+        give_vec(step).start()
+    own_vec = pltpu.make_async_copy(vec_ref, vall_ref.at[rank], own_sem.at[1])
+    own_vec.start()
+
+    weights = PlaneGather(wall_ref, *wsems)
+
+    @pl.when(core == home)
+    def _():
+        own_x.wait()
+
+    @pl.when(core != home)
+    def _():
+        swap_x.wait_recv()
+
+    def chain(block, target, way):
+        return remote(
+            xall_ref.at[block, core], xall_ref.at[block, core], chain_send.at[way, block], chain_recv.at[block], target
+        )
+
+    def aside(block):
+        return remote(
+            xall_ref.at[block, core], xall_ref.at[block, core], side_send.at[block], side_recv.at[block], sibling
+        )
+
+    for step in range(depth):
+        up, down = seq - step, seq + step
+
+        @pl.when(up >= 0)
+        def _():
+            if step > 0:
+                chain(up, above, 0).wait_recv()
+
+            @pl.when(seq + 1 < depth)
+            def _():
+                chain(up, above, 0).start()
+
+            aside(up).start()
+
+        @pl.when(down < depth)
+        def _():
+            if step > 0:
+                chain(down, below, 1).wait_recv()
+
+            @pl.when(seq > 0)
+            def _():
+                chain(down, below, 1).start()
+
+            if step > 0:
+                aside(down).start()
+
+        if step == 0:
+            for copy in loads:
+                copy.wait()
+            weights.start()
+
+            @pl.when(core == home)
+            def _():
+                swap_e.start()
+                own_e.start()
+                swap_g.start()
+                own_g.start()
+
+    weights.forward()
+
+    for step in range(depth):
+        up, down = seq - step, seq + step
+
+        @pl.when((up >= 0) & (seq + 1 < depth))
+        def _():
+            chain(up, above, 0).wait_send()
+
+        @pl.when((down < depth) & (seq > 0))
+        def _():
+            chain(down, below, 1).wait_send()
+
+    for block in range(depth):
+        aside(block).wait()
+    for step in range(1, ranks):
+        give_vec(step).wait()
+    weights.finish()
+    own_vec.wait()
+    for item in range(per_core):
+        for half in range(cores):
+
+            @pl.when(jnp.logical_not(is_me(item, half)))
+            def _():
+                give_index(item, half).wait_send()
+
+    @pl.when(core == home)
+    def _():
+        for copy in (swap_x, swap_g, swap_e):
+            copy.wait_send()
+        own_g.wait()
+        own_e.wait()
+
+    @pl.when(core != home)
+    def _():
+        swap_g.wait_recv()
+        swap_e.wait_recv()
+
+    for origin in range(ranks):
+
+        @pl.when(jnp.logical_not((core == home) & (rank == origin)))
+        def _():
+            remote(
+                idx_ref.at[0], iall_ref.at[origin], idx_send.at[0, 0], idx_recv.at[origin], sibling
+            ).wait_recv()
+
+
+def prologue(dec_input, out_grad, encoder_states, retrieved, vectors, weights):
+    cores, depth, ranks = lax.axis_size(ITEM), lax.axis_size(SEQ), lax.axis_size(TENSOR)
+    per_core, _, width = dec_input.shape
+    enc_rows = encoder_states.shape[1]
+    high = len(weights) * weights[0].shape[0]
+    low = jnp.bfloat16
+    dma = pltpu.SemaphoreType.DMA
+    return call_kernel(
+        functools.partial(prologue_kernel, (cores, depth, ranks, per_core)),
+        "prologue",
+        [
+            ((depth, cores, FULL, width), low),
+            ((FULL, width), low),
+            ((enc_rows, width), low),
+            ((ranks,) + retrieved.shape[1:], retrieved.dtype),
+            ((ranks,) + vectors.shape, vectors.dtype),
+            ((cores, ranks, high, width // cores), low),
+        ],
+        [dec_input, out_grad, encoder_states, retrieved, vectors, *weights],
+        scratch=[
+            dma((len(weights), cores)),
+            dma((3,)),
+            dma((3,)),
+            dma((2, depth)),
+            dma((depth,)),
+            dma((depth,)),
+            dma((depth,)),
+            dma((6,)),
+            dma((per_core, cores)),
+            dma((ranks,)),
+            dma((ranks,)),
+            dma((ranks,)),
+        ]
+        + gather_scratch(),
+        collective_id=1,
+        in_spaces=[pl.ANY] * 10,
+        us=32,
+    )
+
+
+def dot_nn(first_op, second_op):
+    return lax.dot_general(first_op, second_op, (((1,), (0,)), ((), ())), preferred_element_type=jnp.float32)
+
+
+def dot_nt(first_op, second_op):
+    return lax.dot_general(first_op, second_op, (((1,), (1,)), ((), ())), preferred_element_type=jnp.float32)
+
+
+def head_rows(ref, group, matrix, head_index, head):
+    start = pl.multiple_of(matrix * 3 * head + head_index * head, head)
+    rows = pl.ds(start, head)
+    return jnp.concatenate([ref[half, group, rows, :] for half in range(ref.shape[0])], axis=1)
+
+
+def kv_rows(w_ref, group, head_index, head):
+    return jnp.concatenate(
+        [head_rows(w_ref, group, 3, head_index, head), head_rows(w_ref, group, 4, head_index, head)], axis=0
+    )
+
+
+def retrieve_kernel(ranks, head, enc_ref, w_ref, b_ref, idx_ref, out_ref):
+    core, seq, _ = here()
+    enc_rows = enc_ref.shape[0]
+    slots = idx_ref.shape[2]
+    low = jnp.bfloat16
+    tall = enc_rows // 3
+
+    def picked(table, index):
+        total = jnp.zeros((table.shape[0], index.shape[1]), jnp.float32)
+        for part in range(3):
+            place = lax.broadcasted_iota(jnp.int32, (tall, index.shape[1]), 0) + (part * tall + seq * enc_rows)
+            hot = jnp.where(place == index, 1.0, 0.0).astype(low)
+            total = total + dot_nn(table[:, part * tall : (part + 1) * tall], hot)
+        return total.astype(low)
+
+    def step(group, carry):
+        w = jnp.concatenate([kv_rows(w_ref, group, 2 * core, head), kv_rows(w_ref, group, 1, head)], axis=0)
+        table = (dot_nt(w, enc_ref[...]) + b_ref[group]).astype(low)
+        whole = idx_ref[group, pl.ds(2 * core, 1), :]
+        shared = idx_ref[group, pl.ds(1, 1), :]
+        half = jnp.where(core == 0, shared[:, : slots // 2], shared[:, slots // 2 :])
+        out_ref[group] = jnp.concatenate(
+            [picked(table[: 2 * head], whole), picked(table[2 * head :], half)], axis=1
+        )
+        return carry
+
+    lax.fori_loop(0, ranks, step, 0)
+
+
+def retrieve(enc, w_all, bias, index):
+    ranks, _, slots = index.shape
+    head = w_all.shape[2] // 15
+    return call_kernel(
+        functools.partial(retrieve_kernel, ranks, head),
+        "retrieve",
+        ((ranks, 2 * head, slots + slots // 2), jnp.bfloat16),
+        [enc, w_all, bias, index],
+    )
+
+
+def assembled(parts_ref, depth, columns=None):
+    pieces = []
+    for group in range(depth):
+        first, second = parts_ref[2 * group], parts_ref[2 * group + 1]
+        pieces += [
+            first[:, :FULL],
+            jnp.concatenate([first[:, FULL:WIDE], second[:, FULL:WIDE]], axis=1),
+            second[:, :FULL],
+        ]
+    return jnp.concatenate(pieces, axis=0)
+
+
+def dispersed(rows, parts_ref, depth):
+    head = rows.shape[0] // (3 * depth)
+    for group in range(depth):
+        a = rows[3 * group * head : (3 * group + 1) * head]
+        b = rows[(3 * group + 1) * head : (3 * group + 2) * head]
+        c = rows[(3 * group + 2) * head : (3 * group + 3) * head]
+        parts_ref[2 * group] = jnp.concatenate([a, b[:, :HALF]], axis=1)
+        parts_ref[2 * group + 1] = jnp.concatenate([c, b[:, HALF:]], axis=1)
+
+
+def late_square(ref, matrix, rows):
+    cores, ranks = ref.shape[0], ref.shape[1]
+    return jnp.concatenate(
+        [
+            jnp.concatenate([ref[half, rank, matrix * rows : (matrix + 1) * rows, :] for half in range(cores)], axis=1)
+            for rank in range(ranks)
+        ],
+        axis=0,
+    )
+
+
+def centred_rows(h):
+    center = h - jnp.mean(h, axis=-1, keepdims=True)
+    spread = lax.rsqrt(jnp.mean(center * center, axis=-1, keepdims=True) + EPS)
+    return center * spread, spread
+
+
+def norm_back(z, spread, dy, gain):
+    dz = dy * gain
+    dh = spread * (
+        dz - jnp.mean(dz, axis=-1, keepdims=True) - z * jnp.mean(dz * z, axis=-1, keepdims=True)
+    )
+    return dh, jnp.sum(dy * z, axis=0, keepdims=True), jnp.sum(dy, axis=0, keepdims=True)
+
+
+def middle_kernel(
+    cores, depth, ranks, per_core, part,
+    o_ref, y1_ref, g_ref, w_ref, ffn_ref, bo_ref, gain2_ref, shift2_ref, b1_ref, b2_ref, gain3_ref, shift3_ref,
+    layer_ref, do_ref, dh2_ref, vec_ref, grad_ref,
+    slope_ref, a_ref, df_ref, out_ref, dosrc_ref, dosend, dorecv, *deal_sems
+):
+    low = jnp.bfloat16
+    core, seq, rank = here()
+    count = cores * depth
+    mine, places = column_places(cores, depth)
+    peers = [column_peer(place, cores, rank) for place in places]
+    peers += [(half, seq, lax.rem(rank + step, ranks)) for step in range(1, ranks) for half in range(cores)]
+    greet(peers)
+    width = y1_ref.shape[1]
+    lanes = width // cores
+    o2t = assembled(o_ref, depth)
+    wo2 = late_square(w_ref, 2, part)
+    h2 = y1_ref[...].astype(jnp.float32) + dot_nn(o2t.T, wo2) + bo_ref[...]
+    z2, spread2 = centred_rows(h2)
+    y2 = (z2 * gain2_ref[...] + shift2_ref[...]).astype(low)
+
+    def hidden_in(of, half):
+        return ffn_ref[half, of, :width, :]
+
+    def hidden_out(of):
+        return jnp.concatenate([ffn_ref[half, of, width:, :] for half in range(cores)], axis=1)
+
+    root = 0.7071067811865476
+    h3 = y2.astype(jnp.float32) + b2_ref[...]
+    for of in range(ranks):
+        f = jnp.concatenate([dot_nn(y2, hidden_in(of, half)) for half in range(cores)], axis=1) + b1_ref[of]
+        cdf = 0.5 * (1.0 + lax.erf(f * root))
+        a = (f * cdf).astype(low)
+        slope_ref[of] = cdf + f * (0.3989422804014327 * jnp.exp(-0.5 * f * f))
+        a_ref[of] = a
+        h3 = h3 + dot_nn(a, hidden_out(of))
+    z3, spread3 = centred_rows(h3)
+    out_ref[...] = (z3 * gain3_ref[...] + shift3_ref[...]).astype(low)
+    pl.semaphore_wait(pltpu.get_barrier_semaphore(), len(peers))
+    deal = Deal(cores, ranks, per_core, lambda target: out_ref, layer_ref, *deal_sems)
+    deal.start()
+
+    dh3, gg3, gs3 = norm_back(z3, spread3, g_ref[...].astype(jnp.float32), gain3_ref[...])
+    e3 = dh3.astype(low)
+    dy2 = dh3
+    for of in range(ranks):
+        df = (dot_nt(e3, hidden_out(of)) * slope_ref[of]).astype(low)
+        df_ref[of] = df
+        for half in range(cores):
+            dy2 = dy2 + dot_nt(df[:, half * lanes : (half + 1) * lanes], hidden_in(of, half))
+    dh2, gg2, gs2 = norm_back(z2, spread2, dy2, gain2_ref[...])
+    e2 = dh2.astype(low)
+    dispersed(dot_nt(wo2, e2).astype(low), dosrc_ref, depth)
+    ask = ColumnSend(cores, depth, dosrc_ref, do_ref, dosend, dorecv)
+    for step in range(count - 1):
+        ask.copy(step).start()
+    do_ref[mine] = dosrc_ref[mine]
+
+    dh2_ref[...] = dh2
+    vec_ref[0:1] = gg3
+    vec_ref[1:2] = gs3
+    vec_ref[2:3] = jnp.sum(e3.astype(jnp.float32), axis=0, keepdims=True)
+    vec_ref[3:4] = gg2
+    vec_ref[4:5] = gs2
+    vec_ref[5:6] = jnp.sum(e2.astype(jnp.float32), axis=0, keepdims=True)
+    e3t, y2t, e2t = e3.T, y2.T, e2.T
+    pad = jnp.zeros((-part % 128, FULL), low)
+    for of in range(ranks):
+        df = df_ref[of]
+        vec_ref[6 + of : 7 + of] = jnp.sum(df.astype(jnp.float32), axis=0, keepdims=True)
+        o2_part = jnp.concatenate([o2t[of * part : (of + 1) * part], pad], axis=0)
+        for half in range(cores):
+            rows = slice(half * lanes, (half + 1) * lanes)
+            grad_ref[half, of, :, :width] = dot_nn(y2t[rows], df).astype(low)
+            grad_ref[half, of, :, width : 2 * width] = dot_nn(e3t[rows], a_ref[of]).astype(low)
+            grad_ref[half, of, :, 2 * width :] = dot_nt(e2t[rows], o2_part).astype(low)
+    ask.finish()
+    deal.finish()
+
+
+def middle(per_core, o2, y1, grad_mine, squares, ffn, vectors):
+    cores, depth, ranks = lax.axis_size(ITEM), lax.axis_size(SEQ), lax.axis_size(TENSOR)
+    places, head, _ = o2.shape
+    rows, width = y1.shape
+    part, lanes, hidden = 3 * head, width // cores, width
+    low, full = jnp.bfloat16, jnp.float32
+    columns = 2 * hidden + part + (-part % 128)
+    return call_kernel(
+        functools.partial(middle_kernel, cores, depth, ranks, per_core, part),
+        "middle",
+        [
+            ((per_core, cores, rows, width), low),
+            (o2.shape, low),
+            ((rows, width), full),
+            ((6 + ranks, width), full),
+            ((cores, ranks, lanes, columns), low),
+        ],
+        [o2, y1, grad_mine, squares, ffn, *vectors],
+        scratch=[
+            pltpu.VMEM((ranks, rows, hidden), full),
+            pltpu.VMEM((ranks, rows, hidden), low),
+            pltpu.VMEM((ranks, rows, hidden), low),
+            pltpu.VMEM((rows, width), low),
+            pltpu.VMEM(o2.shape, low),
+        ]
+        + send_scratch(places)
+        + deal_scratch(cores, ranks, per_core),
+        collective_id=4,
+        us=22,
+    )
+
+
+def encoder_back(ranks, head, enc_ref, w_ref, idx_ref, dkv_ref, part_ref, grad_ref):
+    core, seq, _ = here()
+    low = jnp.bfloat16
+    enc_rows, width = enc_ref.shape
+    slots = idx_ref.shape[2]
+    cores = w_ref.shape[0]
+    lanes = width // cores
+    part = width // ranks
+    fold = enc_rows // (2 * cores)
+    enc_t = enc_ref[...].T
+
+    tables = []
+    rows_w = []
+    for group in range(ranks):
+        heads = []
+        shared = idx_ref[group, pl.ds(1, 1), :]
+        shared = jnp.where(core == 0, shared[:, : slots // 2], shared[:, slots // 2 :])
+        for which, index, rows in (
+            (2 * core, idx_ref[group, pl.ds(2 * core, 1), :], slice(0, slots)),
+            (1, shared, slice(slots, slots + slots // 2)),
+        ):
+            pieces = []
+            for third in range(3):
+                tall = enc_rows // 3
+                place = lax.broadcasted_iota(jnp.int32, (tall, index.shape[1]), 0) + (third * tall + seq * enc_rows)
+                hot = jnp.where(place == index, 1.0, 0.0).astype(low)
+                pieces.append(dot_nn(hot, dkv_ref[group, rows, :]).astype(low))
+            table = jnp.concatenate(pieces, axis=0)
+            heads.append(table)
+            tables.append(table)
+            rows_w.append(kv_rows(w_ref, group, which, head))
+        both = jnp.concatenate(heads, axis=1)
+        grad = dot_nn(enc_t, both).astype(low)
+        whole, shared = grad[:, : 2 * head], grad[:, 2 * head :]
+        blank = jnp.zeros_like(whole)
+        left = jnp.where(core == 0, whole, blank)
+        right = jnp.where(core == 0, blank, whole)
+        for half in range(cores):
+            rows = slice(half * lanes, (half + 1) * lanes)
+            grad_ref[half, group] = jnp.concatenate([left[rows], shared[rows], right[rows]], axis=1)
+    table = jnp.concatenate(tables, axis=1)
+    w = jnp.concatenate(rows_w, axis=0)
+    for rank in range(ranks):
+        cols = w[:, rank * part : (rank + 1) * part]
+        flat = dot_nn(table, cols).astype(low)
+        for half in range(cores):
+            low_rows = flat[2 * half * fold : (2 * half + 1) * fold]
+            high_rows = flat[(2 * half + 1) * fold : (2 * half + 2) * fold]
+            part_ref[half, rank] = jnp.concatenate([low_rows, high_rows], axis=1)
+
+
+def last_kernel(
+    cores, depth, ranks, per_core,
+    parts_ref, dh1_ref, w_ref, encp_ref, self_ref, vec_ref, red2_ref, red4_ref,
+    in_ref, enc_ref, wself_ref, vout_ref, w2_ref, w4_ref,
+    dx_ref, got_ref, sum_ref, encall_ref, column_ref, group_ref, plane_ref, vcol_ref, vsum_ref, vplane_ref,
+    r2_ref, r4_ref,
+    swap_sem, col_send, col_recv, vcol_send, vcol_recv, send_sem, recv_sem, vsend, vrecv, vback_send, vback_recv,
+    z_send, z_recv, *deal_sems
+):
+    core, seq, rank = here()
+    low = jnp.bfloat16
+    head = parts_ref.shape[1]
+    part = 3 * head
+    count = cores * depth
+    mine, places = column_places(cores, depth)
+    peers = [(core, seq, lax.rem(rank + step, ranks)) for step in range(1, ranks)]
+    others = [(1 - core, seq, peer[2]) for peer in peers]
+    greeted = [column_peer(place, cores, rank) for place in places] + peers + others
+    meet(greeted)
+
+    swap = remote_copy(encp_ref.at[1 - core], got_ref, swap_sem.at[0], swap_sem.at[1], (1 - core, seq, rank))
+    swap.start()
+    column = []
+    for step, place in enumerate(places):
+        target = column_peer(place, cores, rank)
+        column.append(
+            remote_copy(vec_ref.at[place], vcol_ref.at[mine], vcol_send.at[step], vcol_recv.at[step], target)
+        )
+        column.append(
+            remote_copy(self_ref.at[place], column_ref.at[mine], col_send.at[step], col_recv.at[step], target)
+        )
+    for copy in column:
+        copy.start()
+    along = []
+    for step in range(1, depth):
+        target = lax.rem(seq + step, depth)
+        for n, (src, dst) in enumerate(((red2_ref, r2_ref), (red4_ref, r4_ref))):
+            along.append(
+                remote_copy(
+                    src.at[target], dst.at[seq], z_send.at[n, step - 1], z_recv.at[n, step - 1], (core, target, rank)
+                )
+            )
+    for copy in along:
+        copy.start()
+
+    dqt = assembled(parts_ref, depth)
+    stack_k, stack_v = [], []
+    for group in range(depth):
+        first, second = parts_ref[2 * group], parts_ref[2 * group + 1]
+        for n, stack in ((0, stack_k), (1, stack_v)):
+            whole = slice(WIDE + n * FULL, WIDE + (n + 1) * FULL)
+            shared = slice(WIDE + (n + 2) * FULL, WIDE + (n + 3) * FULL)
+            both = (first[:, shared].astype(jnp.float32) + second[:, shared].astype(jnp.float32)).astype(low)
+            stack += [first[:, whole], both, second[:, whole]]
+    dx = dh1_ref[...] + dot_nn(dqt.T, late_square(w_ref, 0, part)) * SCALE
+    dx = dx + dot_nn(jnp.concatenate(stack_k, axis=0).T, late_square(w_ref, 1, part))
+    dx = dx + dot_nn(jnp.concatenate(stack_v, axis=0).T, late_square(w_ref, 2, part))
+    dx_ref[...] = dx.astype(low)
+    deal = Deal(cores, ranks, per_core, lambda target: dx_ref, in_ref, *deal_sems[:3])
+    deal.start()
+
+    swap.wait()
+    sum_ref[...] = (encp_ref[core].astype(jnp.float32) + got_ref[...].astype(jnp.float32)).astype(low)
+    deal_enc = Deal(cores, ranks, per_core, lambda target: sum_ref.at[target], encall_ref, *deal_sems[3:])
+    deal_enc.start()
+
+    for copy in column:
+        copy.wait()
+    total = vec_ref[mine]
+    for place in places:
+        total = total + vcol_ref[place]
+    vsum_ref[...] = total
+    column_ref[mine] = self_ref[mine]
+    for group in range(depth):
+        first, second = column_ref[2 * group], column_ref[2 * group + 1]
+        pieces = []
+        for n in range(3):
+            whole = slice(2 * n * head, (2 * n + 1) * head)
+            shared = slice((2 * n + 1) * head, (2 * n + 2) * head)
+            both = (first[:, shared].astype(jnp.float32) + second[:, shared].astype(jnp.float32)).astype(low)
+            pieces += [first[:, whole], both, second[:, whole]]
+        group_ref[group] = jnp.concatenate(pieces, axis=1)
+    plane = []
+    for step, peer in enumerate(peers):
+        plane.append(remote_copy(vsum_ref, vplane_ref.at[rank], vsend.at[step], vrecv.at[step], peer))
+        plane.append(
+            remote_copy(group_ref.at[peer[2]], plane_ref.at[rank], send_sem.at[step], recv_sem.at[step], peer)
+        )
+    for copy in plane:
+        copy.start()
+
+    for copy in along:
+        copy.wait()
+    for src, dst, out in ((red2_ref, r2_ref, w2_ref), (red4_ref, r4_ref, w4_ref)):
+        total = src[seq].astype(jnp.float32)
+        for step in range(1, depth):
+            total = total + dst[lax.rem(seq + step, depth)].astype(jnp.float32)
+        out[...] = total
+
+    for copy in plane:
+        copy.wait()
+    vplane_ref[rank] = vsum_ref[...]
+    total = vplane_ref[0]
+    for origin in range(1, ranks):
+        total = total + vplane_ref[origin]
+    vout_ref[mine] = total
+    vectors = []
+    for step, place in enumerate(places):
+        vectors.append(
+            remote_copy(
+                vout_ref.at[mine], vout_ref.at[mine], vback_send.at[step], vback_recv.at[step],
+                column_peer(place, cores, rank),
+            )
+        )
+    for copy in vectors:
+        copy.start()
+    total = group_ref[rank].astype(jnp.float32)
+    for step in range(1, ranks):
+        total = total + plane_ref[lax.rem(rank + step, ranks)].astype(jnp.float32)
+    wself_ref[...] = total
+    deal_enc.finish()
+    fold = encall_ref.shape[2]
+    for item in range(per_core):
+        for half in range(cores):
+            for side in range(2):
+                rows = slice((2 * half + side) * fold, (2 * half + side + 1) * fold)
+                enc_ref[item, rows, :] = encall_ref[item, half, :, side * part : (side + 1) * part]
+    for copy in vectors:
+        copy.wait()
+    deal.finish()
+
+
+def last_rows(per_core, dqkv, dh1, early, enc_parts, self_parts, vectors, second, fourth):
+    cores, depth, ranks = lax.axis_size(ITEM), lax.axis_size(SEQ), lax.axis_size(TENSOR)
+    places, head, _ = dqkv.shape
+    rows, width = dh1.shape
+    low, full = jnp.bfloat16, jnp.float32
+    dma = pltpu.SemaphoreType.DMA
+    _, high, lanes = self_parts.shape
+    wide = lanes // 2 * 3
+    _, _, fold, side = enc_parts.shape
+    columns = second.shape[1]
+    second = second.reshape(depth, -1, columns)
+    fourth = fourth.reshape(depth, -1, columns)
+    along = second.shape[1]
+    return call_kernel(
+        functools.partial(last_kernel, cores, depth, ranks, per_core),
+        "last_rows",
+        [
+            ((per_core, cores, rows, width), low),
+            ((per_core, 2 * cores * fold, side // 2), low),
+            ((high, wide), full),
+            (vectors.shape, full),
+            ((along, columns), full),
+            ((along, columns), full),
+        ],
+        [dqkv, dh1, early, enc_parts, self_parts, vectors, second, fourth],
+        scratch=[
+            pltpu.VMEM((rows, width), low),
+            pltpu.VMEM(enc_parts.shape[1:], low),
+            pltpu.VMEM(enc_parts.shape[1:], low),
+            pltpu.VMEM((per_core, cores, fold, side), low),
+            pltpu.VMEM(self_parts.shape, low),
+            pltpu.VMEM((depth, high, wide), low),
+            pltpu.VMEM((ranks, high, wide), low),
+            pltpu.VMEM(vectors.shape, full),
+            pltpu.VMEM(vectors.shape[1:], full),
+            pltpu.VMEM((ranks,) + vectors.shape[1:], full),
+            pltpu.VMEM(second.shape, low),
+            pltpu.VMEM(fourth.shape, low),
+            dma((2,)),
+        ]
+        + send_scratch(places)
+        + send_scratch(places)
+        + [dma((ranks - 1,)) for _ in range(4)]
+        + send_scratch(places)
+        + [dma((2, depth - 1)), dma((2, depth - 1))]
+        + deal_scratch(cores, ranks, per_core)
+        + deal_scratch(cores, ranks, per_core),
+        collective_id=7,
+        us=30,
+    )
+
+
+def self_grads(blocks, cores, places, x_ref, g_ref, out_ref):
+    core, seq, rank = here()
+    low = jnp.bfloat16
+    head = g_ref.shape[1]
+    width = x_ref.shape[2]
+    rows = width // places
+    total = jnp.zeros((width, 6 * head), jnp.float32)
+    sums = jnp.zeros((16, 6 * head), jnp.float32)
+    ones = jnp.ones((16, FULL), low)
+    zero = jnp.zeros((head, HALF), low)
+    for block in range(blocks):
+        g = g_ref[block]
+        shared = jnp.where(
+            core == 0,
+            jnp.concatenate([g[:, FULL:WIDE], zero], axis=1),
+            jnp.concatenate([zero, g[:, FULL:WIDE]], axis=1),
+        )
+        flat = jnp.concatenate(
+            [g[:, :FULL], shared]
+            + [g[:, WIDE + n * FULL : WIDE + (n + 1) * FULL] for n in (0, 2, 1, 3)],
+            axis=0,
+        )
+        total = total + dot_nt(x_ref[block].T, flat)
+        sums = sums + dot_nt(ones, flat)
+    for place in range(places):
+        start = ((place % cores) * (places // cores) + place // cores) * rows
+        out_ref[place, :rows, :] = total[start : start + rows].astype(low)
+        out_ref[place, rows:, :] = sums.astype(low)
+
+
+def widen(block):
+    lane = lax.broadcasted_iota(jnp.int32, block.shape, 1)
+    zero = jnp.zeros_like(block)
+    return jnp.concatenate([jnp.where(lane < FULL, block, zero), jnp.where(lane < FULL, zero, block)], axis=0)
+
+
+def narrow(block):
+    head = block.shape[0] // 2
+    return jnp.concatenate([block[:head, :FULL], block[head:, FULL:]], axis=1)
+
+
+def causal_block(core):
+    key = lax.broadcasted_iota(jnp.int32, (FULL, WIDE), 0)
+    lane = lax.broadcasted_iota(jnp.int32, (FULL, WIDE), 1)
+    token = jnp.where(lane < FULL, lane, lane - FULL + HALF * core)
+    return key <= token
+
+
+def attend_block(block, causal, core, slots, q, k_ref, vt_ref, s_ref):
+    low = jnp.bfloat16
+    head = q.shape[0]
+    wide = widen(q)
+    last = block if causal else slots // FULL
+
+    def rows_of(key_block):
+        return pl.ds(pl.multiple_of(key_block * FULL, FULL), FULL)
+
+    def top_of(s):
+        return jnp.max(s.reshape(FULL // 8, 8, WIDE), axis=0)
+
+    def look(key_block, top):
+        rows = rows_of(key_block)
+        s = dot_nn(k_ref[rows, :], wide)
+        s_ref[rows, :] = s
+        return jnp.maximum(top, top_of(s))
+
+    top = lax.fori_loop(0, last, look, jnp.full((8, WIDE), NEG, jnp.float32))
+    if causal:
+        rows = rows_of(block)
+        s = jnp.where(causal_block(core), dot_nn(k_ref[rows, :], wide), NEG)
+        s_ref[rows, :] = s
+        top = jnp.maximum(top, top_of(s))
+        last = block + 1
+    top = jnp.max(top, axis=0, keepdims=True)
+
+    def gather(key_block, state):
+        total, out = state
+        rows = rows_of(key_block)
+        p = jnp.exp(s_ref[rows, :] - top)
+        total = total + jnp.sum(p.reshape(FULL // 8, 8, WIDE), axis=0)
+        out = out + dot_nn(vt_ref[:, rows], p.astype(low))
+        return total, out
+
+    total, out = lax.fori_loop(
+        0, last, gather, (jnp.zeros((8, WIDE), jnp.float32), jnp.zeros((2 * head, WIDE), jnp.float32))
+    )
+    total = jnp.sum(total, axis=0, keepdims=True)
+    return (narrow(out) / total).astype(low), top + jnp.log(total)
+
+
+def self_kernel(
+    cores, depth, ranks,
+    x_ref, w_ref, b_ref, wo1_ref, wq2_ref, wo2_ref,
+    q_ref, k_ref, kt_ref, v_ref, vt_ref, o_ref, lse_ref, oall_ref, wall_ref,
+    group_ref, s_ref, load_sem, group_sem, osend, orecv, *wsems
+):
+    core, seq, rank = here()
+    low = jnp.bfloat16
+    blocks = cores * depth
+    head = q_ref.shape[1]
+    high = wo1_ref.shape[0]
+    lanes = wo1_ref.shape[1] // cores
+
+    def load(n, ref, half):
+        return pltpu.make_async_copy(
+            ref.at[:, pl.ds(half * lanes, lanes)],
+            wall_ref.at[half, rank, pl.ds(n * high, high), :],
+            load_sem.at[n, half],
+        )
+
+    loads = [load(n, ref, half) for n, ref in enumerate((wo1_ref, wq2_ref, wo2_ref)) for half in range(cores)]
+    groups = [pltpu.make_async_copy(w_ref.at[half, seq], group_ref.at[half, 0], group_sem.at[half]) for half in range(cores)]
+    for copy in groups + loads:
+        copy.start()
+    mine, places = column_places(cores, depth)
+    gather = PlaneGather(wall_ref, *wsems)
+    peers = [column_peer(place, cores, rank) for place in places] + gather.peers
+    greet(peers)
+
+    for copy in groups + loads:
+        copy.wait()
+    pl.semaphore_wait(pltpu.get_barrier_semaphore(), len(peers))
+    gather.start()
+
+    w = jnp.concatenate(
+        [head_rows(group_ref, 0, n, which, head) for n in range(3) for which in (2 * core, 1)], axis=0
+    )
+    bias = b_ref[...]
+
+    def project(block, carry):
+        lanes = pl.ds(pl.multiple_of(block * FULL, FULL), FULL)
+        flat = dot_nt(w, x_ref[block])
+        q = ((flat[: 2 * head] + bias[: 2 * head]) * SCALE).astype(low)
+        shared = jnp.where(core == 0, q[head:, :HALF], q[head:, HALF:])
+        q_ref[block] = jnp.concatenate([q[:head], shared], axis=1)
+        k = flat[2 * head : 4 * head].astype(low)
+        v = (flat[4 * head :] + bias[2 * head :]).astype(low)
+        kt_ref[:, lanes] = k
+        vt_ref[:, lanes] = v
+        k_ref[lanes, :] = k.T
+        v_ref[lanes, :] = v.T
+        return carry
+
+    lax.fori_loop(0, blocks, project, 0)
+
+    back = ColumnSend(cores, depth, o_ref, oall_ref, osend, orecv)
+
+    def attend(block):
+        out, lse = attend_block(block, True, core, blocks * FULL, q_ref[block], k_ref, vt_ref, s_ref)
+        o_ref[block] = out
+        lse_ref[block] = lse
+        return out
+
+    def step(n, carry):
+        attend(lax.rem(mine + 1 + n, blocks))
+        back.copy(n).start()
+        return carry
+
+    lax.fori_loop(0, blocks - 1, step, 0)
+    gather.forward()
+    oall_ref[mine] = attend(mine)
+    back.finish()
+    gather.finish()
+
+
+def attend_self(x_all, w_all, bias, head, wo1, wq2, wo2):
+    cores, depth, ranks = lax.axis_size(ITEM), lax.axis_size(SEQ), lax.axis_size(TENSOR)
+    places = cores * depth
+    rows = places * FULL
+    low = jnp.bfloat16
+    dma = pltpu.SemaphoreType.DMA
+    _, _, high, lanes = w_all.shape
+    return call_kernel(
+        functools.partial(self_kernel, cores, depth, ranks),
+        "attend_self",
+        [
+            ((places, head, WIDE), low),
+            ((rows, 2 * head), low),
+            ((2 * head, rows), low),
+            ((rows, 2 * head), low),
+            ((2 * head, rows), low),
+            ((places, head, WIDE), low),
+            ((places, 1, WIDE), jnp.float32),
+            ((places, head, WIDE), low),
+            ((cores, ranks, 3 * wo1.shape[0], lanes), low),
+        ],
+        [x_all, w_all, bias, wo1, wq2, wo2],
+        scratch=[
+            pltpu.VMEM((cores, 1, high, lanes), low),
+            pltpu.VMEM((rows, WIDE), jnp.float32),
+            dma((3, cores)),
+            dma((cores,)),
+        ]
+        + send_scratch(places)
+        + gather_scratch(),
+        collective_id=2,
+        in_spaces=[pltpu.VMEM, pl.ANY, pltpu.VMEM, pl.ANY, pl.ANY, pl.ANY],
+        us=30,
+    )
+
+
+def cross_kernel(
+    cores, depth, part,
+    o_ref, x_ref, w_ref, bo_ref, gain_ref, shift_ref, bq_ref, kv_ref,
+    h_ref, y_ref, q_ref, k_ref, kt_ref, v_ref, parts_ref, lse_ref, oall_ref,
+    qsrc_ref, half_ref, other_ref, vt_ref, s_ref, swap_sem, qsend, qrecv, osend, orecv,
+):
+    core, seq, rank = here()
+    low = jnp.bfloat16
+    count = cores * depth
+    mine, places = column_places(cores, depth)
+    peers = [column_peer(place, cores, rank) for place in places]
+    greet(peers)
+    slots, head = k_ref.shape[0], q_ref.shape[1]
+    half_ref[...] = kv_ref[:, slots:]
+
+    o1 = assembled(o_ref, depth).T
+    h1 = x_ref[...].astype(jnp.float32) + dot_nn(o1, late_square(w_ref, 0, part)) + bo_ref[...]
+    z, _ = centred_rows(h1)
+    y1 = (z * gain_ref[...] + shift_ref[...]).astype(low)
+    h_ref[...] = h1
+    y_ref[...] = y1
+    q2t = ((dot_nt(late_square(w_ref, 1, part), y1) + bq_ref[...]) * SCALE).astype(low)
+    dispersed(q2t, qsrc_ref, depth)
+
+    pl.semaphore_wait(pltpu.get_barrier_semaphore(), len(peers))
+    ask = ColumnSend(cores, depth, qsrc_ref, q_ref, qsend, qrecv)
+    swap = remote_copy(half_ref, other_ref, swap_sem.at[0], swap_sem.at[1], (1 - core, seq, rank))
+    swap.start()
+    for step in range(count - 1):
+        ask.copy(step).start()
+    q_ref[mine] = qsrc_ref[mine]
+    swap.wait()
+    whole = kv_ref[:, :slots]
+    half, other = half_ref[...], other_ref[...]
+    shared = jnp.concatenate([jnp.where(core == 0, half, other), jnp.where(core == 0, other, half)], axis=1)
+    kt = jnp.concatenate([whole[:head], shared[:head]], axis=0)
+    vt = jnp.concatenate([whole[head:], shared[head:]], axis=0)
+    kt_ref[...] = kt
+    vt_ref[...] = vt
+    k_ref[...] = kt.T
+    v_ref[...] = vt.T
+
+    back = ColumnSend(cores, depth, parts_ref, oall_ref, osend, orecv)
+
+    def attend(block):
+        out, lse = attend_block(block, False, core, slots, q_ref[block], k_ref, vt_ref, s_ref)
+        parts_ref[block] = out
+        lse_ref[block] = lse
+        return out
+
+    oall_ref[mine] = attend(mine)
+
+    def step(n, carry):
+        ask.wait_from(n)
+        attend(lax.rem(mine + count - 1 - n, count))
+        back.copy(count - 2 - n).start()
+        return carry
+
+    lax.fori_loop(0, count - 1, step, 0)
+    ask.finish_sends()
+    back.finish()
+
+
+def attend_cross(o1, x_mine, squares, bo, gain, shift, bq, kv_mine, slots):
+    cores, depth = lax.axis_size(ITEM), lax.axis_size(SEQ)
+    places, head, _ = o1.shape
+    rows, width = x_mine.shape
+    low, full = jnp.bfloat16, jnp.float32
+    parts = (places, head, WIDE)
+    return call_kernel(
+        functools.partial(cross_kernel, cores, depth, 3 * head),
+        "attend_cross",
+        [
+            ((rows, width), full),
+            ((rows, width), low),
+            (parts, low),
+            ((slots, 2 * head), low),
+            ((2 * head, slots), low),
+            ((slots, 2 * head), low),
+            (parts, low),
+            ((places, 1, WIDE), full),
+            (parts, low),
+        ],
+        [o1, x_mine, squares, bo, gain, shift, bq, kv_mine],
+        scratch=[
+            pltpu.VMEM(parts, low),
+            pltpu.VMEM((2 * head, slots // 2), low),
+            pltpu.VMEM((2 * head, slots // 2), low),
+            pltpu.VMEM((2 * head, slots), low),
+            pltpu.VMEM((slots, WIDE), full),
+            pltpu.SemaphoreType.DMA((2,)),
+        ]
+        + send_scratch(places)
+        + send_scratch(places),
+        collective_id=3,
+        us=28,
+    )
+
+
+def back_block(block, causal, core, slots, q, do, o, lse, k_ref, kt_ref, v_ref, whole_ref, shared_ref):
+    low = jnp.bfloat16
+    head = q.shape[0]
+    wide_q, wide_do = widen(q), widen(do)
+    delta = jnp.sum(do.astype(jnp.float32) * o.astype(jnp.float32), axis=0, keepdims=True)
+    qd = jnp.concatenate([q, jnp.zeros_like(q)], axis=0).T
+    dd = jnp.concatenate([jnp.zeros_like(do), do], axis=0).T
+    mix_whole = jnp.concatenate([qd[:FULL], dd[:FULL]], axis=0)
+    mix_shared = jnp.concatenate([qd[FULL:], dd[FULL:]], axis=0)
+
+    def one(key_block, dq, masked):
+        rows = pl.ds(pl.multiple_of(key_block * FULL, FULL), FULL)
+        s = dot_nn(k_ref[rows, :], wide_q)
+        if masked:
+            s = jnp.where(causal_block(core), s, NEG)
+        p = jnp.exp(s - lse)
+        dp = dot_nn(v_ref[rows, :], wide_do)
+        ds = (p * (dp - delta)).astype(low)
+        p = p.astype(low)
+        dq = dq + dot_nn(kt_ref[:, rows], ds)
+        whole_ref[rows, :] += dot_nn(jnp.concatenate([ds[:, :FULL], p[:, :FULL]], axis=1), mix_whole)
+        shared_ref[rows, :] += dot_nn(jnp.concatenate([ds[:, FULL:], p[:, FULL:]], axis=1), mix_shared)
+        return dq
+
+    last = block if causal else slots // FULL
+    dq = lax.fori_loop(0, last, lambda kb, dq: one(kb, dq, False), jnp.zeros((2 * head, WIDE), jnp.float32))
+    if causal:
+        dq = one(block, dq, True)
+    return narrow(dq).astype(low)
+
+
+def cross_back_kernel(
+    cores, depth,
+    q_ref, k_ref, kt_ref, v_ref, o_ref, lse_ref, do_ref,
+    dqall_ref, dkv_ref,
+    dq_ref, whole_ref, shared_ref, give_ref, got_ref, swap_sem, send_sem, recv_sem,
+):
+    core, seq, rank = here()
+    low = jnp.bfloat16
+    count = cores * depth
+    mine, places = column_places(cores, depth)
+    peers = [column_peer(place, cores, rank) for place in places]
+    greet(peers)
+    slots = k_ref.shape[0]
+    whole_ref[...] = jnp.zeros_like(whole_ref)
+    shared_ref[...] = jnp.zeros_like(shared_ref)
+    back = ColumnSend(cores, depth, dq_ref, dqall_ref, send_sem, recv_sem)
+
+    def go(block):
+        return back_block(
+            block, False, core, slots, q_ref[block], do_ref[block], o_ref[block], lse_ref[block],
+            k_ref, kt_ref, v_ref, whole_ref, shared_ref,
+        )
+
+    dq_ref[places[0]] = go(places[0])
+    pl.semaphore_wait(pltpu.get_barrier_semaphore(), len(peers))
+    back.copy(0).start()
+
+    def step(n, carry):
+        block = lax.rem(mine + 1 + n, count)
+        dq_ref[block] = go(block)
+        back.copy(n).start()
+        return carry
+
+    lax.fori_loop(1, count - 1, step, 0)
+    dqall_ref[mine] = go(mine)
+    half = slots // 2
+    give_ref[...] = shared_ref[pl.ds(pl.multiple_of((1 - core) * half, half), half), :].astype(low)
+    swap = remote_copy(give_ref, got_ref, swap_sem.at[0], swap_sem.at[1], (1 - core, seq, rank))
+    swap.start()
+    dkv_ref[:slots] = whole_ref[...].astype(low)
+    swap.wait()
+    kept = shared_ref[pl.ds(pl.multiple_of(core * half, half), half), :]
+    dkv_ref[slots:] = (kept + got_ref[...].astype(jnp.float32)).astype(low)
+    back.finish()
+
+
+def attend_cross_back(q, k, kt, v, o, lse, do):
+    cores, depth = lax.axis_size(ITEM), lax.axis_size(SEQ)
+    places, head, _ = q.shape
+    slots = k.shape[0]
+    low = jnp.bfloat16
+    sums = pltpu.VMEM((slots, 2 * head), jnp.float32)
+    return call_kernel(
+        functools.partial(cross_back_kernel, cores, depth),
+        "back_cross",
+        [(q.shape, low), ((slots + slots // 2, 2 * head), low)],
+        [q, k, kt, v, o, lse, do],
+        scratch=[
+            pltpu.VMEM(q.shape, low),
+            sums,
+            sums,
+            pltpu.VMEM((slots // 2, 2 * head), low),
+            pltpu.VMEM((slots // 2, 2 * head), low),
+            pltpu.SemaphoreType.DMA((2,)),
+        ]
+        + send_scratch(places),
+        collective_id=5,
+        us=24,
+    )
+
+
+def self_back_kernel(
+    cores, depth, ranks, part,
+    dq2_ref, dh2_ref, h1_ref, y1_ref, oin_ref, w_ref, gain_ref,
+    q_ref, k_ref, kt_ref, v_ref, o_ref, lse_ref, dkv_ref, enc_ref, early_ref, idx_ref, x_ref,
+    dh1_ref, vec_ref, gall_ref, self_ref, encp_ref, second_ref, fourth_ref,
+    dosrc_ref, do_ref, g_ref, whole_ref, shared_ref, dkvall_ref, grad2_ref, grad4_ref,
+    dosend, dorecv, gsend, grecv, kvsend, kvrecv, *reduce_refs
+):
+    core, seq, rank = here()
+    low = jnp.bfloat16
+    count = cores * depth
+    head = part // 3
+    mine, places = column_places(cores, depth)
+    first = PlaneReduce(ranks, grad2_ref, *reduce_refs[:6])
+    second = PlaneReduce(ranks, grad4_ref, *reduce_refs[6:])
+    peers = [column_peer(place, cores, rank) for place in places] + first.peers
+    greet(peers)
+    chain = Chain(depth, dkvall_ref, kvsend, kvrecv)
+
+    width = y1_ref.shape[1]
+    lanes = width // cores
+    dq2t = assembled(dq2_ref, depth)
+    dy1 = dh2_ref[...] + dot_nn(dq2t.T, late_square(w_ref, 1, part)) * SCALE
+    z1, spread1 = centred_rows(h1_ref[...])
+    dh1, gg1, gs1 = norm_back(z1, spread1, dy1, gain_ref[...])
+    e1 = dh1.astype(low)
+    dispersed(dot_nt(late_square(w_ref, 0, part), e1).astype(low), dosrc_ref, depth)
+    pl.semaphore_wait(pltpu.get_barrier_semaphore(), len(peers))
+    ask = ColumnSend(cores, depth, dosrc_ref, do_ref, dosend, dorecv)
+    for step in range(count - 1):
+        ask.copy(step).start()
+    do_ref[mine] = dosrc_ref[mine]
+    dkvall_ref[seq] = dkv_ref[...]
+    dh1_ref[...] = dh1
+    vec_ref[0:1] = gg1
+    vec_ref[1:2] = gs1
+    vec_ref[2:3] = jnp.sum(e1.astype(jnp.float32), axis=0, keepdims=True)
+    ones = jnp.ones((8, FULL), low)
+    vec_ref[3:4] = dot_nt(ones, dq2t)[0:1] * SCALE
+    o1t = assembled(oin_ref, depth)
+    both = jnp.concatenate([y1_ref[...].T, e1.T], axis=1)
+    blank = jnp.zeros((part, FULL), low)
+    for to in range(ranks):
+        rows = slice(to * part, (to + 1) * part)
+        right = jnp.concatenate(
+            [
+                jnp.concatenate([dq2t[rows], blank], axis=1),
+                jnp.concatenate([blank, o1t[rows]], axis=1),
+            ],
+            axis=0,
+        )
+        for half in range(cores):
+            grad2_ref[half, to] = dot_nt(both[half * lanes : (half + 1) * lanes], right).astype(low)
+    first.start()
+
+    whole_ref[...] = jnp.zeros_like(whole_ref)
+    shared_ref[...] = jnp.zeros_like(shared_ref)
+    for step in range(count - 1):
+        ask.wait_from(step)
+    chain.step(0)
+
+    back = ColumnSend(cores, depth, g_ref, gall_ref, gsend, grecv)
+
+    def go(block):
+        g_ref[block, :, :WIDE] = back_block(
+            block, True, core, count * FULL, q_ref[block], do_ref[block], o_ref[block], lse_ref[block],
+            k_ref, kt_ref, v_ref, whole_ref, shared_ref,
+        )
+        rows = pl.ds(pl.multiple_of(block * FULL, FULL), FULL)
+        whole = whole_ref[rows, :].T.astype(low)
+        shared = shared_ref[rows, :].T.astype(low)
+        g_ref[block, :, WIDE:] = jnp.concatenate([whole[:head], whole[head:], shared[:head], shared[head:]], axis=1)
+
+        @pl.when(block != mine)
+        def _():
+            back.copy(lax.rem(block + 2 * count - mine - 1, count)).start()
+
+        @pl.when(block == mine)
+        def _():
+            gall_ref[mine] = g_ref[mine]
+
+    def step(n, carry):
+        go(count - 1 - n)
+        return carry
+
+    lax.fori_loop(0, 2, step, 0)
+    first.middle()
+    chain.step(1)
+    lax.fori_loop(2, 4, step, 0)
+    for n in range(2, depth):
+        chain.step(n)
+    lax.fori_loop(4, count, step, 0)
+
+    encoder_back(ranks, head, enc_ref, early_ref, idx_ref, dkvall_ref, encp_ref, grad4_ref)
+    second.start()
+    self_grads(count, cores, count, x_ref, g_ref, self_ref)
+    second.middle()
+    second_ref[...] = first.finish().astype(low)
+    chain.finish()
+    ask.finish_sends()
+    back.finish()
+    fourth_ref[...] = second.finish().astype(low)
+
+
+def attend_self_back(*args):
+    cores, depth, ranks = lax.axis_size(ITEM), lax.axis_size(SEQ), lax.axis_size(TENSOR)
+    dq2, dh2, h1, y1, o1, squares, gain, q, k, kt, v, o, lse, dkv, enc, early, index, x_all = args
+    places, head, _ = q.shape
+    rows, width = y1.shape
+    low, full = jnp.bfloat16, jnp.float32
+    part, lanes = 3 * head, width // cores
+    all_rows = places * rows
+    dma = pltpu.SemaphoreType.DMA
+    grads = (cores, ranks, lanes, 2 * part)
+    message = (places, head, WIDE + 4 * FULL)
+    sums = pltpu.VMEM((all_rows, 2 * head), full)
+    return call_kernel(
+        functools.partial(self_back_kernel, cores, depth, ranks, part),
+        "back_self",
+        [
+            ((rows, width), full),
+            ((4, width), full),
+            (message, low),
+            ((places, width // places + 16, 6 * head), low),
+            ((cores, ranks, enc.shape[0] // (2 * cores), 2 * part), low),
+            ((lanes, 2 * part), low),
+            ((lanes, 2 * part), low),
+        ],
+        list(args),
+        scratch=[
+            pltpu.VMEM(q.shape, low),
+            pltpu.VMEM(q.shape, low),
+            pltpu.VMEM(message, low),
+            sums,
+            sums,
+            pltpu.VMEM((depth,) + dkv.shape, low),
+            pltpu.VMEM(grads, low),
+            pltpu.VMEM(grads, low),
+        ]
+        + send_scratch(places)
+        + send_scratch(places)
+        + [dma((2, depth)), dma((depth,))]
+        + reduce_scratch(ranks, lanes, 2 * part, low)
+        + reduce_scratch(ranks, lanes, 2 * part, low),
+        collective_id=6,
+        us=60,
+    )
+
+
+def column_body(
+    dec_input,
+    encoder_states,
+    retrieved,
+    self_wq,
+    self_bq,
+    self_wk,
+    self_wv,
+    self_bv,
+    self_wo,
+    self_bo,
+    norm1_gain,
+    norm1_bias,
+    cross_wq,
+    cross_bq,
+    cross_wk,
+    cross_wv,
+    cross_bv,
+    cross_wo,
+    cross_bo,
+    norm2_gain,
+    norm2_bias,
+    ffn_w1,
+    ffn_b1,
+    ffn_w2,
+    ffn_b2,
+    norm3_gain,
+    norm3_bias,
+    out_grad,
+):
+    low, full = jnp.bfloat16, jnp.float32
+    core, seq, rank = here()
+    cores, depth, ranks = lax.axis_size(ITEM), lax.axis_size(SEQ), lax.axis_size(TENSOR)
+    per_core, _, width = dec_input.shape
+    slots = retrieved.shape[2]
+    part = self_wq.shape[1]
+    head = part // 3
+    places = cores * depth
+    lanes = width // cores
+    hidden = ffn_w1.shape[1]
+
+    def row(vector):
+        return vector.reshape(1, width)
+
+    vectors = jnp.concatenate([self_bq, self_bv, cross_bq, cross_bv, ffn_b1]).reshape(-1, 128)
+    x_all, grad_mine, enc, index, vectors, early = prologue(
+        dec_input, out_grad, encoder_states, retrieved, vectors, [self_wq.T, self_wk.T, self_wv.T, cross_wk.T, cross_wv.T]
+    )
+    ffn = jnp.concatenate(
+        [lax.dynamic_slice_in_dim(w, core * lanes, lanes, axis=1) for w in (ffn_w1, ffn_w2)], axis=0
+    )
+    ffn = lax.optimization_barrier((ffn, index))[0]
+    ffn = lax.all_gather(ffn, TENSOR, axis=0, tiled=False)
+    x_mine = x_all[seq, core]
+    x_all = x_all.reshape(places, FULL, width)
+    vectors = vectors.reshape(ranks, -1)
+    all_bq1, all_bv1, all_bq2, all_bv2 = [vectors[:, n * part : (n + 1) * part] for n in range(4)]
+    all_b1 = vectors[:, 4 * part :].reshape(ranks, 1, hidden)
+
+    by_head = all_bv2.reshape(ranks, 3, 1, head)
+    blank = jnp.zeros((ranks, 2, head), full)
+    two = jnp.concatenate([lax.dynamic_slice_in_dim(by_head, 2 * core, 1, axis=1), by_head[:, 1:2]], axis=1)
+    bias_kv = jnp.concatenate([blank[:, :, None], two], axis=2).reshape(ranks, 4 * head, 1)
+    pieces = retrieve(enc, early, bias_kv, index)
+    kv_mine = lax.psum_scatter(pieces, SEQ, scatter_dimension=0, tiled=False)
+
+    def two_heads(rows):
+        rows = lax.dynamic_index_in_dim(rows, seq, 0, keepdims=False).reshape(3, head)
+        return jnp.concatenate([lax.dynamic_slice_in_dim(rows, 2 * core, 1, axis=0), rows[1:2]], axis=0)
+
+    bias = jnp.concatenate([two_heads(all_bq1), two_heads(all_bv1)], axis=0).reshape(4 * head, 1)
+    q1, k1, k1t, v1, v1t, o1_parts, lse1, o1, squares = attend_self(
+        x_all, early, bias, head, self_wo, cross_wq.T, cross_wo
+    )
+
+    h1, y1, q2, k2, k2t, v2, o2_parts, lse2, o2 = attend_cross(
+        o1, x_mine, squares, row(self_bo), row(norm1_gain), row(norm1_bias), all_bq2.reshape(width, 1), kv_mine, slots
+    )
+    ffn = lax.optimization_barrier((ffn, o1))[0]
+    ffn = lax.all_gather(ffn, ITEM, axis=0, tiled=False)
+    layer_out, do2, dh2, vec_mid, grad_mid = middle(
+        per_core,
+        o2,
+        y1,
+        grad_mine,
+        squares,
+        ffn,
+        [
+            row(cross_bo),
+            row(norm2_gain),
+            row(norm2_bias),
+            all_b1,
+            row(ffn_b2),
+            row(norm3_gain),
+            row(norm3_bias),
+        ],
+    )
+    layer_out = layer_out.reshape(per_core, cores * FULL, width)
+    first_sum = lax.psum_scatter(grad_mid, ITEM, scatter_dimension=0, tiled=False)
+    dq2, dkv2 = attend_cross_back(q2, k2, k2t, v2, o2_parts, lse2, do2)
+    dq2, first_sum = lax.optimization_barrier((dq2, first_sum))
+    first_sum = lax.psum_scatter(first_sum, TENSOR, scatter_dimension=0, tiled=False)
+    dh1, vec_second, dqkv, self_parts, enc_parts, second_sum, fourth_sum = attend_self_back(
+        dq2, dh2, h1, y1, o1, squares, row(norm1_gain),
+        q1, k1, k1t, v1, o1_parts, lse1, dkv2, enc, early, index, x_all,
+    )
+    first_sum = lax.psum_scatter(first_sum, SEQ, scatter_dimension=0, tiled=True)
+
+    dv_heads = [jnp.sum(rows[:, head:].astype(full), axis=0) for rows in (dkv2[:slots], dkv2[slots:])]
+    slot_of = jnp.arange(3 * depth)[:, None]
+    bv_rows = jnp.where(slot_of == 3 * seq + 2 * core, dv_heads[0], 0.0) + jnp.where(
+        slot_of == 3 * seq + 1, dv_heads[1], 0.0
+    )
+    vectors = jnp.concatenate([vec_mid, vec_second, bv_rows.reshape(1, width)], axis=0)
+    count = vectors.shape[0]
+    piece = 16 * 128
+    vectors = jnp.pad(vectors.reshape(-1), (0, places * piece - count * width)).reshape(places, 16, 128)
+    input_grad, encoder_grad, third_sum, summed, second_sum, fourth_sum = last_rows(
+        per_core, dqkv, dh1, early, enc_parts, self_parts, vectors, second_sum, fourth_sum
+    )
+    input_grad = input_grad.reshape(per_core, cores * FULL, width)
+    summed = summed.reshape(-1)[: count * width].reshape(count, width)
+
+    rows = width // places
+    first_sum = first_sum.astype(full)
+    gself_wq = third_sum[:rows, :part] * SCALE
+    gself_wk = third_sum[:rows, part : 2 * part]
+    gself_wv = third_sum[:rows, 2 * part :]
+    gself_bq = third_sum[rows, :part] * SCALE
+    gself_bv = third_sum[rows, 2 * part :]
+    gffn_w1 = first_sum[:, :hidden]
+    gffn_w2 = first_sum[:, hidden : 2 * hidden].T
+    gcross_wo = first_sum[:, 2 * hidden : 2 * hidden + part].T
+    gcross_wq = second_sum[:, :part] * SCALE
+    gself_wo = second_sum[:, part:].T
+    grad_kv = fourth_sum.reshape(rows, 3, 2, head)
+    gcross_wk = grad_kv[:, :, 0].reshape(rows, part)
+    gcross_wv = grad_kv[:, :, 1].reshape(rows, part)
+
+    gnorm3_gain, gnorm3_bias, gffn_b2, gnorm2_gain, gnorm2_bias, gcross_bo = [summed[n] for n in range(6)]
+    gffn_b1 = lax.dynamic_index_in_dim(summed[6 : 6 + ranks], rank, 0, keepdims=False)
+    gnorm1_gain, gnorm1_bias, gself_bo = [summed[6 + ranks + n] for n in range(3)]
+
+    def rank_part(vector):
+        return lax.dynamic_slice_in_dim(vector, rank * part, part)
+
+    gcross_bq = rank_part(summed[9 + ranks])
+    gcross_bv = rank_part(summed[10 + ranks])
+    return (
+        layer_out,
+        input_grad,
+        encoder_grad,
+        gself_wq,
+        gself_bq,
+        gself_wk,
+        gself_wv,
+        gself_bv,
+        gself_wo,
+        gself_bo,
+        gnorm1_gain,
+        gnorm1_bias,
+        gcross_wq,
+        gcross_bq,
+        gcross_wk,
+        gcross_wv,
+        gcross_bv,
+        gcross_wo,
+        gcross_bo,
+        gnorm2_gain,
+        gnorm2_bias,
+        gffn_w1,
+        gffn_b1,
+        gffn_w2,
+        gffn_b2,
+        gnorm3_gain,
+        gnorm3_bias,
+    )
+
+
 def solution(mesh):
     placed = (
-        P("item", "seq", None),
-        P("item", "seq", None),
-        P("item", "tensor", None),
-        P(None, "tensor"),
-        P("tensor"),
-        P(None, "tensor"),
-        P(None, "tensor"),
-        P("tensor"),
-        P("tensor", None),
+        P(ITEM, SEQ, None),
+        P(ITEM, SEQ, None),
+        P(ITEM, TENSOR, None),
+        P(None, TENSOR),
+        P(TENSOR),
+        P(None, TENSOR),
+        P(None, TENSOR),
+        P(TENSOR),
+        P(TENSOR, None),
         P(),
         P(),
         P(),
-        P(None, "tensor"),
-        P("tensor"),
-        P(None, "tensor"),
-        P(None, "tensor"),
-        P("tensor"),
-        P("tensor", None),
+        P(None, TENSOR),
+        P(TENSOR),
+        P(None, TENSOR),
+        P(None, TENSOR),
+        P(TENSOR),
+        P(TENSOR, None),
         P(),
         P(),
         P(),
-        P(None, "tensor"),
-        P("tensor"),
-        P("tensor", None),
+        P(None, TENSOR),
+        P(TENSOR),
+        P(TENSOR, None),
         P(),
         P(),
         P(),
-        P("item", "seq", None),
-    )
-    return jax.shard_map(
-        body,
-        mesh=mesh,
-        in_specs=placed,
-        out_specs=(
-            P("item", "seq", None),
-            P("item", "seq", None),
-            P("item", "seq", "tensor"),
-            P(("item", "seq"), "tensor"),
-            P("tensor"),
-            P(("item", "seq"), "tensor"),
-            P(("item", "seq"), "tensor"),
-            P("tensor"),
-            P("tensor", ("item", "seq")),
-            P(),
-            P(),
-            P(),
-            P(("item", "seq"), "tensor"),
-            P("tensor"),
-            P(("item", "seq"), "tensor"),
-            P(("item", "seq"), "tensor"),
-            P("tensor"),
-            P("tensor", ("item", "seq")),
-            P(),
-            P(),
-            P(),
-            P(("item", "seq"), "tensor"),
-            P("tensor"),
-            P("tensor", ("item", "seq")),
-            P(),
-            P(),
-            P(),
-        ),
-        check_vma=False,
-    )
+        P(ITEM, SEQ, None),
+    )
+    reduced = (
+        P(ITEM, SEQ, None),
+        P(ITEM, SEQ, None),
+        P(ITEM, SEQ, TENSOR),
+        P((ITEM, SEQ), TENSOR),
+        P(TENSOR),
+        P((ITEM, SEQ), TENSOR),
+        P((ITEM, SEQ), TENSOR),
+        P(TENSOR),
+        P(TENSOR, (ITEM, SEQ)),
+        P(),
+        P(),
+        P(),
+        P((ITEM, SEQ), TENSOR),
+        P(TENSOR),
+        P((ITEM, SEQ), TENSOR),
+        P((ITEM, SEQ), TENSOR),
+        P(TENSOR),
+        P(TENSOR, (ITEM, SEQ)),
+        P(),
+        P(),
+        P(),
+        P((ITEM, SEQ), TENSOR),
+        P(TENSOR),
+        P(TENSOR, (ITEM, SEQ)),
+        P(),
+        P(),
+        P(),
+    )
+
+    def layer(*arrays):
+        chosen = column_body if column_plan_fits(mesh, arrays) else general_body
+        return jax.shard_map(
+            chosen,
+            mesh=mesh,
+            in_specs=placed,
+            out_specs=reduced,
+            check_vma=False,
+        )(*arrays)
+
+    return layer

time: 1570 us -> 445 us (0.28)
  waiting for transfers between devices: 889 us -> 14.5 us
  Pallas kernels: 0 us -> 372 us
  blocking collectives: 229 us -> 0 us
  matrix products: 166 us -> 0 us
  other arithmetic: 160 us -> 5.41 us
  local copies, waits for them, and re-layouts: 95 us -> 29.7 us
    psum x7 -> x0, waiting for transfers between devices: 501 us -> none  [the longest x6 436 us: tensor_total(): return lax.psum(partial_rows, 'tensor')]
    pallas_call x0 -> x8, Pallas kernels: none -> 372 us  [call_kernel(): pl.pallas_call(kernel, out_shape=[jax.ShapeDtypeStruct(s, d) for s, d in...]
    psum x2 -> x0, blocking collectives: 229 us -> none  [the longest x1 199 us: body(): kv_grad = lax.psum(kv_grad_part, 'seq').astype(jnp.bfloat16)]
    reduce_scatter x7 -> x3, waiting for transfers between devices: 219 us -> 0.02 us  [the longest x1 0.02 us: column_body(): lax.psum_scatter(grad_mid, ITEM, scatter_dimension=0, tiled=False)]
    dot_general x39 -> x0, matrix products: 166 us -> none  [the longest x8 19 us: matmul(): return jnp.dot(first_op, second_op, preferred_element_type=jnp.float32)]
    unnamed x25 -> x7, waiting for transfers between devices: 108 us -> 0.1 us
    reduce_sum x18 -> x2, other arithmetic: 55 us -> 0.37 us  [column_body(): jnp.sum(rows[:, head:].astype(full), axis=0)]
    all_gather x1 -> x2, waiting for transfers between devices: 61.7 us -> 14.3 us  [the longest x1 14.3 us: column_body(): ffn = lax.all_gather(ffn, TENSOR, axis=0, tiled=False)]
  transfers between devices with their start and end apart: 20 -> 6, of which waited for: 17 -> 1; matrix products, arithmetic and copies ran while one was open for 14% -> 5% of each run, Pallas kernels for 0% -> 66%
where the time goes in v1:
time: 445 us; the launch traced here: 438 us
  Pallas kernels  372 us (84%)
  local copies, waits for them, and re-layouts  29.7 us (7%)
  between operations  15.8 us (4%)
  waiting for transfers between devices  14.5 us (3%)
  other arithmetic  5.41 us (1%)
    pallas_call x8, Pallas kernels, call_kernel(): pl.pallas_call(kernel, out_shape=[jax.ShapeDtypeStruct(s, d) for s, d in...  372 us
    all_gather x1, waiting for transfers between devices, column_body(): ffn = lax.all_gather(ffn, TENSOR, axis=0, tiled=False)  14.3 us
    unnamed x55, local copies, waits for them, and re-layouts  11.5 us
  transfers between devices with their start and end apart: 6, of which 1 were waited for; matrix products, arithmetic and copies ran while one was open for 5% of the time, Pallas kernels for 66%

profile of v1, /device:TPU:0, one launch (start us, length us, event | category | flops | bytes accessed | tf_op | source)
XLA Modules:
  0.0 438.1 jit_solution(268838238102822280)
XLA Ops:
  8.1 1.4 copy.82.idx_ref
  9.5 1.4 constant_dynamic-slice_fusion
  10.9 1.1 pad_maximum_fusion
  12.0 0.7 concatenate.18
  12.7 52.9 %prologue.1 = (bf16[4,2,256,768]{3,2,1,0:T(8,128)(2,1)}, bf16[256,768]{1,0:T(8,128)(2,1)}, bf16[1152,768]{1,0:T(8,128)(2,1)}, s32[4,3,1024]{2,1,0:T(4,128)}, f32...) custom-call(bf16[2,512,768]{2,1,0:T(8,128)(2,1)} %x_ref.1, bf16[2,512,768]{2,1,0:T(8,128)(2,1)} %g_ref.1, ...), custom_call_target="tpu_custom_call" | custom-call | flops 32000000000 | bytes 96000000 | tf_op jit(solution)/shard_map/prologue/pallas_call | solution.py:419
  65.6 0.0 reduce-scatter.7.cloned.1.call-start
  65.7 0.8 copy.96
  66.4 0.1 fusion.6
  66.5 0.1 reshape.241
  66.6 1.3 reshape.263.b_ref
  67.9 9.8 %retrieve.1 = bf16[4,128,1536]{2,1,0:T(8,128)(2,1)} custom-call(bf16[1152,768]{1,0:T(8,128)(2,1)} %get-tuple-element.79.enc_ref, bf16[2,4,960,384]{3,2,1,0:T(8,128)(2,1)} %get-tuple-element.75.w_ref.early_ref, f32[4,256,1]{2,1,0:T(8,128)} %reshape.263.b_ref, s32[4,3,1024]{2,1,0:T(4,128)} %get-tuple-element.80.idx_ref), custom_call_target="tpu_custom_call" | custom-call | flops 10000000000 | bytes 30000000 | tf_op jit(solution)/shard_map/retrieve/pallas_call | solution.py:419
  77.7 0.0 all-gather.7.cloned.1.call-start
  77.8 0.1 dynamic-slice.4
  77.9 0.1 dynamic-slice.5
  77.9 0.1 reshape.234
  78.0 0.1 reshape.235
  78.1 0.8 reshape.261.b_ref
  78.9 39.5 %attend_self.1 = (bf16[8,64,384]{2,1,0:T(8,128)(2,1)}, bf16[2048,128]{1,0:T(8,128)(2,1)}, bf16[128,2048]{1,0:T(8,128)(2,1)}, bf16[2048,128]{1,0:T(8,128)(2,1)}, ...) custom-call(bf16[8,256,768]{2,1,0:T(8,128)(2,1)} %bitcast.51, ...), custom_call_target="tpu_custom_call" | custom-call | flops 30000001024 | bytes 90000000 | tf_op jit(solution)/shard_map/attend_self/pallas_call | solution.py:419
  118.4 14.3 %all-gather.5.cloned.1.call-done = bf16[6144,384]{1,0:T(8,128)(2,1)} async-done(((bf16[1536,384]{1,0:T(8,128)(2,1)}), bf16[6144,384]{1,0:T(8,128)(2,1)}) %all-gather.5.cloned.1.call-update) | async-done | bytes 4718608 | tf_op jit(solution)/shard_map/all_gather | solution.py:2014
  132.9 1.0 reshape.262.bq_ref
  133.9 0.6 reshape.238.gain_ref
  134.5 0.6 reshape.237.bo_ref
  135.1 0.6 reshape.239.shift_ref
  135.6 0.6 reshape.246.b1_ref
  136.2 0.6 reshape.243.bo_ref
  136.8 0.6 reshape.244.gain2_ref
  137.4 0.6 reshape.245.shift2_ref
  138.0 0.6 reshape.247.b2_ref
  138.6 0.6 reshape.248.gain3_ref
  139.2 0.6 reshape.249.shift3_ref
  139.7 1.8 dynamic-slice_bitcast_fusion.x_ref
  141.6 30.5 %attend_cross.1 = (f32[256,768]{1,0:T(8,128)}, bf16[256,768]{1,0:T(8,128)(2,1)}, bf16[8,64,384]{2,1,0:T(8,128)(2,1)}, bf16[1024,128]{1,0:T(8,128)(2,1)}, bf16[12...) custom-call(bf16[8,64,384]{2,1,0:T(8,128)(2,1)} %get-tuple-element.7, ...), custom_call_target="tpu_custom_call" | custom-call | flops 28000000000 | bytes 84000000 | tf_op jit(solution)/shard_map/attend_cross/pallas_call | solution.py:419
  172.1 31.3 %middle.1 = (bf16[2,2,256,768]{3,2,1,0:T(8,128)(2,1)}, bf16[8,64,384]{2,1,0:T(8,128)(2,1)}, f32[256,768]{1,0:T(8,128)}, f32[10,768]{1,0:T(8,128)}, bf16[2,4,384,1792]{3,2,1,0:T(8,128)(2,1)}) custom-call(bf16[8,64,384]{2,1,0:T(8,128)(2,1)} %get-tuple-element.81.o_ref, bf16[256,768]{1,0:T(8,128)(2,1)} %get-tuple-element.82.y1_ref, ...), custom_call_target="tpu_custom_call" | custom-call | flops 22000001024 | bytes 66000000 | tf_op jit(solution)/shard_map/middle/pallas_call | solution.py:419
  203.4 0.0 reduce-scatter.13.cloned.1.call-start
  203.4 23.2 %back_cross.1 = (bf16[8,64,384]{2,1,0:T(8,128)(2,1)}, bf16[1536,128]{1,0:T(8,128)(2,1)}) custom-call(bf16[8,64,384]{2,1,0:T(8,128)(2,1)} %get-tuple-element.87.q_ref, bf16[1024,128]{1,0:T(8,128)(2,1)} %get-tuple-element.88.k_ref, bf16[128,1024]{1,0:T(8,128)(2,1)} %get-tuple-element.89.kt_ref, bf16[1024,128]{1,0:T(8,128)(2,1)} %get-tuple-element.90.v_ref, ...), custom_call_target="tpu_custom_call" | custom-call | flops 24000000000 | bytes 72000000 | tf_op jit(solution)/shard_map/back_cross/pallas_call | solution.py:419
  226.7 0.0 reduce-scatter.11.cloned.1.call-start
  226.8 0.9 copy-done.3
  227.7 0.1 convert_reduce_fusion.1
  227.8 0.2 convert_reduce_fusion
  228.0 0.1 select_add_fusion
  228.1 0.1 add.64
  228.2 114.9 %back_self.1 = (f32[256,768]{1,0:T(8,128)}, f32[4,768]{1,0:T(4,128)}, bf16[8,64,1408]{2,1,0:T(8,128)(2,1)}, bf16[8,112,384]{2,1,0:T(8,128)(2,1)}, bf16[2,4,288,3...) custom-call(bf16[8,64,384]{2,1,0:T(8,128)(2,1)} %get-tuple-element.96.dq2_ref, ...), custom_call_target="tpu_custom_call" | custom-call | flops 60000002048 | bytes 180000000 | tf_op jit(solution)/shard_map/back_self/pallas_call | solution.py:419
  343.1 0.7 pad_maximum_fusion.1
  343.9 0.6 pad.5
  344.5 70.5 %last_rows.1 = (bf16[2,2,256,768]{3,2,1,0:T(8,128)(2,1)}, bf16[2,1152,192]{2,1,0:T(8,128)(2,1)}, f32[112,576]{1,0:T(8,128)}, f32[8,16,128]{2,1,0:T(8,128)}, f32[96,384]{1,0:T(8,128)}, /*index=5*/f32[96,384]{1,0:T(8,128)}) custom-call(bf16[8,64,1408]{2,1,0:T(8,128)(2,1)} %get-tuple-element.106.parts_ref, f32[256,768]{1,0:T(8,128)} %get-tuple-element.107.dh1_ref, ...), custom_call_target="tpu_custom_call" | custom-call | flops 30000001024 | bytes 90000000 | tf_op jit(solution)/shard_map/last_rows/pallas_call | solution.py:419
  415.1 2.4 copy.88
  417.4 0.1 copy.87
  417.6 0.7 copy.90
  418.3 0.7 copy.91
  419.0 0.7 slice_multiply_fusion
  419.7 0.7 copy.89
  420.4 0.6 fusion.5
  421.1 0.6 dynamic_slice.43
  421.7 0.6 dynamic_slice.44
  422.4 0.6 dynamic-slice_reduce_fusion
  423.0 0.6 fusion.2
  423.5 0.8 fusion.3
  424.3 1.1 convert_element_type.13
  425.4 0.7 slice_bitcast_fusion
  426.2 0.7 copy.92
  426.9 0.7 slice.189
  427.6 1.1 copy.99
  428.8 0.8 copy-done.1
  429.6 1.1 copy.100
  (71 shorter events, 0.5 us)
Async XLA Ops:
  8.0 124.7 %all-gather.5.cloned.1.call-start = ((), (), s32[]{:S(2)}) async-start(), calls=%async_computation.7 | async-start | bytes 5898240 | tf_op jit(solution)/shard_map/all_gather | solution.py:2014
  10.8 1.2 copy-start.18
  10.8 1.2 copy-start.19
  10.8 1.2 copy-start.20
  10.9 1.2 copy-start.21
  10.9 1.2 copy-start.22
  65.6 76.0 %reduce-scatter.7.cloned.1.call-start = ((), (), s32[]{:S(2)}) async-start(), calls=%async_computation.4 | async-start | bytes 1966080 | tf_op jit(solution)/shard_map/reduce_scatter | solution.py:2026
  77.7 94.4 %all-gather.7.cloned.1.call-start = ((), (), s32[]{:S(2)}) async-start(), calls=%async_computation.8 | async-start | bytes 14155776 | tf_op jit(solution)/shard_map/all_gather | solution.py:2041
  132.7 1.2 copy-start.9
  132.7 1.8 copy-start.10
  132.7 2.3 copy-start.11
  132.7 3.5 copy-start.12
  132.7 4.1 copy-start.13
  132.7 4.7 %copy-start.14 = (f32[768]{0:T(1024)S(1)}, f32[768]{0:T(1024)}, u32[]{:S(2)}) copy-start(f32[768]{0:T(1024)} %param.48) | copy-start | bytes 9220
  132.7 5.3 %copy-start.15 = (f32[768]{0:T(1024)S(1)}, f32[768]{0:T(1024)}, u32[]{:S(2)}) copy-start(f32[768]{0:T(1024)} %param.52) | copy-start | bytes 9220
  132.8 5.8 %copy-start.16 = (f32[768]{0:T(1024)S(1)}, f32[768]{0:T(1024)}, u32[]{:S(2)}) copy-start(f32[768]{0:T(1024)} %param.53) | copy-start | bytes 9220
  132.8 6.4 %copy-start.17 = (f32[768]{0:T(1024)S(1)}, f32[768]{0:T(1024)}, u32[]{:S(2)}) copy-start(f32[768]{0:T(1024)} %param.54) | copy-start | bytes 9220
  132.8 93.9 %reduce-scatter.9.cloned.1.call-start = ((), (), s32[]{:S(2)}) async-start(), calls=%async_computation.5 | async-start | bytes 16515072 | tf_op jit(solution)/shard_map/reduce_scatter | solution.py:2060
  203.4 141.1 %reduce-scatter.13.cloned.1.call-start = ((), (), s32[]{:S(2)}) async-start(), calls=%async_computation.9 | async-start | bytes 6881280
  226.7 1.0 copy-start.3
  226.7 197.6 %reduce-scatter.11.cloned.1.call-start = ((), (), s32[]{:S(2)}) async-start(), calls=%async_computation.6 | async-start | bytes 1720320 | tf_op jit(solution)/shard_map/reduce_scatter | solution.py:2068
  228.2 114.9 %copy-start.8 = (f32[10,768]{1,0:T(8,128)S(1)}, f32[10,768]{1,0:T(8,128)}, u32[]{:S(2)}) copy-start(f32[10,768]{1,0:T(8,128)} %get-tuple-element.110) | copy-start | bytes 92164
  415.0 2.4 copy-start.6
  415.0 4.0 copy-start.5
  415.0 5.4 %copy-start.7 = (f32[8,16,128]{2,1,0:T(8,128)S(1)}, f32[8,16,128]{2,1,0:T(8,128)}, u32[]{:S(2)}) copy-start(f32[8,16,128]{2,1,0:T(8,128)} %get-tuple-element.118) | copy-start | bytes 196612
  415.1 7.9 %copy-start.4 = (f32[112,576]{1,0:T(8,128)S(1)}, f32[112,576]{1,0:T(8,128)}, u32[]{:S(2)}) copy-start(f32[112,576]{1,0:T(8,128)} %get-tuple-element.116) | copy-start | bytes 774148
  423.5 4.1 copy-start
  424.3 2.6 copy-start.2
  427.6 2.0 copy-start.1
Sparse Core Ops, SparseCore 0:
  65.7 66.9 all-gather.4
  134.3 20.3 all-gather.6
  203.5 18.8 reduce-scatter.8
  226.8 74.9 reduce-scatter.12
Sparse Core Ops, SparseCore 1:
  77.8 41.1 reduce-scatter.6
  344.6 58.2 reduce-scatter.10

commit v2 on v1

--- a/solution.py
+++ b/solution.py
@@ -380,7 +380,7 @@
     )
 
 
-VMEM_LIMIT = 56 * 1024 * 1024
+VMEM_LIMIT = 58 * 1024 * 1024
 FULL = 256
 HALF = 128
 WIDE = FULL + HALF
@@ -411,7 +411,7 @@
 def call_kernel(kernel, name, outs, args, scratch=(), collective_id=None, in_spaces=None, out_space=None, us=10):
     single = isinstance(outs, tuple)
     listed = [outs] if single else list(outs)
-    space = pltpu.VMEM if out_space is None else out_space
+    out_spaces = [pltpu.VMEM] * len(listed) if out_space is None else out_space
     spaces = [pltpu.VMEM] * len(args) if in_spaces is None else in_spaces
     params = dict(vmem_limit_bytes=VMEM_LIMIT)
     if collective_id is not None:
@@ -420,7 +420,7 @@
         kernel,
         out_shape=[jax.ShapeDtypeStruct(s, d) for s, d in listed],
         in_specs=[pl.BlockSpec(memory_space=s) for s in spaces],
-        out_specs=[pl.BlockSpec(memory_space=space) for _ in listed],
+        out_specs=[pl.BlockSpec(memory_space=s) for s in out_spaces],
         scratch_shapes=list(scratch),
         compiler_params=pltpu.CompilerParams(**params),
         cost_estimate=pl.CostEstimate(flops=us * 10**9, bytes_accessed=us * 3 * 10**6, transcendentals=0),
@@ -571,16 +571,38 @@
             self.onward(way).start()
             sides[way].start()
 
-    def finish(self):
+    def arrive(self):
         sides = self.sides()
         for way in range(2):
             self.onward(way).wait_recv()
             sides[2 + way].start()
+        for side in sides:
+            side.wait_recv()
+
+    def finish(self):
         for way in range(2):
             self.give(way).wait_send()
             self.onward(way).wait_send()
-        for side in sides:
-            side.wait()
+        for side in self.sides():
+            side.wait_send()
+
+
+def own_weights(refs, all_ref, sem):
+    cores, _, _, lanes = all_ref.shape
+    rank = lax.axis_index(TENSOR)
+    copies, first = [], 0
+    for n, ref in enumerate(refs):
+        rows = ref.shape[0]
+        for half in range(cores):
+            copies.append(
+                pltpu.make_async_copy(
+                    ref.at[:, pl.ds(half * lanes, lanes)],
+                    all_ref.at[half, rank, pl.ds(first, rows), :],
+                    sem.at[n, half],
+                )
+            )
+        first += rows
+    return copies
 
 
 def gather_scratch():
@@ -631,6 +653,45 @@
         return total
 
 
+class PlaneSum:
+    def __init__(self, ranks, src_ref, first, all_ref, own_sem, send_sem, recv_sem):
+        self.ranks, self.src_ref, self.first = ranks, src_ref, first
+        self.all_ref, self.own_sem, self.send_sem, self.recv_sem = all_ref, own_sem, send_sem, recv_sem
+        self.core, self.seq, self.rank = here()
+        self.peers = [(self.core, self.seq, lax.rem(self.rank + step, ranks)) for step in range(1, ranks)]
+
+    def block(self, rank):
+        return self.src_ref.at[rank, :, pl.ds(self.first, self.all_ref.shape[2])]
+
+    def own(self):
+        return pltpu.make_async_copy(self.block(self.rank), self.all_ref.at[self.rank], self.own_sem)
+
+    def copy(self, step):
+        peer = self.peers[step]
+        return remote_copy(
+            self.block(peer[2]), self.all_ref.at[self.rank], self.send_sem.at[step], self.recv_sem.at[step], peer
+        )
+
+    def start(self):
+        self.own().start()
+        for step in range(self.ranks - 1):
+            self.copy(step).start()
+
+    def finish(self):
+        self.own().wait()
+        for step in range(self.ranks - 1):
+            self.copy(step).wait()
+        total = self.all_ref[0].astype(jnp.float32)
+        for origin in range(1, self.ranks):
+            total = total + self.all_ref[origin].astype(jnp.float32)
+        return total
+
+
+def sum_scratch(ranks, rows, columns, dtype):
+    dma = pltpu.SemaphoreType.DMA
+    return [pltpu.VMEM((ranks, rows, columns), dtype), dma, dma((ranks - 1,)), dma((ranks - 1,))]
+
+
 def reduce_scratch(ranks, rows, columns, dtype):
     dma = pltpu.SemaphoreType.DMA
     block = pltpu.VMEM((ranks, rows, columns), dtype)
@@ -724,58 +785,191 @@
                 self.copy(down, 1).wait_send()
 
 
-def prologue_kernel(
+class VectorSum:
+    def __init__(self, cores, depth, ranks, out_ref, src_ref, col_ref, sum_ref, plane_ref, a_send, a_recv, b_send, b_recv, c_send, c_recv):
+        self.cores, self.depth, self.ranks = cores, depth, ranks
+        self.out_ref, self.src_ref, self.col_ref = out_ref, src_ref, col_ref
+        self.sum_ref, self.plane_ref = sum_ref, plane_ref
+        self.sems = ((a_send, a_recv), (b_send, b_recv), (c_send, c_recv))
+        core, seq, self.rank = here()
+        self.mine, self.places = column_places(cores, depth)
+        self.peers = [(core, seq, lax.rem(self.rank + step, ranks)) for step in range(1, ranks)]
+
+    def copies(self, stage):
+        send, recv = self.sems[stage]
+        if stage == 1:
+            return [
+                remote_copy(self.sum_ref, self.plane_ref.at[self.rank], send.at[n], recv.at[n], peer)
+                for n, peer in enumerate(self.peers)
+            ]
+        src = self.src_ref if stage == 0 else self.out_ref
+        dst = self.col_ref if stage == 0 else self.out_ref
+        return [
+            remote_copy(
+                src.at[place if stage == 0 else self.mine],
+                dst.at[self.mine],
+                send.at[n],
+                recv.at[n],
+                column_peer(place, self.cores, self.rank),
+            )
+            for n, place in enumerate(self.places)
+        ]
+
+    def start(self, rows):
+        height = self.src_ref.shape[1]
+        for n, row in enumerate(rows):
+            self.src_ref[n // height, n % height : n % height + 1, :] = row
+        for copy in self.copies(0):
+            copy.start()
+
+    def second(self):
+        for copy in self.copies(0):
+            copy.wait()
+        total = self.src_ref[self.mine]
+        for place in self.places:
+            total = total + self.col_ref[place]
+        self.sum_ref[...] = total
+        for copy in self.copies(1):
+            copy.start()
+
+    def third(self):
+        for copy in self.copies(1):
+            copy.wait()
+        self.plane_ref[self.rank] = self.sum_ref[...]
+        total = self.plane_ref[0]
+        for origin in range(1, self.ranks):
+            total = total + self.plane_ref[origin]
+        self.out_ref[self.mine] = total
+        for copy in self.copies(2):
+            copy.start()
+
+    def finish(self):
+        for copy in self.copies(2):
+            copy.wait()
+
+
+def vector_scratch(shape, places, ranks):
+    full = jnp.float32
+    return [
+        pltpu.VMEM(shape, full),
+        pltpu.VMEM(shape, full),
+        pltpu.VMEM(shape[1:], full),
+        pltpu.VMEM((ranks,) + shape[1:], full),
+    ] + [pltpu.SemaphoreType.DMA((n - 1,)) for n in (places, places, ranks, ranks, places, places)]
+
+
+def front_kernel(
     sizes,
-    x_ref, g_ref, m_ref, idx_ref, vec_ref, wq_ref, wk_ref, wv_ref, ck_ref, cv_ref,
-    xall_ref, gmine_ref, enc_ref, iall_ref, vall_ref, wall_ref,
-    load_sem,
+    x_ref, g_ref, m_ref, idx_ref, vec_ref, ck_ref, cv_ref, wq_ref, wk_ref, wv_ref, wo1_ref, wq2_ref, wo2_ref, w1_ref, w2_ref,
+    bo_ref, gain_ref, shift_ref,
+    xout_ref, eout_ref, wkvout_ref, wsout_ref, sqout_ref, w1out_ref, w2out_ref,
+    gmine_ref, iall_ref, vall_ref, q_ref, k_ref, kt_ref, v_ref, o_ref, lse_ref, oall_ref,
+    h_ref, y_ref, q2_ref, k2_ref, k2t_ref, v2_ref, o2_ref, lse2_ref, o2all_ref,
+    xall_ref, enc_ref, wkv_ref, ws_ref, sq_ref, w1all_ref, w2all_ref, piece_ref, got_ref, vt_ref, s_ref,
+    qsrc_ref, half_ref, other_ref, v2t_ref,
+    load_kv, load_s, load_sq, load_w1, load_w2,
     swap_send, swap_recv, chain_send, chain_recv, side_send, side_recv, own_sem,
-    idx_send, idx_recv, vec_send, vec_recv, *wsems
+    idx_send, idx_recv, vec_send, vec_recv, kvsend, kvrecv, osend, orecv, out_sem,
+    half_sem, qsend, qrecv, o2send, o2recv, *wsems
 ):
     cores, depth, ranks, per_core = sizes
+    low = jnp.bfloat16
     core, seq, rank = here()
     home = rank // per_core
     local = lax.rem(rank, per_core)
+    blocks = cores * depth
+    head = q_ref.shape[1]
     sibling = (1 - core, seq, rank)
     above = (core, lax.rem(seq + 1, depth), rank)
     below = (core, lax.rem(seq + depth - 1, depth), rank)
-    plane = []
-    for step in range(1, cores * ranks):
-        place = lax.rem(rank * cores + core + step, cores * ranks)
-        plane.append((lax.rem(place, cores), seq, place // cores))
-    high = wq_ref.shape[0]
-    lanes = wq_ref.shape[1] // cores
-
-    def load(n, ref, half):
-        return pltpu.make_async_copy(
-            ref.at[:, pl.ds(half * lanes, lanes)],
-            wall_ref.at[half, rank, pl.ds(n * high, high), :],
-            load_sem.at[n, half],
-        )
-
-    loads = [load(n, ref, half) for n, ref in enumerate((wq_ref, wk_ref, wv_ref, ck_ref, cv_ref)) for half in range(cores)]
-    for copy in loads:
-        copy.start()
-    meet(plane + [above, below])
+    mine, places = column_places(cores, depth)
+    gathers = [PlaneGather(ref, *wsems[6 * n : 6 * n + 6]) for n, ref in enumerate((wkv_ref, ws_ref, sq_ref, w1all_ref, w2all_ref))]
+    gather_kv, gather_s, gather_sq, gather_w1, gather_w2 = gathers
+    loads = [
+        own_weights((ck_ref, cv_ref), wkv_ref, load_kv),
+        own_weights((wq_ref, wk_ref, wv_ref), ws_ref, load_s),
+        own_weights((wo1_ref, wq2_ref, wo2_ref), sq_ref, load_sq),
+        own_weights((w1_ref,), w1all_ref, load_w1),
+        own_weights((w2_ref,), w2all_ref, load_w2),
+    ]
+    for group in loads:
+        for copy in group:
+            copy.start()
+    plane = plane_peers(cores, ranks)
+    peers = plane + [column_peer(place, cores, rank) for place in places]
+    meet(peers)
 
     def remote(src, dst, send, recv, device):
-        return pltpu.make_async_remote_copy(
-            src_ref=src, dst_ref=dst, send_sem=send, recv_sem=recv, device_id=device, device_id_type=MESH
-        )
+        return remote_copy(src, dst, send, recv, device)
 
     there = pl.ds((1 - core) * FULL, FULL)
-    mine = pl.ds(core * FULL, FULL)
+    half_rows = pl.ds(core * FULL, FULL)
     swap_x = remote(x_ref.at[local, there], xall_ref.at[seq, 1 - core], swap_send.at[0], swap_recv.at[0], sibling)
     swap_g = remote(g_ref.at[local, there], gmine_ref, swap_send.at[1], swap_recv.at[1], sibling)
     swap_e = remote(m_ref.at[local], enc_ref, swap_send.at[2], swap_recv.at[2], sibling)
-    own_x = pltpu.make_async_copy(x_ref.at[local, mine], xall_ref.at[seq, core], own_sem.at[3])
-    own_g = pltpu.make_async_copy(g_ref.at[local, mine], gmine_ref, own_sem.at[4])
+    own_x = pltpu.make_async_copy(x_ref.at[local, half_rows], xall_ref.at[seq, core], own_sem.at[3])
+    own_g = pltpu.make_async_copy(g_ref.at[local, half_rows], gmine_ref, own_sem.at[4])
     own_e = pltpu.make_async_copy(m_ref.at[local], enc_ref, own_sem.at[5])
 
     @pl.when(core == home)
     def _():
         swap_x.start()
         own_x.start()
+
+    for copy in loads[0]:
+        copy.wait()
+    gather_kv.start()
+
+    def chain(block, target, way):
+        part = xall_ref.at[block, core]
+        return remote(part, part, chain_send.at[way, block], chain_recv.at[block], target)
+
+    def aside(block):
+        part = xall_ref.at[block, core]
+        return remote(part, part, side_send.at[block], side_recv.at[block], sibling)
+
+    def chain_step(step):
+        up, down = seq - step, seq + step
+
+        @pl.when(up >= 0)
+        def _():
+            if step > 0:
+                chain(up, above, 0).wait_recv()
+
+            @pl.when(seq + 1 < depth)
+            def _():
+                chain(up, above, 0).start()
+
+            aside(up).start()
+
+        @pl.when(down < depth)
+        def _():
+            if step > 0:
+                chain(down, below, 1).wait_recv()
+
+            @pl.when(seq > 0)
+            def _():
+                chain(down, below, 1).start()
+
+            if step > 0:
+                aside(down).start()
+
+    @pl.when(core == home)
+    def _():
+        own_x.wait()
+
+    @pl.when(core != home)
+    def _():
+        swap_x.wait_recv()
+
+    chain_step(0)
+
+    @pl.when(core == home)
+    def _():
+        swap_e.start()
+        own_e.start()
+        swap_g.start()
+        own_g.start()
 
     def give_index(item, half):
         return remote(
@@ -799,78 +993,207 @@
                 own.start()
                 own.wait()
 
-    peers = [(core, seq, lax.rem(rank + step, ranks)) for step in range(1, ranks)]
-
-    def give_vec(step):
-        return remote(vec_ref, vall_ref.at[rank], vec_send.at[step], vec_recv.at[step], peers[step - 1])
-
-    for step in range(1, ranks):
-        give_vec(step).start()
+    across = [(core, seq, lax.rem(rank + step, ranks)) for step in range(1, ranks)]
+    vecs = [
+        remote(vec_ref, vall_ref.at[rank], vec_send.at[step], vec_recv.at[step], peer)
+        for step, peer in enumerate(across)
+    ]
+    for copy in vecs:
+        copy.start()
     own_vec = pltpu.make_async_copy(vec_ref, vall_ref.at[rank], own_sem.at[1])
     own_vec.start()
 
-    weights = PlaneGather(wall_ref, *wsems)
+    gather_kv.forward()
+    for copy in loads[1]:
+        copy.wait()
+    gather_s.start()
+    chain_step(1)
+    for copy in vecs:
+        copy.wait()
+    own_vec.wait()
 
     @pl.when(core == home)
     def _():
-        own_x.wait()
+        own_e.wait()
 
     @pl.when(core != home)
     def _():
-        swap_x.wait_recv()
-
-    def chain(block, target, way):
+        swap_e.wait_recv()
+
+    for origin in range(ranks):
+
+        @pl.when(jnp.logical_not((core == home) & (rank == origin)))
+        def _():
+            remote(
+                idx_ref.at[0], iall_ref.at[origin], idx_send.at[0, 0], idx_recv.at[origin], sibling
+            ).wait_recv()
+
+    gather_kv.arrive()
+
+    def give_kv(step):
         return remote(
-            xall_ref.at[block, core], xall_ref.at[block, core], chain_send.at[way, block], chain_recv.at[block], target
-        )
-
-    def aside(block):
-        return remote(
-            xall_ref.at[block, core], xall_ref.at[block, core], side_send.at[block], side_recv.at[block], sibling
-        )
-
-    for step in range(depth):
-        up, down = seq - step, seq + step
-
-        @pl.when(up >= 0)
-        def _():
-            if step > 0:
-                chain(up, above, 0).wait_recv()
-
-            @pl.when(seq + 1 < depth)
-            def _():
-                chain(up, above, 0).start()
-
-            aside(up).start()
-
-        @pl.when(down < depth)
-        def _():
-            if step > 0:
-                chain(down, below, 1).wait_recv()
-
-            @pl.when(seq > 0)
-            def _():
-                chain(down, below, 1).start()
-
-            if step > 0:
-                aside(down).start()
-
-        if step == 0:
-            for copy in loads:
-                copy.wait()
-            weights.start()
-
-            @pl.when(core == home)
-            def _():
-                swap_e.start()
-                own_e.start()
-                swap_g.start()
-                own_g.start()
-
-    weights.forward()
-
-    for step in range(depth):
-        up, down = seq - step, seq + step
+            piece_ref.at[step], got_ref.at[step], kvsend.at[step], kvrecv.at[step],
+            (core, lax.rem(seq + 1 + step, depth), rank),
+        )
+
+    def pick(step):
+        retrieve(lax.rem(seq + 1 + step, depth), step, enc_ref, wkv_ref, vall_ref, iall_ref, piece_ref)
+
+    pick(0)
+    gather_s.forward()
+    for copy in loads[2]:
+        copy.wait()
+    gather_sq.start()
+    pick(1)
+    chain_step(2)
+    pick(2)
+    pick(3)
+    for step in range(3, depth):
+        chain_step(step)
+    for step in range(depth - 1):
+        give_kv(step).start()
+    gather_s.arrive()
+    gather_sq.forward()
+    for copy in loads[3]:
+        copy.wait()
+    gather_w1.start()
+    for block in range(depth):
+        aside(block).wait_recv()
+
+    outs = [
+        pltpu.make_async_copy(src, dst, out_sem.at[n])
+        for n, (src, dst) in enumerate(
+            (
+                (xall_ref, xout_ref),
+                (enc_ref, eout_ref),
+                (wkv_ref, wkvout_ref),
+                (ws_ref, wsout_ref),
+                (sq_ref, sqout_ref),
+                (w1all_ref, w1out_ref),
+                (w2all_ref, w2out_ref),
+            )
+        )
+    ]
+    for copy in outs[:4]:
+        copy.start()
+
+    w = jnp.concatenate([head_rows(ws_ref, seq, n, which, head) for n in range(3) for which in (2 * core, 1)], axis=0)
+    rows = [vall_ref[seq, n : n + 1, :] for n in range(2)]
+    bias = column_of(
+        jnp.concatenate(
+            [
+                piece
+                for row in rows
+                for piece in (jnp.where(core == 0, row[:, :head], row[:, 2 * head : 3 * head]), row[:, head : 2 * head])
+            ],
+            axis=1,
+        )
+    )
+
+    def project(block, carry):
+        lanes = pl.ds(pl.multiple_of(block * FULL, FULL), FULL)
+        flat = dot_nt(w, xall_ref[block // cores, lax.rem(block, cores)])
+        q = ((flat[: 2 * head] + bias[: 2 * head]) * SCALE).astype(low)
+        shared = jnp.where(core == 0, q[head:, :HALF], q[head:, HALF:])
+        q_ref[block] = jnp.concatenate([q[:head], shared], axis=1)
+        k = flat[2 * head : 4 * head].astype(low)
+        v = (flat[4 * head :] + bias[2 * head :]).astype(low)
+        kt_ref[:, lanes] = k
+        vt_ref[:, lanes] = v
+        k_ref[lanes, :] = k.T
+        v_ref[lanes, :] = v.T
+        return carry
+
+    lax.fori_loop(0, blocks, project, 0)
+
+    back = ColumnSend(cores, depth, o_ref, oall_ref, osend, orecv)
+
+    def attend(block):
+        out, lse = attend_block(block, True, core, blocks * FULL, q_ref[block], k_ref, vt_ref, s_ref)
+        o_ref[block] = out
+        lse_ref[block] = lse
+        return out
+
+    def step(n, carry):
+        attend(lax.rem(mine + 1 + n, blocks))
+        back.copy(n).start()
+        return carry
+
+    lax.fori_loop(0, 3, step, 0)
+    gather_sq.arrive()
+    outs[4].start()
+    lax.fori_loop(3, 6, step, 0)
+    gather_w1.forward()
+    for copy in loads[4]:
+        copy.wait()
+    gather_w2.start()
+    lax.fori_loop(6, blocks - 1, step, 0)
+    oall_ref[mine] = attend(mine)
+    for n in range(blocks - 1):
+        back.wait_from(n)
+
+    part = 3 * head
+    o1 = assembled(oall_ref, depth).T
+    h1 = xall_ref[seq, core].astype(jnp.float32) + dot_nn(o1, late_square(sq_ref, 0, part)) + as_row(bo_ref)
+    z, _ = centred_rows(h1)
+    y1 = (z * as_row(gain_ref) + as_row(shift_ref)).astype(low)
+    h_ref[...] = h1
+    y_ref[...] = y1
+    bias2 = column_of(jnp.concatenate([vall_ref[of, 2:3, :part] for of in range(ranks)], axis=1))
+    q2t = ((dot_nt(late_square(sq_ref, 1, part), y1) + bias2) * SCALE).astype(low)
+    dispersed(q2t, qsrc_ref, depth)
+    ask = ColumnSend(cores, depth, qsrc_ref, q2_ref, qsend, qrecv)
+    for n in range(blocks - 1):
+        ask.copy(n).start()
+    q2_ref[mine] = qsrc_ref[mine]
+
+    slots = k2_ref.shape[0]
+    total = piece_ref[depth - 1]
+    for n in range(depth - 1):
+        give_kv(n).wait_recv()
+        total = total + got_ref[n]
+    half_ref[...] = total[:, slots:]
+    swap = remote(half_ref, other_ref, half_sem.at[0], half_sem.at[1], sibling)
+    swap.start()
+    gather_w1.arrive()
+    outs[5].start()
+    swap.wait()
+    half, other = half_ref[...], other_ref[...]
+    shared = jnp.concatenate([jnp.where(core == 0, half, other), jnp.where(core == 0, other, half)], axis=1)
+    kt = jnp.concatenate([total[:head, :slots], shared[:head]], axis=0)
+    vt = jnp.concatenate([total[head:, :slots], shared[head:]], axis=0)
+    k2t_ref[...] = kt
+    v2t_ref[...] = vt
+    k2_ref[...] = kt.T
+    v2_ref[...] = vt.T
+
+    back2 = ColumnSend(cores, depth, o2_ref, o2all_ref, o2send, o2recv)
+
+    def attend2(block):
+        out, lse = attend_block(block, False, core, slots, q2_ref[block], k2_ref, v2t_ref, s_ref)
+        o2_ref[block] = out
+        lse2_ref[block] = lse
+        return out
+
+    o2all_ref[mine] = attend2(mine)
+
+    def step2(n, carry):
+        ask.wait_from(n)
+        attend2(lax.rem(mine + blocks - 1 - n, blocks))
+        back2.copy(blocks - 2 - n).start()
+        return carry
+
+    lax.fori_loop(0, 2, step2, 0)
+    gather_w2.forward()
+    lax.fori_loop(2, 5, step2, 0)
+    gather_w2.arrive()
+    outs[6].start()
+    lax.fori_loop(5, blocks - 1, step2, 0)
+
+    for n in range(depth - 1):
+        give_kv(n).wait_send()
+    for n in range(depth):
+        up, down = seq - n, seq + n
 
         @pl.when((up >= 0) & (seq + 1 < depth))
         def _():
@@ -880,61 +1203,94 @@
         def _():
             chain(down, below, 1).wait_send()
 
-    for block in range(depth):
-        aside(block).wait()
-    for step in range(1, ranks):
-        give_vec(step).wait()
-    weights.finish()
-    own_vec.wait()
-    for item in range(per_core):
-        for half in range(cores):
-
-            @pl.when(jnp.logical_not(is_me(item, half)))
-            def _():
-                give_index(item, half).wait_send()
+        aside(n).wait_send()
 
     @pl.when(core == home)
     def _():
         for copy in (swap_x, swap_g, swap_e):
             copy.wait_send()
         own_g.wait()
-        own_e.wait()
 
     @pl.when(core != home)
     def _():
         swap_g.wait_recv()
-        swap_e.wait_recv()
-
-    for origin in range(ranks):
-
-        @pl.when(jnp.logical_not((core == home) & (rank == origin)))
-        def _():
-            remote(
-                idx_ref.at[0], iall_ref.at[origin], idx_send.at[0, 0], idx_recv.at[origin], sibling
-            ).wait_recv()
-
-
-def prologue(dec_input, out_grad, encoder_states, retrieved, vectors, weights):
+
+    for item in range(per_core):
+        for half in range(cores):
+
+            @pl.when(jnp.logical_not(is_me(item, half)))
+            def _():
+                give_index(item, half).wait_send()
+
+    ask.finish_sends()
+    back.finish_sends()
+    back2.finish()
+    for gather in gathers:
+        gather.finish()
+    for copy in outs:
+        copy.wait()
+
+
+def front(dec_input, out_grad, encoder_states, retrieved, vectors, kv, selfs, squares, w1, w2, rows1):
     cores, depth, ranks = lax.axis_size(ITEM), lax.axis_size(SEQ), lax.axis_size(TENSOR)
     per_core, _, width = dec_input.shape
     enc_rows = encoder_states.shape[1]
-    high = len(weights) * weights[0].shape[0]
-    low = jnp.bfloat16
+    slots = retrieved.shape[2]
+    part = kv[0].shape[0]
+    head = part // 3
+    places = cores * depth
+    rows = places * FULL
+    lanes = width // cores
+    low, full = jnp.bfloat16, jnp.float32
     dma = pltpu.SemaphoreType.DMA
+
+    def all_of(weights):
+        return (cores, ranks, sum(w.shape[0] for w in weights), lanes)
+
+    big = [(depth, cores, FULL, width), (enc_rows, width)] + [all_of(w) for w in (kv, selfs, squares, [w1], [w2])]
+    kv_shape = (2 * head, slots + slots // 2)
+    parts = (places, head, WIDE)
+    small = [
+        ((FULL, width), low),
+        ((ranks,) + retrieved.shape[1:], retrieved.dtype),
+        ((ranks,) + vectors.shape, vectors.dtype),
+        ((places, head, WIDE), low),
+        ((rows, 2 * head), low),
+        ((2 * head, rows), low),
+        ((rows, 2 * head), low),
+        ((places, head, WIDE), low),
+        ((places, 1, WIDE), full),
+        (parts, low),
+        ((FULL, width), full),
+        ((FULL, width), low),
+        (parts, low),
+        ((slots, 2 * head), low),
+        ((2 * head, slots), low),
+        ((slots, 2 * head), low),
+        (parts, low),
+        ((places, 1, WIDE), full),
+        (parts, low),
+    ]
     return call_kernel(
-        functools.partial(prologue_kernel, (cores, depth, ranks, per_core)),
-        "prologue",
-        [
-            ((depth, cores, FULL, width), low),
-            ((FULL, width), low),
-            ((enc_rows, width), low),
-            ((ranks,) + retrieved.shape[1:], retrieved.dtype),
-            ((ranks,) + vectors.shape, vectors.dtype),
-            ((cores, ranks, high, width // cores), low),
-        ],
-        [dec_input, out_grad, encoder_states, retrieved, vectors, *weights],
-        scratch=[
-            dma((len(weights), cores)),
+        functools.partial(front_kernel, (cores, depth, ranks, per_core)),
+        "front",
+        [(shape, low) for shape in big] + small,
+        [dec_input, out_grad, encoder_states, retrieved, vectors, *kv, *selfs, *squares, w1, w2, *rows1],
+        scratch=[pltpu.VMEM(shape, low) for shape in big]
+        + [
+            pltpu.VMEM((depth,) + kv_shape, low),
+            pltpu.VMEM((depth - 1,) + kv_shape, low),
+            pltpu.VMEM((2 * head, rows), low),
+            pltpu.VMEM((rows, WIDE), full),
+            pltpu.VMEM(parts, low),
+            pltpu.VMEM((2 * head, slots // 2), low),
+            pltpu.VMEM((2 * head, slots // 2), low),
+            pltpu.VMEM((2 * head, slots), low),
+            dma((2, cores)),
+            dma((3, cores)),
+            dma((3, cores)),
+            dma((1, cores)),
+            dma((1, cores)),
             dma((3,)),
             dma((3,)),
             dma((2, depth)),
@@ -944,13 +1300,18 @@
             dma((6,)),
             dma((per_core, cores)),
             dma((ranks,)),
-            dma((ranks,)),
-            dma((ranks,)),
         ]
-        + gather_scratch(),
+        + send_scratch(ranks)
+        + send_scratch(depth)
+        + send_scratch(places)
+        + [dma((7,)), dma((2,))]
+        + send_scratch(places)
+        + send_scratch(places)
+        + gather_scratch() * 5,
         collective_id=1,
-        in_spaces=[pl.ANY] * 10,
-        us=32,
+        in_spaces=[pl.ANY] * 15 + [pltpu.VMEM] * 3,
+        out_space=[pl.ANY] * 7 + [pltpu.VMEM] * len(small),
+        us=90,
     )
 
 
@@ -968,16 +1329,25 @@
     return jnp.concatenate([ref[half, group, rows, :] for half in range(ref.shape[0])], axis=1)
 
 
+def as_row(ref):
+    return ref[...].reshape(1, ref.shape[0])
+
+
+def column_of(row):
+    return jnp.broadcast_to(row, (8, row.shape[1])).T[:, :1]
+
+
 def kv_rows(w_ref, group, head_index, head):
     return jnp.concatenate(
-        [head_rows(w_ref, group, 3, head_index, head), head_rows(w_ref, group, 4, head_index, head)], axis=0
-    )
-
-
-def retrieve_kernel(ranks, head, enc_ref, w_ref, b_ref, idx_ref, out_ref):
+        [head_rows(w_ref, group, 0, head_index, head), head_rows(w_ref, group, 1, head_index, head)], axis=0
+    )
+
+
+def retrieve(group, step, enc_ref, w_ref, vec_ref, idx_ref, out_ref):
     core, seq, _ = here()
     enc_rows = enc_ref.shape[0]
     slots = idx_ref.shape[2]
+    head = out_ref.shape[1] // 2
     low = jnp.bfloat16
     tall = enc_rows // 3
 
@@ -989,29 +1359,16 @@
             total = total + dot_nn(table[:, part * tall : (part + 1) * tall], hot)
         return total.astype(low)
 
-    def step(group, carry):
-        w = jnp.concatenate([kv_rows(w_ref, group, 2 * core, head), kv_rows(w_ref, group, 1, head)], axis=0)
-        table = (dot_nt(w, enc_ref[...]) + b_ref[group]).astype(low)
-        whole = idx_ref[group, pl.ds(2 * core, 1), :]
-        shared = idx_ref[group, pl.ds(1, 1), :]
-        half = jnp.where(core == 0, shared[:, : slots // 2], shared[:, slots // 2 :])
-        out_ref[group] = jnp.concatenate(
-            [picked(table[: 2 * head], whole), picked(table[2 * head :], half)], axis=1
-        )
-        return carry
-
-    lax.fori_loop(0, ranks, step, 0)
-
-
-def retrieve(enc, w_all, bias, index):
-    ranks, _, slots = index.shape
-    head = w_all.shape[2] // 15
-    return call_kernel(
-        functools.partial(retrieve_kernel, ranks, head),
-        "retrieve",
-        ((ranks, 2 * head, slots + slots // 2), jnp.bfloat16),
-        [enc, w_all, bias, index],
-    )
+    w = jnp.concatenate([kv_rows(w_ref, group, 2 * core, head), kv_rows(w_ref, group, 1, head)], axis=0)
+    row = vec_ref[group, 3:4, :]
+    blank = jnp.zeros((1, head), jnp.float32)
+    first = jnp.where(core == 0, row[:, :head], row[:, 2 * head : 3 * head])
+    bias = column_of(jnp.concatenate([blank, first, blank, row[:, head : 2 * head]], axis=1))
+    table = (dot_nt(w, enc_ref[...]) + bias).astype(low)
+    whole = idx_ref[group, pl.ds(2 * core, 1), :]
+    shared = idx_ref[group, pl.ds(1, 1), :]
+    half = jnp.where(core == 0, shared[:, : slots // 2], shared[:, slots // 2 :])
+    out_ref[step] = jnp.concatenate([picked(table[: 2 * head], whole), picked(table[2 * head :], half)], axis=1)
 
 
 def assembled(parts_ref, depth, columns=None):
@@ -1063,9 +1420,10 @@
 
 def middle_kernel(
     cores, depth, ranks, per_core, part,
-    o_ref, y1_ref, g_ref, w_ref, ffn_ref, bo_ref, gain2_ref, shift2_ref, b1_ref, b2_ref, gain3_ref, shift3_ref,
+    o_ref, y1_ref, g_ref, w_ref, w1_in, w2_in, bo_ref, gain2_ref, shift2_ref, b1_ref, b2_ref, gain3_ref, shift3_ref,
     layer_ref, do_ref, dh2_ref, vec_ref, grad_ref,
-    slope_ref, a_ref, df_ref, out_ref, dosrc_ref, dosend, dorecv, *deal_sems
+    w1_ref, w2_ref, slope_ref, a_ref, df_ref, out_ref, dosrc_ref, turn_ref, give_ref, got_ref,
+    ffn_sem, grad_sem, dosend, dorecv, *deal_sems
 ):
     low = jnp.bfloat16
     core, seq, rank = here()
@@ -1076,34 +1434,41 @@
     greet(peers)
     width = y1_ref.shape[1]
     lanes = width // cores
+    loads = [
+        pltpu.make_async_copy(src, dst, ffn_sem.at[n]) for n, (src, dst) in enumerate(((w1_in, w1_ref), (w2_in, w2_ref)))
+    ]
+    for load in loads:
+        load.start()
     o2t = assembled(o_ref, depth)
     wo2 = late_square(w_ref, 2, part)
-    h2 = y1_ref[...].astype(jnp.float32) + dot_nn(o2t.T, wo2) + bo_ref[...]
+    h2 = y1_ref[...].astype(jnp.float32) + dot_nn(o2t.T, wo2) + as_row(bo_ref)
     z2, spread2 = centred_rows(h2)
-    y2 = (z2 * gain2_ref[...] + shift2_ref[...]).astype(low)
+    y2 = (z2 * as_row(gain2_ref) + as_row(shift2_ref)).astype(low)
 
     def hidden_in(of, half):
-        return ffn_ref[half, of, :width, :]
+        return w1_ref[half, of]
 
     def hidden_out(of):
-        return jnp.concatenate([ffn_ref[half, of, width:, :] for half in range(cores)], axis=1)
+        return jnp.concatenate([w2_ref[half, of] for half in range(cores)], axis=1)
 
     root = 0.7071067811865476
-    h3 = y2.astype(jnp.float32) + b2_ref[...]
+    h3 = y2.astype(jnp.float32) + as_row(b2_ref)
+    for load in loads:
+        load.wait()
     for of in range(ranks):
-        f = jnp.concatenate([dot_nn(y2, hidden_in(of, half)) for half in range(cores)], axis=1) + b1_ref[of]
+        f = jnp.concatenate([dot_nn(y2, hidden_in(of, half)) for half in range(cores)], axis=1) + b1_ref[of, 4:5, :]
         cdf = 0.5 * (1.0 + lax.erf(f * root))
         a = (f * cdf).astype(low)
         slope_ref[of] = cdf + f * (0.3989422804014327 * jnp.exp(-0.5 * f * f))
         a_ref[of] = a
         h3 = h3 + dot_nn(a, hidden_out(of))
     z3, spread3 = centred_rows(h3)
-    out_ref[...] = (z3 * gain3_ref[...] + shift3_ref[...]).astype(low)
+    out_ref[...] = (z3 * as_row(gain3_ref) + as_row(shift3_ref)).astype(low)
     pl.semaphore_wait(pltpu.get_barrier_semaphore(), len(peers))
     deal = Deal(cores, ranks, per_core, lambda target: out_ref, layer_ref, *deal_sems)
     deal.start()
 
-    dh3, gg3, gs3 = norm_back(z3, spread3, g_ref[...].astype(jnp.float32), gain3_ref[...])
+    dh3, gg3, gs3 = norm_back(z3, spread3, g_ref[...].astype(jnp.float32), as_row(gain3_ref))
     e3 = dh3.astype(low)
     dy2 = dh3
     for of in range(ranks):
@@ -1111,7 +1476,7 @@
         df_ref[of] = df
         for half in range(cores):
             dy2 = dy2 + dot_nt(df[:, half * lanes : (half + 1) * lanes], hidden_in(of, half))
-    dh2, gg2, gs2 = norm_back(z2, spread2, dy2, gain2_ref[...])
+    dh2, gg2, gs2 = norm_back(z2, spread2, dy2, as_row(gain2_ref))
     e2 = dh2.astype(low)
     dispersed(dot_nt(wo2, e2).astype(low), dosrc_ref, depth)
     ask = ColumnSend(cores, depth, dosrc_ref, do_ref, dosend, dorecv)
@@ -1126,22 +1491,44 @@
     vec_ref[3:4] = gg2
     vec_ref[4:5] = gs2
     vec_ref[5:6] = jnp.sum(e2.astype(jnp.float32), axis=0, keepdims=True)
-    e3t, y2t, e2t = e3.T, y2.T, e2.T
+    turn_ref[0] = y2.T
+    turn_ref[1] = e3.T
+    turn_ref[2] = e2.T
     pad = jnp.zeros((-part % 128, FULL), low)
+
+    def grad_of(of, half):
+        rows = pl.ds(pl.multiple_of(half * lanes, lanes), lanes)
+        o2_part = jnp.concatenate([o2t[of * part : (of + 1) * part], pad], axis=0)
+        return (
+            dot_nn(turn_ref[0, rows, :], df_ref[of]),
+            dot_nn(turn_ref[1, rows, :], a_ref[of]),
+            dot_nt(turn_ref[2, rows, :], o2_part),
+        )
+
+    spans = (slice(0, width), slice(width, 2 * width), slice(2 * width, None))
+
+    def swap(of):
+        return remote_copy(
+            give_ref.at[of], got_ref.at[of], grad_sem.at[0, of], grad_sem.at[1, of], (1 - core, seq, rank)
+        )
+
     for of in range(ranks):
-        df = df_ref[of]
-        vec_ref[6 + of : 7 + of] = jnp.sum(df.astype(jnp.float32), axis=0, keepdims=True)
-        o2_part = jnp.concatenate([o2t[of * part : (of + 1) * part], pad], axis=0)
-        for half in range(cores):
-            rows = slice(half * lanes, (half + 1) * lanes)
-            grad_ref[half, of, :, :width] = dot_nn(y2t[rows], df).astype(low)
-            grad_ref[half, of, :, width : 2 * width] = dot_nn(e3t[rows], a_ref[of]).astype(low)
-            grad_ref[half, of, :, 2 * width :] = dot_nt(e2t[rows], o2_part).astype(low)
+        vec_ref[6 + of : 7 + of] = jnp.sum(df_ref[of].astype(jnp.float32), axis=0, keepdims=True)
+        for span, grad in zip(spans, grad_of(of, 1 - core)):
+            give_ref[of, :, span] = grad.astype(low)
+        swap(of).start()
+    for of in range(ranks):
+        grads = grad_of(of, core)
+        swap(of).wait_recv()
+        for span, grad in zip(spans, grads):
+            grad_ref[of, :, span] = (grad + got_ref[of, :, span].astype(jnp.float32)).astype(low)
+    for of in range(ranks):
+        swap(of).wait_send()
     ask.finish()
     deal.finish()
 
 
-def middle(per_core, o2, y1, grad_mine, squares, ffn, vectors):
+def middle(per_core, o2, y1, grad_mine, squares, w1, w2, vectors):
     cores, depth, ranks = lax.axis_size(ITEM), lax.axis_size(SEQ), lax.axis_size(TENSOR)
     places, head, _ = o2.shape
     rows, width = y1.shape
@@ -1156,19 +1543,27 @@
             (o2.shape, low),
             ((rows, width), full),
             ((6 + ranks, width), full),
-            ((cores, ranks, lanes, columns), low),
+            ((ranks, lanes, columns), low),
         ],
-        [o2, y1, grad_mine, squares, ffn, *vectors],
+        [o2, y1, grad_mine, squares, w1, w2, *vectors],
         scratch=[
+            pltpu.VMEM(w1.shape, low),
+            pltpu.VMEM(w2.shape, low),
             pltpu.VMEM((ranks, rows, hidden), full),
             pltpu.VMEM((ranks, rows, hidden), low),
             pltpu.VMEM((ranks, rows, hidden), low),
             pltpu.VMEM((rows, width), low),
             pltpu.VMEM(o2.shape, low),
+            pltpu.VMEM((3, width, rows), low),
+            pltpu.VMEM((ranks, lanes, columns), low),
+            pltpu.VMEM((ranks, lanes, columns), low),
+            pltpu.SemaphoreType.DMA((2,)),
+            pltpu.SemaphoreType.DMA((2, ranks)),
         ]
         + send_scratch(places)
         + deal_scratch(cores, ranks, per_core),
         collective_id=4,
+        in_spaces=[pltpu.VMEM] * 4 + [pl.ANY] * 2 + [pltpu.VMEM] * len(vectors),
         us=22,
     )
 
@@ -1224,79 +1619,56 @@
             part_ref[half, rank] = jnp.concatenate([low_rows, high_rows], axis=1)
 
 
-def last_kernel(
-    cores, depth, ranks, per_core,
-    parts_ref, dh1_ref, w_ref, encp_ref, self_ref, vec_ref, red2_ref, red4_ref,
-    in_ref, enc_ref, wself_ref, vout_ref, w2_ref, w4_ref,
-    dx_ref, got_ref, sum_ref, encall_ref, column_ref, group_ref, plane_ref, vcol_ref, vsum_ref, vplane_ref,
-    r2_ref, r4_ref,
-    swap_sem, col_send, col_recv, vcol_send, vcol_recv, send_sem, recv_sem, vsend, vrecv, vback_send, vback_recv,
-    z_send, z_recv, *deal_sems
-):
-    core, seq, rank = here()
+class SeqSum:
+    def __init__(self, depth, src_ref, all_ref, send_sem, recv_sem):
+        self.depth, self.src_ref, self.all_ref = depth, src_ref, all_ref
+        self.send_sem, self.recv_sem = send_sem, recv_sem
+        self.core, self.seq, self.rank = here()
+
+    def copy(self, step):
+        target = lax.rem(self.seq + 1 + step, self.depth)
+        return remote_copy(
+            self.src_ref.at[target],
+            self.all_ref.at[self.seq],
+            self.send_sem.at[step],
+            self.recv_sem.at[step],
+            (self.core, target, self.rank),
+        )
+
+    def start(self):
+        for step in range(self.depth - 1):
+            self.copy(step).start()
+
+    def finish(self):
+        for step in range(self.depth - 1):
+            self.copy(step).wait()
+        self.all_ref[self.seq] = self.src_ref[self.seq]
+        total = self.all_ref[0].astype(jnp.float32)
+        for origin in range(1, self.depth):
+            total = total + self.all_ref[origin].astype(jnp.float32)
+        return total
+
+
+def input_rows(depth, parts_ref, dh1_ref, w_ref):
     low = jnp.bfloat16
-    head = parts_ref.shape[1]
-    part = 3 * head
-    count = cores * depth
-    mine, places = column_places(cores, depth)
-    peers = [(core, seq, lax.rem(rank + step, ranks)) for step in range(1, ranks)]
-    others = [(1 - core, seq, peer[2]) for peer in peers]
-    greeted = [column_peer(place, cores, rank) for place in places] + peers + others
-    meet(greeted)
-
-    swap = remote_copy(encp_ref.at[1 - core], got_ref, swap_sem.at[0], swap_sem.at[1], (1 - core, seq, rank))
-    swap.start()
-    column = []
-    for step, place in enumerate(places):
-        target = column_peer(place, cores, rank)
-        column.append(
-            remote_copy(vec_ref.at[place], vcol_ref.at[mine], vcol_send.at[step], vcol_recv.at[step], target)
-        )
-        column.append(
-            remote_copy(self_ref.at[place], column_ref.at[mine], col_send.at[step], col_recv.at[step], target)
-        )
-    for copy in column:
-        copy.start()
-    along = []
-    for step in range(1, depth):
-        target = lax.rem(seq + step, depth)
-        for n, (src, dst) in enumerate(((red2_ref, r2_ref), (red4_ref, r4_ref))):
-            along.append(
-                remote_copy(
-                    src.at[target], dst.at[seq], z_send.at[n, step - 1], z_recv.at[n, step - 1], (core, target, rank)
-                )
-            )
-    for copy in along:
-        copy.start()
-
+    part = 3 * parts_ref.shape[1]
     dqt = assembled(parts_ref, depth)
     stack_k, stack_v = [], []
     for group in range(depth):
         first, second = parts_ref[2 * group], parts_ref[2 * group + 1]
         for n, stack in ((0, stack_k), (1, stack_v)):
             whole = slice(WIDE + n * FULL, WIDE + (n + 1) * FULL)
-            shared = slice(WIDE + (n + 2) * FULL, WIDE + (n + 3) * FULL)
-            both = (first[:, shared].astype(jnp.float32) + second[:, shared].astype(jnp.float32)).astype(low)
+            shared = slice(WIDE + 2 * FULL + n * HALF, WIDE + 2 * FULL + (n + 1) * HALF)
+            both = jnp.concatenate([first[:, shared], second[:, shared]], axis=1)
             stack += [first[:, whole], both, second[:, whole]]
     dx = dh1_ref[...] + dot_nn(dqt.T, late_square(w_ref, 0, part)) * SCALE
     dx = dx + dot_nn(jnp.concatenate(stack_k, axis=0).T, late_square(w_ref, 1, part))
     dx = dx + dot_nn(jnp.concatenate(stack_v, axis=0).T, late_square(w_ref, 2, part))
-    dx_ref[...] = dx.astype(low)
-    deal = Deal(cores, ranks, per_core, lambda target: dx_ref, in_ref, *deal_sems[:3])
-    deal.start()
-
-    swap.wait()
-    sum_ref[...] = (encp_ref[core].astype(jnp.float32) + got_ref[...].astype(jnp.float32)).astype(low)
-    deal_enc = Deal(cores, ranks, per_core, lambda target: sum_ref.at[target], encall_ref, *deal_sems[3:])
-    deal_enc.start()
-
-    for copy in column:
-        copy.wait()
-    total = vec_ref[mine]
-    for place in places:
-        total = total + vcol_ref[place]
-    vsum_ref[...] = total
-    column_ref[mine] = self_ref[mine]
+    return dx.astype(low)
+
+
+def merge_heads(depth, head, column_ref, group_ref):
+    low = group_ref.dtype
     for group in range(depth):
         first, second = column_ref[2 * group], column_ref[2 * group + 1]
         pieces = []
@@ -1306,105 +1678,71 @@
             both = (first[:, shared].astype(jnp.float32) + second[:, shared].astype(jnp.float32)).astype(low)
             pieces += [first[:, whole], both, second[:, whole]]
         group_ref[group] = jnp.concatenate(pieces, axis=1)
-    plane = []
-    for step, peer in enumerate(peers):
-        plane.append(remote_copy(vsum_ref, vplane_ref.at[rank], vsend.at[step], vrecv.at[step], peer))
-        plane.append(
-            remote_copy(group_ref.at[peer[2]], plane_ref.at[rank], send_sem.at[step], recv_sem.at[step], peer)
-        )
-    for copy in plane:
-        copy.start()
-
-    for copy in along:
-        copy.wait()
-    for src, dst, out in ((red2_ref, r2_ref, w2_ref), (red4_ref, r4_ref, w4_ref)):
-        total = src[seq].astype(jnp.float32)
-        for step in range(1, depth):
-            total = total + dst[lax.rem(seq + step, depth)].astype(jnp.float32)
-        out[...] = total
-
-    for copy in plane:
-        copy.wait()
-    vplane_ref[rank] = vsum_ref[...]
-    total = vplane_ref[0]
-    for origin in range(1, ranks):
-        total = total + vplane_ref[origin]
-    vout_ref[mine] = total
-    vectors = []
-    for step, place in enumerate(places):
-        vectors.append(
-            remote_copy(
-                vout_ref.at[mine], vout_ref.at[mine], vback_send.at[step], vback_recv.at[step],
-                column_peer(place, cores, rank),
-            )
-        )
-    for copy in vectors:
-        copy.start()
-    total = group_ref[rank].astype(jnp.float32)
-    for step in range(1, ranks):
-        total = total + plane_ref[lax.rem(rank + step, ranks)].astype(jnp.float32)
-    wself_ref[...] = total
-    deal_enc.finish()
-    fold = encall_ref.shape[2]
-    for item in range(per_core):
-        for half in range(cores):
-            for side in range(2):
-                rows = slice((2 * half + side) * fold, (2 * half + side + 1) * fold)
-                enc_ref[item, rows, :] = encall_ref[item, half, :, side * part : (side + 1) * part]
-    for copy in vectors:
-        copy.wait()
-    deal.finish()
-
-
-def last_rows(per_core, dqkv, dh1, early, enc_parts, self_parts, vectors, second, fourth):
-    cores, depth, ranks = lax.axis_size(ITEM), lax.axis_size(SEQ), lax.axis_size(TENSOR)
-    places, head, _ = dqkv.shape
-    rows, width = dh1.shape
-    low, full = jnp.bfloat16, jnp.float32
-    dma = pltpu.SemaphoreType.DMA
-    _, high, lanes = self_parts.shape
-    wide = lanes // 2 * 3
-    _, _, fold, side = enc_parts.shape
-    columns = second.shape[1]
-    second = second.reshape(depth, -1, columns)
-    fourth = fourth.reshape(depth, -1, columns)
-    along = second.shape[1]
+
+
+def outputs_kernel(
+    ranks, part, head,
+    total_ref, squares_ref, pairs_ref, rest_ref, vec_ref,
+    wq1_ref, wk1_ref, wv1_ref, wo1_ref, wq2_ref, wk2_ref, wv2_ref, wo2_ref, w2_ref,
+    bq1_ref, bv1_ref, bo1_ref, g1_ref, s1_ref, bq2_ref, bv2_ref, bo2_ref, g2_ref, s2_ref, b1_ref, b2_ref, g3_ref, s3_ref,
+):
+    rank = lax.axis_index(TENSOR)
+    height = vec_ref.shape[1]
+
+    def line(n):
+        return vec_ref[n // height, n % height : n % height + 1, :]
+
+    def whole(row):
+        return row.reshape(row.shape[1])
+
+    def rank_part(row):
+        found = row[:, :part]
+        for other in range(1, ranks):
+            found = jnp.where(rank == other, row[:, other * part : (other + 1) * part], found)
+        return whole(found)
+
+    for ref, n in ((g3_ref, 0), (s3_ref, 1), (b2_ref, 2), (g2_ref, 3), (s2_ref, 4), (bo2_ref, 5)):
+        ref[...] = whole(line(n))
+    hidden = line(6)
+    for other in range(1, ranks):
+        hidden = jnp.where(rank == other, line(6 + other), hidden)
+    b1_ref[...] = whole(hidden)
+    for ref, n in ((g1_ref, 0), (s1_ref, 1), (bo1_ref, 2)):
+        ref[...] = whole(line(6 + ranks + n))
+    bq2_ref[...] = rank_part(line(9 + ranks))
+    bv2_ref[...] = rank_part(line(10 + ranks))
+    squares = squares_ref[...]
+    wq2_ref[...] = squares[:, :part] * SCALE
+    wo1_ref[...] = squares[:, part:].T
+    pairs = pairs_ref[...]
+    for n, ref in enumerate((wk2_ref, wv2_ref)):
+        ref[...] = jnp.concatenate(
+            [pairs[:, (2 * k + n) * head : (2 * k + n + 1) * head] for k in range(3)], axis=1
+        )
+    span = w2_ref.shape[1]
+    w2_ref[...] = rest_ref[:, :span]
+    wo2_ref[...] = rest_ref[:, span : span + part].T
+    total = total_ref[...]
+    rows = wq1_ref.shape[0]
+    wq1_ref[...] = total[:rows, :part] * SCALE
+    wk1_ref[...] = total[:rows, part : 2 * part]
+    wv1_ref[...] = total[:rows, 2 * part :]
+    bq1_ref[...] = whole(total[rows : rows + 1, :part] * SCALE)
+    bv1_ref[...] = whole(total[rows : rows + 1, 2 * part :])
+
+
+def outputs(head, width, total, squares, pairs, rest, vectors):
+    ranks = lax.axis_size(TENSOR)
+    few, part, full = squares.shape[0], 3 * head, jnp.float32
+    square, turned = ((few, part), full), ((part, few), full)
+    long, short = ((width,), full), ((part,), full)
     return call_kernel(
-        functools.partial(last_kernel, cores, depth, ranks, per_core),
-        "last_rows",
-        [
-            ((per_core, cores, rows, width), low),
-            ((per_core, 2 * cores * fold, side // 2), low),
-            ((high, wide), full),
-            (vectors.shape, full),
-            ((along, columns), full),
-            ((along, columns), full),
-        ],
-        [dqkv, dh1, early, enc_parts, self_parts, vectors, second, fourth],
-        scratch=[
-            pltpu.VMEM((rows, width), low),
-            pltpu.VMEM(enc_parts.shape[1:], low),
-            pltpu.VMEM(enc_parts.shape[1:], low),
-            pltpu.VMEM((per_core, cores, fold, side), low),
-            pltpu.VMEM(self_parts.shape, low),
-            pltpu.VMEM((depth, high, wide), low),
-            pltpu.VMEM((ranks, high, wide), low),
-            pltpu.VMEM(vectors.shape, full),
-            pltpu.VMEM(vectors.shape[1:], full),
-            pltpu.VMEM((ranks,) + vectors.shape[1:], full),
-            pltpu.VMEM(second.shape, low),
-            pltpu.VMEM(fourth.shape, low),
-            dma((2,)),
-        ]
-        + send_scratch(places)
-        + send_scratch(places)
-        + [dma((ranks - 1,)) for _ in range(4)]
-        + send_scratch(places)
-        + [dma((2, depth - 1)), dma((2, depth - 1))]
-        + deal_scratch(cores, ranks, per_core)
-        + deal_scratch(cores, ranks, per_core),
-        collective_id=7,
-        us=30,
+        functools.partial(outputs_kernel, ranks, part, head),
+        "outputs",
+        [square, square, square, turned, square, square, square, turned, ((few, width), full)]
+        + [short, short, long, long, long, short, short, long, long, long, long, long, long, long],
+        [total, squares, pairs, rest, vectors],
+        us=2,
     )
 
 
@@ -1420,14 +1758,23 @@
     zero = jnp.zeros((head, HALF), low)
     for block in range(blocks):
         g = g_ref[block]
-        shared = jnp.where(
-            core == 0,
-            jnp.concatenate([g[:, FULL:WIDE], zero], axis=1),
-            jnp.concatenate([zero, g[:, FULL:WIDE]], axis=1),
-        )
+
+        def own_half(first):
+            part = g[:, first : first + HALF]
+            return jnp.where(
+                core == 0, jnp.concatenate([part, zero], axis=1), jnp.concatenate([zero, part], axis=1)
+            )
+
+        whole = WIDE + 2 * FULL
         flat = jnp.concatenate(
-            [g[:, :FULL], shared]
-            + [g[:, WIDE + n * FULL : WIDE + (n + 1) * FULL] for n in (0, 2, 1, 3)],
+            [
+                g[:, :FULL],
+                own_half(FULL),
+                g[:, WIDE : WIDE + FULL],
+                own_half(whole),
+                g[:, WIDE + FULL : whole],
+                own_half(whole + HALF),
+            ],
             axis=0,
         )
         total = total + dot_nt(x_ref[block].T, flat)
@@ -1496,216 +1843,6 @@
     )
     total = jnp.sum(total, axis=0, keepdims=True)
     return (narrow(out) / total).astype(low), top + jnp.log(total)
-
-
-def self_kernel(
-    cores, depth, ranks,
-    x_ref, w_ref, b_ref, wo1_ref, wq2_ref, wo2_ref,
-    q_ref, k_ref, kt_ref, v_ref, vt_ref, o_ref, lse_ref, oall_ref, wall_ref,
-    group_ref, s_ref, load_sem, group_sem, osend, orecv, *wsems
-):
-    core, seq, rank = here()
-    low = jnp.bfloat16
-    blocks = cores * depth
-    head = q_ref.shape[1]
-    high = wo1_ref.shape[0]
-    lanes = wo1_ref.shape[1] // cores
-
-    def load(n, ref, half):
-        return pltpu.make_async_copy(
-            ref.at[:, pl.ds(half * lanes, lanes)],
-            wall_ref.at[half, rank, pl.ds(n * high, high), :],
-            load_sem.at[n, half],
-        )
-
-    loads = [load(n, ref, half) for n, ref in enumerate((wo1_ref, wq2_ref, wo2_ref)) for half in range(cores)]
-    groups = [pltpu.make_async_copy(w_ref.at[half, seq], group_ref.at[half, 0], group_sem.at[half]) for half in range(cores)]
-    for copy in groups + loads:
-        copy.start()
-    mine, places = column_places(cores, depth)
-    gather = PlaneGather(wall_ref, *wsems)
-    peers = [column_peer(place, cores, rank) for place in places] + gather.peers
-    greet(peers)
-
-    for copy in groups + loads:
-        copy.wait()
-    pl.semaphore_wait(pltpu.get_barrier_semaphore(), len(peers))
-    gather.start()
-
-    w = jnp.concatenate(
-        [head_rows(group_ref, 0, n, which, head) for n in range(3) for which in (2 * core, 1)], axis=0
-    )
-    bias = b_ref[...]
-
-    def project(block, carry):
-        lanes = pl.ds(pl.multiple_of(block * FULL, FULL), FULL)
-        flat = dot_nt(w, x_ref[block])
-        q = ((flat[: 2 * head] + bias[: 2 * head]) * SCALE).astype(low)
-        shared = jnp.where(core == 0, q[head:, :HALF], q[head:, HALF:])
-        q_ref[block] = jnp.concatenate([q[:head], shared], axis=1)
-        k = flat[2 * head : 4 * head].astype(low)
-        v = (flat[4 * head :] + bias[2 * head :]).astype(low)
-        kt_ref[:, lanes] = k
-        vt_ref[:, lanes] = v
-        k_ref[lanes, :] = k.T
-        v_ref[lanes, :] = v.T
-        return carry
-
-    lax.fori_loop(0, blocks, project, 0)
-
-    back = ColumnSend(cores, depth, o_ref, oall_ref, osend, orecv)
-
-    def attend(block):
-        out, lse = attend_block(block, True, core, blocks * FULL, q_ref[block], k_ref, vt_ref, s_ref)
-        o_ref[block] = out
-        lse_ref[block] = lse
-        return out
-
-    def step(n, carry):
-        attend(lax.rem(mine + 1 + n, blocks))
-        back.copy(n).start()
-        return carry
-
-    lax.fori_loop(0, blocks - 1, step, 0)
-    gather.forward()
-    oall_ref[mine] = attend(mine)
-    back.finish()
-    gather.finish()
-
-
-def attend_self(x_all, w_all, bias, head, wo1, wq2, wo2):
-    cores, depth, ranks = lax.axis_size(ITEM), lax.axis_size(SEQ), lax.axis_size(TENSOR)
-    places = cores * depth
-    rows = places * FULL
-    low = jnp.bfloat16
-    dma = pltpu.SemaphoreType.DMA
-    _, _, high, lanes = w_all.shape
-    return call_kernel(
-        functools.partial(self_kernel, cores, depth, ranks),
-        "attend_self",
-        [
-            ((places, head, WIDE), low),
-            ((rows, 2 * head), low),
-            ((2 * head, rows), low),
-            ((rows, 2 * head), low),
-            ((2 * head, rows), low),
-            ((places, head, WIDE), low),
-            ((places, 1, WIDE), jnp.float32),
-            ((places, head, WIDE), low),
-            ((cores, ranks, 3 * wo1.shape[0], lanes), low),
-        ],
-        [x_all, w_all, bias, wo1, wq2, wo2],
-        scratch=[
-            pltpu.VMEM((cores, 1, high, lanes), low),
-            pltpu.VMEM((rows, WIDE), jnp.float32),
-            dma((3, cores)),
-            dma((cores,)),
-        ]
-        + send_scratch(places)
-        + gather_scratch(),
-        collective_id=2,
-        in_spaces=[pltpu.VMEM, pl.ANY, pltpu.VMEM, pl.ANY, pl.ANY, pl.ANY],
-        us=30,
-    )
-
-
-def cross_kernel(
-    cores, depth, part,
-    o_ref, x_ref, w_ref, bo_ref, gain_ref, shift_ref, bq_ref, kv_ref,
-    h_ref, y_ref, q_ref, k_ref, kt_ref, v_ref, parts_ref, lse_ref, oall_ref,
-    qsrc_ref, half_ref, other_ref, vt_ref, s_ref, swap_sem, qsend, qrecv, osend, orecv,
-):
-    core, seq, rank = here()
-    low = jnp.bfloat16
-    count = cores * depth
-    mine, places = column_places(cores, depth)
-    peers = [column_peer(place, cores, rank) for place in places]
-    greet(peers)
-    slots, head = k_ref.shape[0], q_ref.shape[1]
-    half_ref[...] = kv_ref[:, slots:]
-
-    o1 = assembled(o_ref, depth).T
-    h1 = x_ref[...].astype(jnp.float32) + dot_nn(o1, late_square(w_ref, 0, part)) + bo_ref[...]
-    z, _ = centred_rows(h1)
-    y1 = (z * gain_ref[...] + shift_ref[...]).astype(low)
-    h_ref[...] = h1
-    y_ref[...] = y1
-    q2t = ((dot_nt(late_square(w_ref, 1, part), y1) + bq_ref[...]) * SCALE).astype(low)
-    dispersed(q2t, qsrc_ref, depth)
-
-    pl.semaphore_wait(pltpu.get_barrier_semaphore(), len(peers))
-    ask = ColumnSend(cores, depth, qsrc_ref, q_ref, qsend, qrecv)
-    swap = remote_copy(half_ref, other_ref, swap_sem.at[0], swap_sem.at[1], (1 - core, seq, rank))
-    swap.start()
-    for step in range(count - 1):
-        ask.copy(step).start()
-    q_ref[mine] = qsrc_ref[mine]
-    swap.wait()
-    whole = kv_ref[:, :slots]
-    half, other = half_ref[...], other_ref[...]
-    shared = jnp.concatenate([jnp.where(core == 0, half, other), jnp.where(core == 0, other, half)], axis=1)
-    kt = jnp.concatenate([whole[:head], shared[:head]], axis=0)
-    vt = jnp.concatenate([whole[head:], shared[head:]], axis=0)
-    kt_ref[...] = kt
-    vt_ref[...] = vt
-    k_ref[...] = kt.T
-    v_ref[...] = vt.T
-
-    back = ColumnSend(cores, depth, parts_ref, oall_ref, osend, orecv)
-
-    def attend(block):
-        out, lse = attend_block(block, False, core, slots, q_ref[block], k_ref, vt_ref, s_ref)
-        parts_ref[block] = out
-        lse_ref[block] = lse
-        return out
-
-    oall_ref[mine] = attend(mine)
-
-    def step(n, carry):
-        ask.wait_from(n)
-        attend(lax.rem(mine + count - 1 - n, count))
-        back.copy(count - 2 - n).start()
-        return carry
-
-    lax.fori_loop(0, count - 1, step, 0)
-    ask.finish_sends()
-    back.finish()
-
-
-def attend_cross(o1, x_mine, squares, bo, gain, shift, bq, kv_mine, slots):
-    cores, depth = lax.axis_size(ITEM), lax.axis_size(SEQ)
-    places, head, _ = o1.shape
-    rows, width = x_mine.shape
-    low, full = jnp.bfloat16, jnp.float32
-    parts = (places, head, WIDE)
-    return call_kernel(
-        functools.partial(cross_kernel, cores, depth, 3 * head),
-        "attend_cross",
-        [
-            ((rows, width), full),
-            ((rows, width), low),
-            (parts, low),
-            ((slots, 2 * head), low),
-            ((2 * head, slots), low),
-            ((slots, 2 * head), low),
-            (parts, low),
-            ((places, 1, WIDE), full),
-            (parts, low),
-        ],
-        [o1, x_mine, squares, bo, gain, shift, bq, kv_mine],
-        scratch=[
-            pltpu.VMEM(parts, low),
-            pltpu.VMEM((2 * head, slots // 2), low),
-            pltpu.VMEM((2 * head, slots // 2), low),
-            pltpu.VMEM((2 * head, slots), low),
-            pltpu.VMEM((slots, WIDE), full),
-            pltpu.SemaphoreType.DMA((2,)),
-        ]
-        + send_scratch(places)
-        + send_scratch(places),
-        collective_id=3,
-        us=28,
-    )
 
 
 def back_block(block, causal, core, slots, q, do, o, lse, k_ref, kt_ref, v_ref, whole_ref, shared_ref):
@@ -1741,15 +1878,16 @@
 
 def cross_back_kernel(
     cores, depth,
-    q_ref, k_ref, kt_ref, v_ref, o_ref, lse_ref, do_ref,
-    dqall_ref, dkv_ref,
-    dq_ref, whole_ref, shared_ref, give_ref, got_ref, swap_sem, send_sem, recv_sem,
+    q_ref, k_ref, kt_ref, v_ref, o_ref, lse_ref, do_ref, grad_ref,
+    dqall_ref, dkv_ref, bv_ref, sum_ref,
+    dq_ref, whole_ref, shared_ref, give_ref, got_ref, swap_sem, send_sem, recv_sem, *sum_refs
 ):
     core, seq, rank = here()
     low = jnp.bfloat16
     count = cores * depth
     mine, places = column_places(cores, depth)
-    peers = [column_peer(place, cores, rank) for place in places]
+    hidden = PlaneSum(grad_ref.shape[0], grad_ref, 0, *sum_refs)
+    peers = [column_peer(place, cores, rank) for place in places] + hidden.peers
     greet(peers)
     slots = k_ref.shape[0]
     whole_ref[...] = jnp.zeros_like(whole_ref)
@@ -1762,8 +1900,9 @@
             k_ref, kt_ref, v_ref, whole_ref, shared_ref,
         )
 
+    pl.semaphore_wait(pltpu.get_barrier_semaphore(), len(peers))
+    hidden.start()
     dq_ref[places[0]] = go(places[0])
-    pl.semaphore_wait(pltpu.get_barrier_semaphore(), len(peers))
     back.copy(0).start()
 
     def step(n, carry):
@@ -1782,11 +1921,23 @@
     swap.wait()
     kept = shared_ref[pl.ds(pl.multiple_of(core * half, half), half), :]
     dkv_ref[slots:] = (kept + got_ref[...].astype(jnp.float32)).astype(low)
+    head = q_ref.shape[1]
+    first = jnp.sum(dkv_ref[:slots].astype(jnp.float32), axis=0, keepdims=True)[:, head:]
+    second = jnp.sum(dkv_ref[slots:].astype(jnp.float32), axis=0, keepdims=True)[:, head:]
+    bv_ref[...] = jnp.concatenate(
+        [
+            jnp.where(n == 3 * seq + 2 * core, first, jnp.where(n == 3 * seq + 1, second, 0.0))
+            for n in range(3 * depth)
+        ],
+        axis=1,
+    )
     back.finish()
-
-
-def attend_cross_back(q, k, kt, v, o, lse, do):
-    cores, depth = lax.axis_size(ITEM), lax.axis_size(SEQ)
+    sum_ref[...] = hidden.finish().astype(low)
+
+
+def attend_cross_back(q, k, kt, v, o, lse, do, grad, columns):
+    cores, depth, ranks = lax.axis_size(ITEM), lax.axis_size(SEQ), lax.axis_size(TENSOR)
+    lanes = grad.shape[1]
     places, head, _ = q.shape
     slots = k.shape[0]
     low = jnp.bfloat16
@@ -1794,8 +1945,13 @@
     return call_kernel(
         functools.partial(cross_back_kernel, cores, depth),
         "back_cross",
-        [(q.shape, low), ((slots + slots // 2, 2 * head), low)],
-        [q, k, kt, v, o, lse, do],
+        [
+            (q.shape, low),
+            ((slots + slots // 2, 2 * head), low),
+            ((1, 3 * depth * head), jnp.float32),
+            ((lanes, columns), low),
+        ],
+        [q, k, kt, v, o, lse, do, grad],
         scratch=[
             pltpu.VMEM(q.shape, low),
             sums,
@@ -1804,51 +1960,86 @@
             pltpu.VMEM((slots // 2, 2 * head), low),
             pltpu.SemaphoreType.DMA((2,)),
         ]
-        + send_scratch(places),
+        + send_scratch(places)
+        + sum_scratch(ranks, lanes, columns, low),
         collective_id=5,
+        in_spaces=[pltpu.VMEM] * 7 + [pl.ANY],
         us=24,
     )
 
 
 def self_back_kernel(
     cores, depth, ranks, part,
-    dq2_ref, dh2_ref, h1_ref, y1_ref, oin_ref, w_ref, gain_ref,
-    q_ref, k_ref, kt_ref, v_ref, o_ref, lse_ref, dkv_ref, enc_ref, early_ref, idx_ref, x_ref,
-    dh1_ref, vec_ref, gall_ref, self_ref, encp_ref, second_ref, fourth_ref,
-    dosrc_ref, do_ref, g_ref, whole_ref, shared_ref, dkvall_ref, grad2_ref, grad4_ref,
-    dosend, dorecv, gsend, grecv, kvsend, kvrecv, *reduce_refs
+    dq2_ref, dh2_ref, h1_ref, y1_ref, oin_ref, w_in, gain_ref,
+    q_ref, k_ref, kt_ref, v_ref, o_ref, lse_ref, dkv_ref, idx_ref, vmid_ref, bv_ref, red1_ref,
+    enc_in, wkv_in, ws_in, x_in, grad_ref,
+    in_ref, encg_ref, total_ref, squares_ref, pairs_ref, rest_ref, w1_ref, vout_ref,
+    w_ref, enc_ref, wkv_ref, ws_ref, x_ref, encp_ref, got_ref, sum_ref, encall_ref,
+    dosrc_ref, do_ref, g_ref, gall_ref, whole_ref, shared_ref, dkvall_ref, grad2_ref,
+    dh1_ref, dx_ref, self_ref, column_ref, group_ref, plane_ref,
+    red2_ref, red4_ref, red5_ref, r1_ref, r2_ref, r4_ref, r5_ref,
+    give_ref, gots_ref, shsend, shrecv, load_sem, swap_sem, dosend, dorecv, gsend, grecv, kvsend, kvrecv, csend, crecv, psend, precv, zsend, zrecv, *more
 ):
     core, seq, rank = here()
     low = jnp.bfloat16
     count = cores * depth
     head = part // 3
+    per_core = encg_ref.shape[0]
     mine, places = column_places(cores, depth)
-    first = PlaneReduce(ranks, grad2_ref, *reduce_refs[:6])
-    second = PlaneReduce(ranks, grad4_ref, *reduce_refs[6:])
+    first = PlaneReduce(ranks, grad2_ref, *more[:6])
+    second = PlaneReduce(ranks, grad2_ref, more[6], more[1], *more[7:11])
+    deal_enc = Deal(cores, ranks, per_core, lambda target: sum_ref.at[target], encall_ref, *more[11:14])
+    deal_in = Deal(cores, ranks, per_core, lambda target: dx_ref, in_ref, *more[14:17])
+    hidden = PlaneSum(ranks, grad_ref, grad_ref.shape[2] - red5_ref.shape[2], *more[17:21])
+    vectors = VectorSum(cores, depth, ranks, vout_ref, *more[21:])
+    along = [
+        SeqSum(depth, src, dst, zsend.at[n], zrecv.at[n])
+        for n, (src, dst) in enumerate(
+            ((red1_ref, r1_ref), (red2_ref, r2_ref), (red4_ref, r4_ref), (red5_ref, r5_ref))
+        )
+    ]
+    loads = [
+        pltpu.make_async_copy(src, dst, load_sem.at[n])
+        for n, (src, dst) in enumerate(((wkv_in, wkv_ref), (enc_in, enc_ref), (x_in, x_ref), (ws_in, ws_ref)))
+    ]
+    squares = [
+        pltpu.make_async_copy(
+            w_in.at[half, of, pl.ds(0, 2 * part), :], w_ref.at[half, of], load_sem.at[4 + half * ranks + of]
+        )
+        for half in range(cores)
+        for of in range(ranks)
+    ]
+    for load in squares + loads:
+        load.start()
     peers = [column_peer(place, cores, rank) for place in places] + first.peers
+    peers += [(1 - core, seq, peer[2]) for peer in first.peers]
     greet(peers)
     chain = Chain(depth, dkvall_ref, kvsend, kvrecv)
+    dkvall_ref[seq] = dkv_ref[...]
+    pl.semaphore_wait(pltpu.get_barrier_semaphore(), len(peers))
+    chain.step(0)
+    hidden.start()
 
     width = y1_ref.shape[1]
     lanes = width // cores
     dq2t = assembled(dq2_ref, depth)
+    for load in squares:
+        load.wait()
     dy1 = dh2_ref[...] + dot_nn(dq2t.T, late_square(w_ref, 1, part)) * SCALE
     z1, spread1 = centred_rows(h1_ref[...])
-    dh1, gg1, gs1 = norm_back(z1, spread1, dy1, gain_ref[...])
+    dh1, gg1, gs1 = norm_back(z1, spread1, dy1, as_row(gain_ref))
     e1 = dh1.astype(low)
     dispersed(dot_nt(late_square(w_ref, 0, part), e1).astype(low), dosrc_ref, depth)
-    pl.semaphore_wait(pltpu.get_barrier_semaphore(), len(peers))
     ask = ColumnSend(cores, depth, dosrc_ref, do_ref, dosend, dorecv)
     for step in range(count - 1):
         ask.copy(step).start()
     do_ref[mine] = dosrc_ref[mine]
-    dkvall_ref[seq] = dkv_ref[...]
     dh1_ref[...] = dh1
-    vec_ref[0:1] = gg1
-    vec_ref[1:2] = gs1
-    vec_ref[2:3] = jnp.sum(e1.astype(jnp.float32), axis=0, keepdims=True)
     ones = jnp.ones((8, FULL), low)
-    vec_ref[3:4] = dot_nt(ones, dq2t)[0:1] * SCALE
+    given = [vmid_ref[n : n + 1] for n in range(vmid_ref.shape[0])]
+    given += [gg1, gs1, jnp.sum(e1.astype(jnp.float32), axis=0, keepdims=True), dot_nt(ones, dq2t)[0:1] * SCALE]
+    given += [bv_ref[...], jnp.zeros_like(gg1)]
+    vectors.start(given)
     o1t = assembled(oin_ref, depth)
     both = jnp.concatenate([y1_ref[...].T, e1.T], axis=1)
     blank = jnp.zeros((part, FULL), low)
@@ -1869,18 +2060,30 @@
     shared_ref[...] = jnp.zeros_like(shared_ref)
     for step in range(count - 1):
         ask.wait_from(step)
-    chain.step(0)
-
+    chain.step(1)
     back = ColumnSend(cores, depth, g_ref, gall_ref, gsend, grecv)
+
+    def swap_shared(block):
+        return remote_copy(
+            give_ref.at[block], gots_ref.at[block], shsend.at[block], shrecv.at[block], (1 - core, seq, rank)
+        )
 
     def go(block):
         g_ref[block, :, :WIDE] = back_block(
             block, True, core, count * FULL, q_ref[block], do_ref[block], o_ref[block], lse_ref[block],
             k_ref, kt_ref, v_ref, whole_ref, shared_ref,
         )
-        rows = pl.ds(pl.multiple_of(block * FULL, FULL), FULL)
-        whole = whole_ref[rows, :].T.astype(low)
-        shared = shared_ref[rows, :].T.astype(low)
+        start = pl.multiple_of(block * FULL, FULL)
+        there = pl.ds(pl.multiple_of(start + (1 - core) * HALF, HALF), HALF)
+        give_ref[block] = shared_ref[there, :].astype(low)
+        swap_shared(block).start()
+
+    def send_back(block):
+        start = pl.multiple_of(block * FULL, FULL)
+        whole = whole_ref[pl.ds(start, FULL), :].T.astype(low)
+        here_rows = pl.ds(pl.multiple_of(start + core * HALF, HALF), HALF)
+        swap_shared(block).wait_recv()
+        shared = (shared_ref[here_rows, :] + gots_ref[block].astype(jnp.float32)).T.astype(low)
         g_ref[block, :, WIDE:] = jnp.concatenate([whole[:head], whole[head:], shared[:head], shared[head:]], axis=1)
 
         @pl.when(block != mine)
@@ -1893,30 +2096,98 @@
 
     def step(n, carry):
         go(count - 1 - n)
+        send_back(count - n)
         return carry
 
-    lax.fori_loop(0, 2, step, 0)
+    go(count - 1)
+    lax.fori_loop(1, 2, step, 0)
     first.middle()
-    chain.step(1)
+    chain.step(2)
+    vectors.second()
     lax.fori_loop(2, 4, step, 0)
-    for n in range(2, depth):
+    vectors.third()
+    along[0].start()
+    for load in loads:
+        load.wait()
+    for n in range(3, depth):
         chain.step(n)
-    lax.fori_loop(4, count, step, 0)
-
-    encoder_back(ranks, head, enc_ref, early_ref, idx_ref, dkvall_ref, encp_ref, grad4_ref)
+
+    encoder_back(ranks, head, enc_ref, wkv_ref, idx_ref, dkvall_ref, encp_ref, grad2_ref)
+    swap = remote_copy(encp_ref.at[1 - core], got_ref, swap_sem.at[0], swap_sem.at[1], (1 - core, seq, rank))
+    swap.start()
     second.start()
+    red2_ref[...] = first.finish().astype(low).reshape(red2_ref.shape)
+    along[1].start()
+    lax.fori_loop(4, 5, step, 0)
+    swap.wait()
+    sum_ref[...] = (encp_ref[core].astype(jnp.float32) + got_ref[...].astype(jnp.float32)).astype(low)
+    deal_enc.start()
+    second.middle()
+    lax.fori_loop(5, count, step, 0)
+    send_back(0)
+
     self_grads(count, cores, count, x_ref, g_ref, self_ref)
-    second.middle()
-    second_ref[...] = first.finish().astype(low)
+    column = [
+        remote_copy(
+            self_ref.at[place], column_ref.at[mine], csend.at[step], crecv.at[step], column_peer(place, cores, rank)
+        )
+        for step, place in enumerate(places)
+    ]
+    for copy in column:
+        copy.start()
+
+    for step in range(count - 1):
+        back.wait_from(step)
+    dx_ref[...] = input_rows(depth, gall_ref, dh1_ref, ws_ref)
+    deal_in.start()
+
+    red5_ref[...] = hidden.finish().astype(low).reshape(red5_ref.shape)
+    along[3].start()
+    vectors.finish()
+
+    for copy in column:
+        copy.wait()
+    column_ref[mine] = self_ref[mine]
+    merge_heads(depth, head, column_ref, group_ref)
+    plane = [
+        remote_copy(group_ref.at[peer[2]], plane_ref.at[rank], psend.at[step], precv.at[step], peer)
+        for step, peer in enumerate(first.peers)
+    ]
+    for copy in plane:
+        copy.start()
+    red4_ref[...] = second.finish().astype(low).reshape(red4_ref.shape)
+    along[2].start()
+
+    deal_enc.finish()
+    fold = encall_ref.shape[2]
+    for item in range(per_core):
+        for half in range(cores):
+            for side in range(2):
+                rows = slice((2 * half + side) * fold, (2 * half + side + 1) * fold)
+                encg_ref[item, rows, :] = encall_ref[item, half, :, side * part : (side + 1) * part]
+    w1_ref[...] = along[0].finish()
+    squares_ref[...] = along[1].finish()
+    for copy in plane:
+        copy.wait()
+    total = group_ref[rank].astype(jnp.float32)
+    for step in range(1, ranks):
+        total = total + plane_ref[lax.rem(rank + step, ranks)].astype(jnp.float32)
+    total_ref[...] = total
+    rest_ref[...] = along[3].finish()
     chain.finish()
     ask.finish_sends()
-    back.finish()
-    fourth_ref[...] = second.finish().astype(low)
-
-
-def attend_self_back(*args):
+    back.finish_sends()
+    for block in range(count):
+        swap_shared(block).wait_send()
+    deal_in.finish()
+    pairs_ref[...] = along[2].finish()
+
+
+def attend_self_back(per_core, *args):
     cores, depth, ranks = lax.axis_size(ITEM), lax.axis_size(SEQ), lax.axis_size(TENSOR)
-    dq2, dh2, h1, y1, o1, squares, gain, q, k, kt, v, o, lse, dkv, enc, early, index, x_all = args
+    (
+        dq2, dh2, h1, y1, o1, squares, gain, q, k, kt, v, o, lse, dkv, index, vec_mid, bv, red1, enc, wkv, ws, x_all, grad
+    ) = args
     places, head, _ = q.shape
     rows, width = y1.shape
     low, full = jnp.bfloat16, jnp.float32
@@ -1924,38 +2195,75 @@
     all_rows = places * rows
     dma = pltpu.SemaphoreType.DMA
     grads = (cores, ranks, lanes, 2 * part)
-    message = (places, head, WIDE + 4 * FULL)
+    message = (places, head, WIDE + 2 * FULL + 2 * HALF)
     sums = pltpu.VMEM((all_rows, 2 * head), full)
+    fold = enc.shape[0] // (2 * cores)
+    rest = grad.shape[2] - width
+    vec_shape = (places, (vec_mid.shape[0] + 6) // places, width)
+    few = width // places
+    high = few + 16
+    red1 = red1.reshape(depth, few, width)
+    along = [pltpu.VMEM((depth, few, columns), low) for columns in (2 * part, 2 * part, rest)]
+    args = (*args[:17], red1, *args[18:])
     return call_kernel(
         functools.partial(self_back_kernel, cores, depth, ranks, part),
         "back_self",
         [
-            ((rows, width), full),
-            ((4, width), full),
-            (message, low),
-            ((places, width // places + 16, 6 * head), low),
-            ((cores, ranks, enc.shape[0] // (2 * cores), 2 * part), low),
-            ((lanes, 2 * part), low),
-            ((lanes, 2 * part), low),
+            ((per_core, cores, rows, width), low),
+            ((per_core, enc.shape[0], part), low),
+            ((high, 3 * part), full),
+            ((few, 2 * part), full),
+            ((few, 2 * part), full),
+            ((few, rest), full),
+            ((few, width), full),
+            (vec_shape, full),
         ],
         list(args),
         scratch=[
+            pltpu.VMEM((cores, ranks, 2 * part, lanes), low),
+            pltpu.VMEM(enc.shape, low),
+            pltpu.VMEM(wkv.shape, low),
+            pltpu.VMEM(ws.shape, low),
+            pltpu.VMEM(x_all.shape, low),
+            pltpu.VMEM((cores, ranks, fold, 2 * part), low),
+            pltpu.VMEM((ranks, fold, 2 * part), low),
+            pltpu.VMEM((ranks, fold, 2 * part), low),
+            pltpu.VMEM((per_core, cores, fold, 2 * part), low),
             pltpu.VMEM(q.shape, low),
             pltpu.VMEM(q.shape, low),
+            pltpu.VMEM(message, low),
             pltpu.VMEM(message, low),
             sums,
             sums,
             pltpu.VMEM((depth,) + dkv.shape, low),
             pltpu.VMEM(grads, low),
-            pltpu.VMEM(grads, low),
+            pltpu.VMEM((rows, width), full),
+            pltpu.VMEM((rows, width), low),
+            pltpu.VMEM((places, high, 6 * head), low),
+            pltpu.VMEM((places, high, 6 * head), low),
+            pltpu.VMEM((depth, high, 3 * part), low),
+            pltpu.VMEM((ranks, high, 3 * part), low),
         ]
+        + along
+        + [pltpu.VMEM(red1.shape, low)]
+        + along
+        + [pltpu.VMEM((places, HALF, 2 * head), low), pltpu.VMEM((places, HALF, 2 * head), low)]
+        + [dma((places,)), dma((places,)), dma((4 + cores * ranks,)), dma((2,))]
         + send_scratch(places)
         + send_scratch(places)
         + [dma((2, depth)), dma((depth,))]
+        + send_scratch(places)
+        + send_scratch(ranks)
+        + [dma((4, depth - 1)), dma((4, depth - 1))]
         + reduce_scratch(ranks, lanes, 2 * part, low)
-        + reduce_scratch(ranks, lanes, 2 * part, low),
+        + reduce_scratch(ranks, lanes, 2 * part, low)[1:]
+        + deal_scratch(cores, ranks, per_core)
+        + deal_scratch(cores, ranks, per_core)
+        + sum_scratch(ranks, lanes, rest, low)
+        + vector_scratch(vec_shape, places, ranks),
         collective_id=6,
-        us=60,
+        in_spaces=[pltpu.VMEM] * 5 + [pl.ANY] + [pltpu.VMEM] * 12 + [pl.ANY] * 5,
+        us=100,
     )
 
 
@@ -2000,113 +2308,51 @@
     lanes = width // cores
     hidden = ffn_w1.shape[1]
 
-    def row(vector):
-        return vector.reshape(1, width)
-
-    vectors = jnp.concatenate([self_bq, self_bv, cross_bq, cross_bv, ffn_b1]).reshape(-1, 128)
-    x_all, grad_mine, enc, index, vectors, early = prologue(
-        dec_input, out_grad, encoder_states, retrieved, vectors, [self_wq.T, self_wk.T, self_wv.T, cross_wk.T, cross_wv.T]
-    )
-    ffn = jnp.concatenate(
-        [lax.dynamic_slice_in_dim(w, core * lanes, lanes, axis=1) for w in (ffn_w1, ffn_w2)], axis=0
-    )
-    ffn = lax.optimization_barrier((ffn, index))[0]
-    ffn = lax.all_gather(ffn, TENSOR, axis=0, tiled=False)
-    x_mine = x_all[seq, core]
+    short = jnp.stack([self_bq, self_bv, cross_bq, cross_bv])
+    vectors = jnp.concatenate([jnp.pad(short, ((0, 0), (0, hidden - part))), ffn_b1.reshape(1, hidden)], axis=0)
+    vectors = jnp.pad(vectors, ((0, 3), (0, 0)))
+    (
+        x_all, enc, weights_kv, weights_self, weights_square, weights_in, weights_out,
+        grad_mine, index, vectors, q1, k1, k1t, v1, o1_parts, lse1, o1,
+        h1, y1, q2, k2, k2t, v2, o2_parts, lse2, o2,
+    ) = front(
+        dec_input, out_grad, encoder_states, retrieved, vectors,
+        [cross_wk.T, cross_wv.T], [self_wq.T, self_wk.T, self_wv.T], [self_wo, cross_wq.T, cross_wo],
+        ffn_w1, ffn_w2, [self_bo, norm1_gain, norm1_bias],
+    )
     x_all = x_all.reshape(places, FULL, width)
-    vectors = vectors.reshape(ranks, -1)
-    all_bq1, all_bv1, all_bq2, all_bv2 = [vectors[:, n * part : (n + 1) * part] for n in range(4)]
-    all_b1 = vectors[:, 4 * part :].reshape(ranks, 1, hidden)
-
-    by_head = all_bv2.reshape(ranks, 3, 1, head)
-    blank = jnp.zeros((ranks, 2, head), full)
-    two = jnp.concatenate([lax.dynamic_slice_in_dim(by_head, 2 * core, 1, axis=1), by_head[:, 1:2]], axis=1)
-    bias_kv = jnp.concatenate([blank[:, :, None], two], axis=2).reshape(ranks, 4 * head, 1)
-    pieces = retrieve(enc, early, bias_kv, index)
-    kv_mine = lax.psum_scatter(pieces, SEQ, scatter_dimension=0, tiled=False)
-
-    def two_heads(rows):
-        rows = lax.dynamic_index_in_dim(rows, seq, 0, keepdims=False).reshape(3, head)
-        return jnp.concatenate([lax.dynamic_slice_in_dim(rows, 2 * core, 1, axis=0), rows[1:2]], axis=0)
-
-    bias = jnp.concatenate([two_heads(all_bq1), two_heads(all_bv1)], axis=0).reshape(4 * head, 1)
-    q1, k1, k1t, v1, v1t, o1_parts, lse1, o1, squares = attend_self(
-        x_all, early, bias, head, self_wo, cross_wq.T, cross_wo
-    )
-
-    h1, y1, q2, k2, k2t, v2, o2_parts, lse2, o2 = attend_cross(
-        o1, x_mine, squares, row(self_bo), row(norm1_gain), row(norm1_bias), all_bq2.reshape(width, 1), kv_mine, slots
-    )
-    ffn = lax.optimization_barrier((ffn, o1))[0]
-    ffn = lax.all_gather(ffn, ITEM, axis=0, tiled=False)
     layer_out, do2, dh2, vec_mid, grad_mid = middle(
         per_core,
         o2,
         y1,
         grad_mine,
-        squares,
-        ffn,
+        weights_square,
+        weights_in,
+        weights_out,
         [
-            row(cross_bo),
-            row(norm2_gain),
-            row(norm2_bias),
-            all_b1,
-            row(ffn_b2),
-            row(norm3_gain),
-            row(norm3_bias),
+            cross_bo,
+            norm2_gain,
+            norm2_bias,
+            vectors,
+            ffn_b2,
+            norm3_gain,
+            norm3_bias,
         ],
     )
     layer_out = layer_out.reshape(per_core, cores * FULL, width)
-    first_sum = lax.psum_scatter(grad_mid, ITEM, scatter_dimension=0, tiled=False)
-    dq2, dkv2 = attend_cross_back(q2, k2, k2t, v2, o2_parts, lse2, do2)
-    dq2, first_sum = lax.optimization_barrier((dq2, first_sum))
-    first_sum = lax.psum_scatter(first_sum, TENSOR, scatter_dimension=0, tiled=False)
-    dh1, vec_second, dqkv, self_parts, enc_parts, second_sum, fourth_sum = attend_self_back(
-        dq2, dh2, h1, y1, o1, squares, row(norm1_gain),
-        q1, k1, k1t, v1, o1_parts, lse1, dkv2, enc, early, index, x_all,
-    )
-    first_sum = lax.psum_scatter(first_sum, SEQ, scatter_dimension=0, tiled=True)
-
-    dv_heads = [jnp.sum(rows[:, head:].astype(full), axis=0) for rows in (dkv2[:slots], dkv2[slots:])]
-    slot_of = jnp.arange(3 * depth)[:, None]
-    bv_rows = jnp.where(slot_of == 3 * seq + 2 * core, dv_heads[0], 0.0) + jnp.where(
-        slot_of == 3 * seq + 1, dv_heads[1], 0.0
-    )
-    vectors = jnp.concatenate([vec_mid, vec_second, bv_rows.reshape(1, width)], axis=0)
-    count = vectors.shape[0]
-    piece = 16 * 128
-    vectors = jnp.pad(vectors.reshape(-1), (0, places * piece - count * width)).reshape(places, 16, 128)
-    input_grad, encoder_grad, third_sum, summed, second_sum, fourth_sum = last_rows(
-        per_core, dqkv, dh1, early, enc_parts, self_parts, vectors, second_sum, fourth_sum
-    )
+    dq2, dkv2, bv, first_sum = attend_cross_back(q2, k2, k2t, v2, o2_parts, lse2, do2, grad_mid, hidden)
+    input_grad, encoder_grad, total, squares, pairs, rest, gffn_w1, vectors = attend_self_back(
+        per_core,
+        dq2, dh2, h1, y1, o1, weights_square, norm1_gain,
+        q1, k1, k1t, v1, o1_parts, lse1, dkv2, index, vec_mid, bv, first_sum, enc, weights_kv, weights_self, x_all, grad_mid,
+    )
+    (
+        gself_wq, gself_wk, gself_wv, gself_wo, gcross_wq, gcross_wk, gcross_wv, gcross_wo, gffn_w2,
+        gself_bq, gself_bv, gself_bo, gnorm1_gain, gnorm1_bias,
+        gcross_bq, gcross_bv, gcross_bo, gnorm2_gain, gnorm2_bias, gffn_b1, gffn_b2, gnorm3_gain, gnorm3_bias,
+    ) = outputs(head, width, total, squares, pairs, rest, vectors)
     input_grad = input_grad.reshape(per_core, cores * FULL, width)
-    summed = summed.reshape(-1)[: count * width].reshape(count, width)
-
-    rows = width // places
-    first_sum = first_sum.astype(full)
-    gself_wq = third_sum[:rows, :part] * SCALE
-    gself_wk = third_sum[:rows, part : 2 * part]
-    gself_wv = third_sum[:rows, 2 * part :]
-    gself_bq = third_sum[rows, :part] * SCALE
-    gself_bv = third_sum[rows, 2 * part :]
-    gffn_w1 = first_sum[:, :hidden]
-    gffn_w2 = first_sum[:, hidden : 2 * hidden].T
-    gcross_wo = first_sum[:, 2 * hidden : 2 * hidden + part].T
-    gcross_wq = second_sum[:, :part] * SCALE
-    gself_wo = second_sum[:, part:].T
-    grad_kv = fourth_sum.reshape(rows, 3, 2, head)
-    gcross_wk = grad_kv[:, :, 0].reshape(rows, part)
-    gcross_wv = grad_kv[:, :, 1].reshape(rows, part)
-
-    gnorm3_gain, gnorm3_bias, gffn_b2, gnorm2_gain, gnorm2_bias, gcross_bo = [summed[n] for n in range(6)]
-    gffn_b1 = lax.dynamic_index_in_dim(summed[6 : 6 + ranks], rank, 0, keepdims=False)
-    gnorm1_gain, gnorm1_bias, gself_bo = [summed[6 + ranks + n] for n in range(3)]
-
-    def rank_part(vector):
-        return lax.dynamic_slice_in_dim(vector, rank * part, part)
-
-    gcross_bq = rank_part(summed[9 + ranks])
-    gcross_bv = rank_part(summed[10 + ranks])
+    gffn_w2 = gffn_w2.T
     return (
         layer_out,
         input_grad,

time: 445 us -> 351 us (0.79)
  Pallas kernels: 372 us -> 335 us
  local copies, waits for them, and re-layouts: 29.7 us -> 8.17 us
  between operations: 15.8 us -> 0.96 us
  waiting for transfers between devices: 14.5 us -> 0 us
    pallas_call x8 -> x5, Pallas kernels: 372 us -> 335 us  [call_kernel(): pl.pallas_call(kernel, out_shape=[jax.ShapeDtypeStruct(s, d) for s, d in...]
    all_gather x2 -> x0, waiting for transfers between devices: 14.3 us -> none  [the longest x1 14.3 us: column_body(): ffn = lax.all_gather(ffn, TENSOR, axis=0, tiled=False)]
    reshape x17 -> x1, local copies, waits for them, and re-layouts: 9.19 us -> 0.69 us  [column_body(): ffn_b1.reshape(1, hidden)]
    unnamed x55 -> x11, local copies, waits for them, and re-layouts: 11.5 us -> 7.48 us
  transfers between devices with their start and end apart: 6 -> 0, of which waited for: 1 -> 0; matrix products, arithmetic and copies ran while one was open for 5% -> 0% of each run, Pallas kernels for 66% -> 0%
where the time goes in v2:
time: 351 us; the launch traced here: 345 us
  Pallas kernels  335 us (95%)
  local copies, waits for them, and re-layouts  8.17 us (2%)
    pallas_call x5, Pallas kernels, call_kernel(): pl.pallas_call(kernel, out_shape=[jax.ShapeDtypeStruct(s, d) for s, d in...  335 us
    unnamed x11, local copies, waits for them, and re-layouts  7.48 us

profile of v2, /device:TPU:0, one launch (start us, length us, event | category | flops | bytes accessed | tf_op | source)
XLA Modules:
  0.0 345.0 jit_solution(4177492839803067565)
XLA Ops:
  0.7 0.7 reshape.69
  1.4 0.7 select_maximum_fusion.1
  2.1 0.6 select_maximum_fusion.vec_ref
  2.7 1.4 copy.55.idx_ref
  4.1 120.9 %front.1 = (bf16[4,2,256,768]{3,2,1,0:T(8,128)(2,1)}, bf16[1152,768]{1,0:T(8,128)(2,1)}, bf16[2,4,384,384]{3,2,1,0:T(8,128)(2,1)}, bf16[2,4,576,384]{3,2,1,0:T(8...) custom-call(bf16[2,512,768]{2,1,0:T(8,128)(2,1)} %x_ref.1, ...), custom_call_target="tpu_custom_call" | custom-call | flops 89999998976 | bytes 270000000 | tf_op jit(solution)/shard_map/front/pallas_call | solution.py:419
  125.0 29.1 %middle.1 = (bf16[2,2,256,768]{3,2,1,0:T(8,128)(2,1)}, bf16[8,64,384]{2,1,0:T(8,128)(2,1)}, f32[256,768]{1,0:T(8,128)}, f32[10,768]{1,0:T(8,128)}, bf16[4,384,1792]{2,1,0:T(8,128)(2,1)}) custom-call(bf16[8,64,384]{2,1,0:T(8,128)(2,1)} %get-tuple-element.93.o_ref, bf16[256,768]{1,0:T(8,128)(2,1)} %get-tuple-element.94.y1_ref, ...), custom_call_target="tpu_custom_call" | custom-call | flops 22000001024 | bytes 66000000 | tf_op jit(solution)/shard_map/middle/pallas_call | solution.py:419
  154.1 33.2 %back_cross.1 = (bf16[8,64,384]{2,1,0:T(8,128)(2,1)}, bf16[1536,128]{1,0:T(8,128)(2,1)}, f32[1,768]{1,0:T(1,128)}, bf16[384,768]{1,0:T(8,128)(2,1)}) custom-call(bf16[8,64,384]{2,1,0:T(8,128)(2,1)} %get-tuple-element.101.q_ref, bf16[1024,128]{1,0:T(8,128)(2,1)} %get-tuple-element.102.k_ref, bf16[128,1024]{1,0:T(8,128)(2,1)} %get-tuple-element.103.kt_ref, ...), custom_call_target="tpu_custom_call" | custom-call | flops 24000000000 | bytes 72000000 | tf_op jit(solution)/shard_map/back_cross/pallas_call | solution.py:419
  187.3 148.8 %back_self.1 = (bf16[2,2,256,768]{3,2,1,0:T(8,128)(2,1)}, bf16[2,1152,192]{2,1,0:T(8,128)(2,1)}, f32[112,576]{1,0:T(8,128)}, f32[96,384]{1,0:T(8,128)}, f32[96,3...) custom-call(bf16[8,64,384]{2,1,0:T(8,128)(2,1)} %get-tuple-element.109.dq2_ref, ...), custom_call_target="tpu_custom_call" | custom-call | flops 99999997952 | bytes 300000000 | tf_op jit(solution)/shard_map/back_self/pallas_call | solution.py:419
  336.1 2.3 copy.56
  338.4 0.0 copy-start
  338.4 2.5 outputs.1
  341.0 0.0 copy-start.1
  341.0 0.0 copy-done
  341.0 1.1 copy.60
  342.1 0.8 copy-done.1
  342.9 0.0 copy-start.2
  342.9 1.1 copy.61
  344.1 0.0 copy-done.2
  344.1 0.7 copy.62
Async XLA Ops:
  338.4 2.6 copy-start
  341.0 2.0 copy-start.1
  342.9 1.1 copy-start.2
